TPU v7x, 32 devices: a whole 2x2x4 slice. The times are simulated.
32 devices in a mesh: groups: 2 (over x), wide: 16 (over z, y, core).
Axes of the slice: x: 2, y: 2, z: 4, core: 2. Of those that a mesh axis runs over, the one named last changes fastest.
Arguments:
- queries: bfloat16 [4096, 512], P(('groups', 'wide')), parts along dimension 0, may hold values from -200 to 200, as said below
- tree_kv: bfloat16 [2, 4096, 128], P(None, ('groups', 'wide')), parts along dimension 1, may hold values from -7 to 7, as said below
- kv_cache: bfloat16 [2, 512, 32, 128], P(None, ('groups', 'wide')), parts along dimension 1, may hold values from -6 to 6, as said below
- block_table: int32 [128, 4], P(('groups', 'wide')), parts along dimension 0, may hold values from 0 to 15, as said below
- cache_lengths: int32 [32, 4], P(('groups', 'wide')), parts along dimension 0, may hold values from 1 to 128, as said below
- parents: int32 [128, 32], P(('groups', 'wide')), parts along dimension 0, may hold values from -1 to 30, as said below
- w_out: bfloat16 [8192, 2048], P('wide'), may hold values from -0.375 to 0.375, as said below
- w_gate: bfloat16 [16, 2048, 768], P('wide'), may hold values from -0.125 to 0.125
- w_up: bfloat16 [16, 2048, 768], P('wide'), may hold values from -0.125 to 0.125
- w_down: bfloat16 [16, 768, 2048], P('wide'), may hold values from -0.4375 to 0.4375
- expert_ids: int32 [512, 8], P(('groups', 'wide')), parts along dimension 0, may hold values from 0 to 15, as said below
- gate_weights: float32 [512, 8], P(('groups', 'wide')), parts along dimension 0, may hold values from 0.05 to 0.5
Outputs:
- mixed: bfloat16 [512, 2048], P(('groups', 'wide')), parts along dimension 0
There are 2 independent parts, one for each index of `groups`. A program takes and returns all parts, laid end to end along the dimension named above; an argument that names none is the same for every part. Nothing has to cross between parts.
Inputs may be any that keep to these rules, and one draw needn't show every extreme that they name: `queries`: its hidden draw may carry large entries. `tree_kv`: blocks of one group whose slices use the same key head are equal. `kv_cache`: pools of one group whose slices use the same key head are equal. `block_table`: each device's rows list every page of its pool once; blocks t * 2 + g are equal for all t. `cache_lengths`: rows t * 2 + g are equal for all t; every row holds one length 128 and one length 1. `parents`: node i of a tree has a parent before it; node 0 is the root with parent -1; blocks t * 2 + g are equal for all t. `w_out`: blocks of one head slice are equal. `expert_ids`: each row lists 8 different experts. Within the rows of one device no expert is listed by more than 10 rows; in every draw one expert is listed by exactly 10 rows of every device.
All inputs are finite; a program needn't handle non-finite values.
Results may differ from a plain program's by a relative error of at most 0.0083.
Values may be sent and summed in bfloat16 or wider, within the bound.
No kernel may reach another device: no remote copies, remote signals or barrier semaphores. Data moves between devices by JAX's collectives and lax.ppermute only.
A program may use at most 64 MiB of HBM per device.

v0:
```python
import jax
import jax.numpy as jnp
from jax import lax
from jax.sharding import PartitionSpec as P

ATT_TP = 8


def from_partner(block, axis, apart):
    count = lax.axis_size(axis)
    route = []
    for low in range(count):
        high = low | 1 << apart
        if high != low and high < count:
            route += [(low, high), (high, low)]
    return lax.ppermute(block, axis, route)


def ancestor_mask(parents):
    node_count = parents.shape[1]
    columns = jnp.arange(node_count, dtype=jnp.int32)
    linked = (parents[:, :, None] == columns).astype(jnp.float32) + jnp.eye(
        node_count, dtype=jnp.float32
    )
    for repeat in range(max(node_count - 1, 1).bit_length()):
        linked = jnp.minimum(
            jnp.einsum("sij,sjk->sik", linked, linked, precision=lax.Precision.HIGHEST), 1.0
        )
    return linked > 0.5


def attend_local(queries, tree_kv, kv_cache, block_table, cache_lengths, parents):
    seq_count = parents.shape[0]
    node_count = parents.shape[1]
    head_dim = tree_kv.shape[-1]
    head_count = queries.shape[1] // head_dim
    cached_rows = kv_cache[:, block_table].reshape(2, seq_count, -1, head_dim)
    cached = cached_rows.shape[2]
    own_tree = tree_kv.reshape(2, seq_count, node_count, head_dim)
    joined = jnp.concatenate([cached_rows, own_tree], axis=2)
    query_heads = queries.reshape(seq_count, node_count, head_count, head_dim)
    scores = jnp.einsum(
        "sqhd,skd->sqhk", query_heads, joined[0], preferred_element_type=jnp.float32
    ) * head_dim ** (-0.5)
    positions = jnp.arange(cached, dtype=jnp.int32)
    cache_open = jnp.broadcast_to(
        positions[None, None, :] < cache_lengths.reshape(seq_count, 1, 1),
        (seq_count, node_count, cached),
    )
    allowed = jnp.concatenate([cache_open, ancestor_mask(parents)], axis=2)[:, :, None, :]
    masked = jnp.where(allowed, scores, -jnp.inf)
    highest = jnp.max(masked, axis=-1, keepdims=True)
    weights = jnp.exp(masked - highest)
    denominator = jnp.sum(weights, axis=-1, keepdims=True)
    blended = jnp.einsum(
        "sqhk,skd->sqhd",
        weights.astype(jnp.bfloat16),
        joined[1],
        preferred_element_type=jnp.float32,
    )
    return (blended / denominator).reshape(seq_count * node_count, -1).astype(jnp.bfloat16)


def expert_rows(received, w_gate, w_up, w_down):
    feature_count = received.shape[-1]
    flattened = received.reshape(-1, feature_count)
    gate_part = jnp.dot(flattened, w_gate[0], preferred_element_type=jnp.float32)
    up_part = jnp.dot(flattened, w_up[0], preferred_element_type=jnp.float32)
    activated = (jax.nn.silu(gate_part) * up_part).astype(jnp.bfloat16)
    produced = jnp.dot(activated, w_down[0], preferred_element_type=jnp.float32).astype(
        jnp.bfloat16
    )
    return produced.reshape(received.shape)


def body(
    queries,
    tree_kv,
    kv_cache,
    block_table,
    cache_lengths,
    parents,
    w_out,
    w_gate,
    w_up,
    w_down,
    expert_ids,
    gate_weights,
):
    attended = attend_local(queries, tree_kv, kv_cache, block_table, cache_lengths, parents)
    projected = jnp.dot(attended, w_out, preferred_element_type=jnp.float32)
    axis_width = lax.axis_size("wide")
    device_index = lax.axis_index("wide")
    top_bit = axis_width.bit_length() - 1
    slice_bits = [top_bit - 1 - step for step in range(ATT_TP.bit_length() - 1)]
    buffer = projected
    for bit in slice_bits:
        half_rows = buffer.shape[0] // 2
        upper_bit = device_index // (1 << bit) % 2 == 1
        kept_half = jnp.where(upper_bit, buffer[half_rows:], buffer[:half_rows])
        sent_half = jnp.where(upper_bit, buffer[:half_rows], buffer[half_rows:])
        buffer = kept_half + from_partner(sent_half, "wide", bit)
    hidden = buffer.astype(jnp.bfloat16)
    row_count = hidden.shape[0]
    mean_rows = row_count * expert_ids.shape[1] // axis_width
    capacity = mean_rows + max(mean_rows // 4, 1)
    numbers = jnp.arange(axis_width, dtype=jnp.int32)
    matches = expert_ids[:, :, None] == numbers
    chosen = jnp.any(matches, axis=1).astype(jnp.int32)
    row_weight = jnp.sum(jnp.where(matches, gate_weights[:, :, None], 0.0), axis=1)
    ranking = jnp.cumsum(chosen, axis=0) - chosen
    slot_ids = jnp.arange(capacity, dtype=jnp.int32)
    placed = (chosen[:, :, None] == 1) & (ranking[:, :, None] == slot_ids)
    placed_int = placed.astype(jnp.int32)
    source_row = jnp.sum(placed_int * jnp.arange(row_count, dtype=jnp.int32)[:, None, None], axis=0)
    occupied = jnp.sum(placed_int, axis=0)
    slot_weight = jnp.sum(jnp.where(placed, row_weight[:, :, None], 0.0), axis=0)
    outgoing = jnp.where(occupied[:, :, None] == 1, hidden[source_row], jnp.zeros((), jnp.bfloat16))
    received = lax.all_to_all(outgoing, "wide", split_axis=0, concat_axis=0, tiled=True)
    returned = lax.all_to_all(
        expert_rows(received, w_gate, w_up, w_down), "wide", split_axis=0, concat_axis=0, tiled=True
    )
    weighted = returned.reshape(-1, returned.shape[-1]).astype(jnp.float32) * slot_weight.reshape(
        -1, 1
    )
    combined = jax.ops.segment_sum(weighted, source_row.reshape(-1), num_segments=row_count)
    return combined.astype(jnp.bfloat16)


def solution(mesh):
    placed = (
        P(("groups", "wide"), None),
        P(None, ("groups", "wide"), None),
        P(None, ("groups", "wide"), None, None),
        P(("groups", "wide"), None),
        P(("groups", "wide"), None),
        P(("groups", "wide"), None),
        P("wide", None),
        P("wide", None, None),
        P("wide", None, None),
        P("wide", None, None),
        P(("groups", "wide"), None),
        P(("groups", "wide"), None),
    )
    return jax.shard_map(
        body, mesh=mesh, in_specs=placed, out_specs=P(("groups", "wide"), None), check_vma=False
    )
```

profile of v0, /device:TPU:0, one launch (start us, length us, event | category | flops | bytes accessed | tf_op | source)
XLA Modules:
  0.0 141.5 jit_solution(13651653561778178837)
XLA Ops:
  0.0 1.5 %iota_compare_fusion.5 = pred[4,128]{1,0:T(4,128)(4,1)} fusion(s32[4]{0:T(128)} %bitcast.67), kind=kLoop, calls=%fused_computation.78 | loop fusion | flops 512 | bytes 528 | tf_op jit(solution)/shard_map/lt | solution.py:47
  2.8 1.0 convolution_minimum_fusion.4
  5.6 1.7 %gather_fusion = bf16[16,2,32,128]{3,2,1,0:T(8,128)(2,1)S(1)} fusion(bf16[2,16,32,128]{3,2,1,0:T(8,128)(2,1)} %param.14, s32[1024]{0:T(1024)} %pad_clamp_fusion.1), kind=kCustom, calls=%fused_computation | custom fusion | bytes 524352 | tf_op jit(solution)/shard_map/gather | solution.py:37
  8.2 1.1 fusion.55
  10.4 1.0 copy-done.1
  12.3 4.1 %collective-permute-start = (f32[64,2048]{1,0:T(8,128)}, f32[64,2048]{1,0:T(8,128)}, u32[]{:S(2)}, u32[]{:S(2)}) collective-permute-start(f32[64,2048]{1,0:T(8,128)} %slice_select_fusion), channel_id=1, source_target_pairs={{0,8},{8,0},{1,9},{9,1},{2,10},{10,2},{3,11},{11,3},{4,12},{12,4},... | collective-permute-start | bytes 1572872 | tf_op jit(solution)/shard_map/ppermute | solution.py:16
  16.6 23.2 %collective-permute-done = f32[64,2048]{1,0:T(8,128)} collective-permute-done((f32[64,2048]{1,0:T(8,128)}, f32[64,2048]{1,0:T(8,128)}, u32[]{:S(2)}, u32[]{:S(2)}) %collective-permute-start) | collective-permute-done | bytes 524320 | tf_op jit(solution)/shard_map/ppermute | solution.py:16
  39.8 1.4 %select_add_fusion = f32[64,2048]{1,0:T(8,128)S(1)} fusion(f32[64,2048]{1,0:T(8,128)} %collective-permute-done, f32[128,2048]{1,0:T(8,128)} %copy-done.1, pred[]{:T(512)S(6)} %eq.93), kind=kLoop, calls=%fused_computation.27 | loop fusion | flops 262144 | bytes 2097153 | tf_op jit(solution)/shard_map/add | solution.py:102
  43.0 6.8 %collective-permute-done.1 = f32[32,2048]{1,0:T(8,128)} collective-permute-done((f32[32,2048]{1,0:T(8,128)S(1)}, f32[32,2048]{1,0:T(8,128)}, u32[]{:S(2)}, u32[]{:S(2)}) %collective-permute-start.1) | collective-permute-done | bytes 262176 | tf_op jit(solution)/shard_map/ppermute | solution.py:16
  49.7 1.1 select_add_fusion.1
  51.5 1.3 collective-permute-start.2
  53.1 3.7 %collective-permute-done.2 = f32[16,2048]{1,0:T(8,128)} collective-permute-done((f32[16,2048]{1,0:T(8,128)}, f32[16,2048]{1,0:T(8,128)}, u32[]{:S(2)}, u32[]{:S(2)}) %collective-permute-start.2) | collective-permute-done | bytes 131104 | tf_op jit(solution)/shard_map/ppermute | solution.py:16
  57.8 1.9 %gather_fusion.1 = bf16[160,2048]{1,0:T(8,128)(2,1)} fusion(bf16[16,2048]{1,0:T(8,128)(2,1)S(1)} %add_convert_fusion, s32[1024]{0:T(1024)S(1)} %pad_clamp_fusion), kind=kCustom, calls=%fused_computation.1 | custom fusion | bytes 1311360 | tf_op jit(solution)/shard_map/gather | solution.py:118
  59.7 2.2 %reshape.110 = bf16[16,10,2048]{2,1,0:T(8,128)(2,1)} reshape(bf16[160,2048]{1,0:T(8,128)(2,1)} %gather_fusion.1) | data formatting | bytes 1310720 | tf_op jit(solution)/shard_map/gather | solution.py:118
  61.8 1.4 broadcast_select_fusion
  63.2 31.4 %all_to_all.10 = bf16[16,10,2048]{2,1,0:T(8,128)(2,1)} all-to-all(bf16[16,10,2048]{2,1,0:T(8,128)(2,1)S(1)} %broadcast_select_fusion), channel_id=1, replica_groups=mesh['groups'=2,'wide'=16] {'wide'}, dimensions={0} | all-to-all | bytes 1310720 | tf_op jit(solution)/shard_map/all_to_all | solution.py:119
  94.6 2.2 %reshape.98 = bf16[160,2048]{1,0:T(8,128)(2,1)} reshape(bf16[16,10,2048]{2,1,0:T(8,128)(2,1)} %all_to_all.10) | data formatting | bytes 1310720 | tf_op jit(solution)/shard_map/reshape | solution.py:66
  96.8 3.6 %fusion.4 = f32[160,768]{1,0:T(8,128)} fusion(bf16[160,2048]{1,0:T(8,128)(2,1)} %reshape.98, bf16[1,2048,768]{2,1,0:T(8,128)(2,1)} %param.19), kind=kOutput, calls=%fused_computation.7 | convolution fusion | flops 503316480 | bytes 4292608 | tf_op jit(solution)/shard_map/dot_general | solution.py:67
  100.3 4.5 %fusion.6 = bf16[160,2048]{1,0:T(8,128)(2,1)} fusion(bf16[1,768,2048]{2,1,0:T(8,128)(2,1)S(1)} %copy-done, bf16[160,2048]{1,0:T(8,128)(2,1)} %reshape.98, bf16[1,2048,768]{2,1,0:T(8,128)(2,1)} %param.20, f32[160,768]{1,0:T(8,128)} %fusion.4), kind=kOutput, calls=%fused_computation.9 | convolution fusion | flops 1007697920 | bytes 8093696 | tf_op jit(solution)/shard_map/dot_general | solution.py:70
  104.8 2.2 %reshape.99 = bf16[16,10,2048]{2,1,0:T(8,128)(2,1)} reshape(bf16[160,2048]{1,0:T(8,128)(2,1)} %fusion.6) | data formatting | bytes 1310720 | tf_op jit(solution)/shard_map/reshape | solution.py:73
  107.0 5.0 %all-to-all-start.1 = ((bf16[16,10,2048]{2,1,0:T(8,128)(2,1)}), bf16[16,10,2048]{2,1,0:T(8,128)(2,1)}, u32[]{:S(2)}, u32[]{:S(2)}) async-start(bf16[16,10,2048]{2,1,0:T(8,128)(2,1)} %reshape.99), calls=%async_computation.1 | async-start | bytes 2097152 | tf_op jit(solution)/shard_map/all_to_all | solution.py:120
  112.6 22.4 %all-to-all-done.1 = bf16[16,10,2048]{2,1,0:T(8,128)(2,1)} async-done(((bf16[16,10,2048]{2,1,0:T(8,128)(2,1)}), bf16[16,10,2048]{2,1,0:T(8,128)(2,1)}, u32[]{:S(2)}, u32[]{:S(2)}) %all-to-all-start.1) | async-done | bytes 655392 | tf_op jit(solution)/shard_map/all_to_all | solution.py:120
  135.0 2.4 %reshape.100 = f32[160,2048]{1,0:T(8,128)} reshape(bf16[16,10,2048]{2,1,0:T(8,128)(2,1)} %all-to-all-done.1) | data formatting | bytes 1966080 | tf_op jit(solution)/shard_map/convert_element_type | solution.py:123
  137.4 3.5 %scatter_custom_fusion = f32[16,2048]{1,0:T(8,128)S(1)} fusion(s32[160]{0:T(256)S(1)} %reshape.119, f32[160,2048]{1,0:T(8,128)} %reshape.100, f32[160]{0:T(256)S(1)} %mul.41, f32[]{:T(128)} %constant.71.clone.1), kind=kCustom, calls=%fused_computation.10 | custom fusion | flops 655360 | bytes 1442820 | tf_op jit(solution)/shard_map/scatter-add | solution.py:126
  (54 shorter events, 10.8 us)
Async XLA Ops:
  0.0 100.3 %copy-start = (bf16[1,768,2048]{2,1,0:T(8,128)(2,1)S(1)}, bf16[1,768,2048]{2,1,0:T(8,128)(2,1)}, u32[]{:S(2)}) copy-start(bf16[1,768,2048]{2,1,0:T(8,128)(2,1)} %param.21) | copy-start | bytes 9437188
  7.3 2.3 %copy-start.6 = (bf16[2,128,128]{2,1,0:T(8,128)(2,1)S(1)}, bf16[2,128,128]{2,1,0:T(8,128)(2,1)}, u32[]{:S(2)}) copy-start(bf16[2,128,128]{2,1,0:T(8,128)(2,1)} %param.13) | copy-start | bytes 196612
  7.3 2.7 %copy-start.3 = (bf16[512,2048]{1,0:T(8,128)(2,1)S(1)}, bf16[512,2048]{1,0:T(8,128)(2,1)}, u32[]{:S(2)}) copy-start(bf16[512,2048]{1,0:T(8,128)(2,1)} %param.18) | copy-start | bytes 6291460
  10.0 6.4 %copy-start.4 = (s32[16,8]{0,1:T(8,128)S(1)}, s32[16,8]{0,1:T(8,128)}, u32[]{:S(2)}) copy-start(s32[16,8]{0,1:T(8,128)} %param.22) | copy-start | bytes 1540
  10.4 1.0 copy-start.1
  12.3 27.5 %collective-permute-start = (f32[64,2048]{1,0:T(8,128)}, f32[64,2048]{1,0:T(8,128)}, u32[]{:S(2)}, u32[]{:S(2)}) collective-permute-start(f32[64,2048]{1,0:T(8,128)} %slice_select_fusion), channel_id=1, source_target_pairs={{0,8},{8,0},{1,9},{9,1},{2,10},{10,2},{3,11},{11,3},{4,12},{12,4},... | collective-permute-start | bytes 1572872 | tf_op jit(solution)/shard_map/ppermute | solution.py:16
  41.3 0.8 copy-start.2
  42.1 7.7 %collective-permute-start.1 = (f32[32,2048]{1,0:T(8,128)S(1)}, f32[32,2048]{1,0:T(8,128)}, u32[]{:S(2)}, u32[]{:S(2)}) collective-permute-start(f32[32,2048]{1,0:T(8,128)S(1)} %slice_select_fusion.1), channel_id=1, source_target_pairs={{0,4},{4,0},{1,5},{5,1},{2,6},{6,2},{3,7},{7,3},{8,12},{12,8},{9,1... | collective-permute-start | bytes 786440 | tf_op jit(solution)/shard_map/ppermute | solution.py:16
  51.5 5.3 %collective-permute-start.2 = (f32[16,2048]{1,0:T(8,128)}, f32[16,2048]{1,0:T(8,128)}, u32[]{:S(2)}, u32[]{:S(2)}) collective-permute-start(f32[16,2048]{1,0:T(8,128)} %slice_select_fusion.2), channel_id=1, source_target_pairs={{0,2},{2,0},{1,3},{3,1},{4,6},{6,4},{5,7},{7,5},{8,10},{10,8},{9,1... | collective-permute-start | bytes 393224 | tf_op jit(solution)/shard_map/ppermute | solution.py:16
  104.8 7.3 %copy-start.5 = (f32[16,8]{0,1:T(8,128)S(1)}, f32[16,8]{0,1:T(8,128)}, u32[]{:S(2)}) copy-start(f32[16,8]{0,1:T(8,128)} %param.23) | copy-start | bytes 1540
  107.0 28.1 %all-to-all-start.1 = ((bf16[16,10,2048]{2,1,0:T(8,128)(2,1)}), bf16[16,10,2048]{2,1,0:T(8,128)(2,1)}, u32[]{:S(2)}, u32[]{:S(2)}) async-start(bf16[16,10,2048]{2,1,0:T(8,128)(2,1)} %reshape.99), calls=%async_computation.1 | async-start | bytes 2097152 | tf_op jit(solution)/shard_map/all_to_all | solution.py:120
where the time goes:
time: 143 us; the launch traced here: 142 us
  waiting for transfers between devices  56.1 us (39%)
  blocking collectives  31.4 us (22%)
  local copies, waits for them, and re-layouts  17 us (12%)
  other arithmetic  14 us (10%)
  matrix products  11.6 us (8%)
  starting transfers between devices  11.2 us (8%)
    ppermute x3, waiting for transfers between devices, from_partner(): return lax.ppermute(block, axis, route)  33.7 us
    all_to_all x1, blocking collectives, body(): lax.all_to_all(outgoing, 'wide', split_axis=0, concat_axis=0, tiled=True)  31.4 us
    all_to_all x1, waiting for transfers between devices, body(): lax.all_to_all(expert_rows(received, w_gate, w_up, w_down), 'wide', split...  22.4 us
    ppermute x3, starting transfers between devices, from_partner(): return lax.ppermute(block, axis, route)  6.14 us
    all_to_all x1, starting transfers between devices, body(): lax.all_to_all(expert_rows(received, w_gate, w_up, w_down), 'wide', split...  5.05 us
    dot_general x1, matrix products, expert_rows(): jnp.dot(activated, w_down[0], preferred_element_type=jnp.float32)  4.47 us
    gather x2, local copies, waits for them, and re-layouts, body(): hidden[source_row]  4.08 us
    dot_general x1, matrix products, expert_rows(): jnp.dot(flattened, w_gate[0], preferred_element_type=jnp.float32)  3.55 us
  transfers between devices with their start and end apart: 4, of which 4 were waited for; matrix products, arithmetic and copies ran while one was open for 1% of the time, Pallas kernels for 0%

commit v1 on v0

v1 whole, which is shorter than its diff:
```python
import functools

import jax
import jax.numpy as jnp
from jax import lax
from jax.experimental import pallas as pl
from jax.experimental.pallas import tpu as pltpu
from jax.sharding import PartitionSpec as P

ATT_TP = 8
CHUNKS = 2
LANES = 128


def bits_of(count):
    return count.bit_length() - 1


def exchange(block, masks):
    count = lax.axis_size("wide")
    return lax.ppermute(block, "wide", [(i, i ^ masks[i & 1]) for i in range(count)])


def slice_orders(axis_width):
    groups = axis_width // ATT_TP
    first = [groups << step for step in range(bits_of(ATT_TP))]
    second = [first[1], first[0]] + first[2:] if groups > 1 and len(first) > 2 else first
    return first, second


def relative_masks(order):
    steps = len(order)
    masks = []
    for j in range(1 << steps):
        mask = 0
        for step in range(steps):
            if j >> (steps - 1 - step) & 1:
                mask ^= order[step]
        masks.append(mask)
    return masks


def attend_kernel(
    axis_width,
    table,
    lengths,
    queries,
    tree_kv,
    kv_cache,
    parents,
    expert_ids,
    gate_weights,
    w_out,
    *refs,
):
    outs, (extra, attended, weights_in, weights_sem) = refs[:-4], refs[-4:]
    copy = pltpu.make_async_copy(w_out, weights_in, weights_sem)
    copy.start()
    seq_count, node_count = parents.shape
    head_dim = tree_kv.shape[-1]
    head_count = queries.shape[1] // head_dim
    pages = table.shape[1]
    cached = pages * kv_cache.shape[2]
    all_nodes = seq_count * node_count
    query_count = head_count * node_count
    f32, bf16 = jnp.float32, jnp.bfloat16

    shifted = [
        jnp.where(parents[s : s + 1, :] >= 0, parents[s : s + 1, :] + s * node_count, -1)
        for s in range(seq_count)
    ]
    parent_row = jnp.concatenate(shifted, axis=1)
    rows = lax.broadcasted_iota(jnp.int32, (all_nodes, all_nodes), 0)
    columns = lax.broadcasted_iota(jnp.int32, (all_nodes, all_nodes), 1)
    reached = ((rows == columns) | (rows == parent_row)).astype(f32).astype(bf16)
    for repeat in range(max(node_count - 1, 1).bit_length()):
        squared = jnp.dot(reached, reached, preferred_element_type=f32)
        reached = jnp.minimum(squared, 1.0).astype(bf16)

    node_rows = lax.broadcasted_iota(jnp.int32, (all_nodes, query_count), 0)
    query_nodes = lax.broadcasted_iota(jnp.int32, (all_nodes, query_count), 1) % node_count
    positions = lax.broadcasted_iota(jnp.int32, (cached, query_count), 0)
    for s in range(seq_count):
        own = slice(s * node_count, (s + 1) * node_count)
        spread = (node_rows == query_nodes + s * node_count).astype(f32).astype(bf16)
        tree_open = jnp.dot(reached[own], spread, preferred_element_type=f32) > 0.5
        keys = [kv_cache[0, table[s, p]] for p in range(pages)]
        values = [kv_cache[1, table[s, p]] for p in range(pages)]
        key_rows = jnp.concatenate(keys + [tree_kv[0, own]], axis=0)
        value_rows = jnp.concatenate(values + [tree_kv[1, own]], axis=0)
        query_rows = jnp.concatenate(
            [queries[own, h * head_dim : (h + 1) * head_dim] for h in range(head_count)], axis=0
        )
        scores = lax.dot_general(
            key_rows, query_rows, (((1,), (1,)), ((), ())), preferred_element_type=f32
        ) * head_dim ** (-0.5)
        cache_scores = jnp.where(positions < lengths[0, s], scores[:cached], -jnp.inf)
        tree_scores = jnp.where(tree_open, scores[cached:], -jnp.inf)
        masked = jnp.concatenate([cache_scores, tree_scores], axis=0)
        highest = jnp.max(masked, axis=0, keepdims=True)
        probs = jnp.exp(masked - highest)
        total = jnp.broadcast_to(jnp.sum(probs, axis=0, keepdims=True), (head_dim, query_count))
        blended = lax.dot_general(
            probs.astype(bf16), value_rows, (((0,), (0,)), ((), ())), preferred_element_type=f32
        )
        blended = (blended / total.T).astype(bf16)
        for h in range(head_count):
            attended[own, h * head_dim : (h + 1) * head_dim] = blended[
                h * node_count : (h + 1) * node_count
            ]

    row_count, listed = expert_ids.shape
    lane = lax.broadcasted_iota(jnp.int32, (row_count, extra.shape[1]), 1)
    weight = jnp.zeros((row_count, extra.shape[1]), f32)
    for k in range(listed):
        weight += jnp.where(
            expert_ids[:, k : k + 1] == lane % axis_width, gate_weights[:, k : k + 1], 0.0
        )
    upper = weight.astype(bf16).astype(f32)
    parts = jnp.where(lane < axis_width, upper, jnp.where(lane < 2 * axis_width, weight - upper, 0.0))
    extra[:row_count] = parts.astype(bf16)
    extra[row_count:] = jnp.zeros((row_count, extra.shape[1]), bf16)

    device = lax.axis_index("wide")
    groups = axis_width // ATT_TP
    first, second = [relative_masks(order) for order in slice_orders(axis_width)]
    block = all_nodes // ATT_TP
    picked = []
    for one, other in zip(first, second):
        target = (device ^ jnp.where(device & 1 == 0, one, other)) // groups
        picked.append(attended[pl.ds(pl.multiple_of(target * block, block), block), :])
    ordered = jnp.concatenate(picked, axis=0)
    copy.wait()
    half = all_nodes // 2
    width = outs[0].shape[1]
    for c in range(len(outs) // 2):
        projected = jnp.dot(
            ordered, weights_in[:, c * width : (c + 1) * width], preferred_element_type=f32
        )
        outs[2 * c][...] = projected[:half]
        outs[2 * c + 1][...] = projected[half:].astype(bf16)


def attend(queries, tree_kv, kv_cache, table, lengths, parents, w_out, expert_ids, gate_weights):
    axis_width = lax.axis_size("wide")
    features = w_out.shape[1]
    rows = queries.shape[0]
    own_rows = expert_ids.shape[0]
    extra_width = -(-2 * axis_width // LANES) * LANES
    smem = pl.BlockSpec(memory_space=pltpu.SMEM)
    vmem = pl.BlockSpec(memory_space=pltpu.VMEM)
    half = (rows // 2, features // CHUNKS)
    kept, sent = jax.ShapeDtypeStruct(half, jnp.float32), jax.ShapeDtypeStruct(half, jnp.bfloat16)
    return pl.pallas_call(
        functools.partial(attend_kernel, axis_width),
        out_shape=[kept, sent] * CHUNKS
        + [jax.ShapeDtypeStruct((2 * own_rows, extra_width), jnp.bfloat16)],
        in_specs=[smem, smem] + [vmem] * 6 + [pl.BlockSpec(memory_space=pl.ANY)],
        out_specs=[vmem] * (2 * CHUNKS + 1),
        scratch_shapes=[
            pltpu.VMEM(queries.shape, jnp.bfloat16),
            pltpu.VMEM(w_out.shape, jnp.bfloat16),
            pltpu.SemaphoreType.DMA,
        ],
        compiler_params=pltpu.CompilerParams(vmem_limit_bytes=16 * 1024 * 1024),
        name="attend",
    )(table, lengths, queries, tree_kv, kv_cache, parents, expert_ids, gate_weights, w_out)


def experts_kernel(axis_width, tile, *refs):
    hidden, (w_gate, w_up, w_down) = refs[:CHUNKS], refs[CHUNKS : CHUNKS + 3]
    outs, activated = refs[CHUNKS + 3 : -1], refs[-1]
    f32, bf16 = jnp.float32, jnp.bfloat16
    width = outs[0].shape[1]
    device = lax.axis_index("wide")
    parts = hidden[-1][:, width:]
    lane = lax.broadcasted_iota(jnp.int32, parts.shape, 1)
    mine = (lane == device) | (lane == device + axis_width)
    weight = jnp.sum(jnp.where(mine, parts.astype(f32), 0.0), axis=1, keepdims=True)
    hidden_width = activated.shape[1]
    half = activated.shape[0] // 2
    for n in range(hidden_width // tile):
        cut = slice(n * tile, (n + 1) * tile)
        gate_part = up_part = 0.0
        for c in range(CHUNKS):
            rows = hidden[c][:, :width]
            down = slice(c * width, (c + 1) * width)
            gate_part += jnp.dot(rows, w_gate[0, down, cut], preferred_element_type=f32)
            up_part += jnp.dot(rows, w_up[0, down, cut], preferred_element_type=f32)
        activated[:, cut] = (gate_part / (1.0 + jnp.exp(-gate_part)) * up_part).astype(bf16)
    for c in range(CHUNKS):
        for n in range(width // tile):
            cut = slice(c * width + n * tile, c * width + (n + 1) * tile)
            produced = jnp.dot(activated[...], w_down[0, :, cut], preferred_element_type=f32)
            weighted = produced * weight
            outs[2 * c][:, n * tile : (n + 1) * tile] = weighted[:half]
            outs[2 * c + 1][:, n * tile : (n + 1) * tile] = weighted[half:].astype(bf16)


def experts(hidden, w_gate, w_up, w_down):
    axis_width = lax.axis_size("wide")
    rows = hidden[0].shape[0]
    hidden_width, features = w_down.shape[1:]
    vmem = pl.BlockSpec(memory_space=pltpu.VMEM)
    tile = 256 if hidden_width % 256 == 0 else LANES
    half = (rows // 2, features // CHUNKS)
    kept, sent = jax.ShapeDtypeStruct(half, jnp.float32), jax.ShapeDtypeStruct(half, jnp.bfloat16)
    return pl.pallas_call(
        functools.partial(experts_kernel, axis_width, tile),
        out_shape=[kept, sent] * CHUNKS,
        in_specs=[vmem] * (CHUNKS + 3),
        out_specs=[vmem] * (2 * CHUNKS),
        scratch_shapes=[pltpu.VMEM((rows, hidden_width), jnp.bfloat16)],
        compiler_params=pltpu.CompilerParams(vmem_limit_bytes=48 * 1024 * 1024),
        name="experts",
    )(*hidden, w_gate, w_up, w_down)


def halved(block):
    half = block.shape[0] // 2
    return block[:half], block[half:].astype(jnp.bfloat16)


def body(
    queries,
    tree_kv,
    kv_cache,
    block_table,
    cache_lengths,
    parents,
    w_out,
    w_gate,
    w_up,
    w_down,
    expert_ids,
    gate_weights,
):
    axis_width = lax.axis_size("wide")
    steps = list(zip(*slice_orders(axis_width)))
    group_steps = [(1 << k, 1 << k) for k in range(bits_of(axis_width // ATT_TP))]
    *halves, extra = attend(
        queries, tree_kv, kv_cache, block_table, cache_lengths, parents, w_out,
        expert_ids, gate_weights,
    )
    hidden = []
    for c in range(CHUNKS):
        kept, sent = halves[2 * c], halves[2 * c + 1]
        for number, masks in enumerate(steps[:-1]):
            kept = kept + exchange(sent, masks).astype(jnp.float32)
            if number < len(steps) - 2:
                kept, sent = halved(kept)
        if c == CHUNKS - 1:
            kept = jnp.concatenate([kept, extra.astype(jnp.float32)], axis=1)
        half = kept.shape[0] // 2
        other = exchange(kept.astype(jnp.bfloat16), steps[-1]).astype(jnp.float32)
        block = kept + jnp.concatenate([other[half:], other[:half]], axis=0)
        block = block.astype(jnp.bfloat16)
        for masks in steps[-2::-1] + group_steps:
            block = jnp.concatenate([block, exchange(block, masks)], axis=0)
        hidden.append(block)
    produced = experts(hidden, w_gate, w_up, w_down)
    results = []
    for c in range(CHUNKS):
        kept, sent = produced[2 * c], produced[2 * c + 1]
        last = len(group_steps) + len(steps) - 1
        for number, masks in enumerate(group_steps[::-1] + steps):
            kept = kept + exchange(sent, masks).astype(jnp.float32)
            if number < last:
                kept, sent = halved(kept)
        results.append(kept.astype(jnp.bfloat16))
    return jnp.concatenate(results, axis=1)


def solution(mesh):
    placed = (
        P(("groups", "wide"), None),
        P(None, ("groups", "wide"), None),
        P(None, ("groups", "wide"), None, None),
        P(("groups", "wide"), None),
        P(("groups", "wide"), None),
        P(("groups", "wide"), None),
        P("wide", None),
        P("wide", None, None),
        P("wide", None, None),
        P("wide", None, None),
        P(("groups", "wide"), None),
        P(("groups", "wide"), None),
    )
    return jax.shard_map(
        body, mesh=mesh, in_specs=placed, out_specs=P(("groups", "wide"), None), check_vma=False
    )
```

time: 143 us -> 66.8 us (0.47)
  waiting for transfers between devices: 56.1 us -> 21.9 us
  blocking collectives: 31.4 us -> 0 us
  starting transfers between devices: 11.2 us -> 26.7 us
  other arithmetic: 14 us -> 1.18 us
  matrix products: 11.6 us -> 0 us
  local copies, waits for them, and re-layouts: 17 us -> 7.92 us
  Pallas kernels: 0 us -> 8.47 us
    all_to_all x1 -> x0, blocking collectives: 31.4 us -> none  [body(): lax.all_to_all(outgoing, 'wide', split_axis=0, concat_axis=0, tiled=True)]
    all_to_all x1 -> x0, waiting for transfers between devices: 22.4 us -> none  [body(): lax.all_to_all(expert_rows(received, w_gate, w_up, w_down), 'wide', split...]
    ppermute x3 -> x20, starting transfers between devices: 6.14 us -> 26.7 us  [exchange(): lax.ppermute(block, 'wide', [(i, i ^ masks[i & 1]) for i in range(count)])]
    ppermute x3 -> x20, waiting for transfers between devices: 33.7 us -> 21.9 us  [exchange(): lax.ppermute(block, 'wide', [(i, i ^ masks[i & 1]) for i in range(count)])]
    dot_general x10 -> x0, matrix products: 11.6 us -> none  [the longest x1 4.47 us: expert_rows(): jnp.dot(activated, w_down[0], preferred_element_type=jnp.float32)]
    pallas_call x0 -> x2, Pallas kernels: none -> 8.47 us  [the longest x1 5.46 us: experts(): pl.pallas_call(functools.partial(experts_kernel, axis_width, tile), out_s...]
    unnamed x16 -> x18, local copies, waits for them, and re-layouts: 1.93 us -> 7.82 us
    gather x4 -> x0, local copies, waits for them, and re-layouts: 5.77 us -> none  [the longest x2 4.08 us: body(): hidden[source_row]]
  transfers between devices with their start and end apart: 4 -> 20, of which waited for: 4 -> 14; matrix products, arithmetic and copies ran while one was open for 1% -> 1% of each run, Pallas kernels for 0% -> 0%
where the time goes in v1:
time: 66.8 us; the launch traced here: 66.4 us
  starting transfers between devices  26.7 us (40%)
  waiting for transfers between devices  21.9 us (33%)
  Pallas kernels  8.47 us (13%)
  local copies, waits for them, and re-layouts  7.92 us (12%)
  other arithmetic  1.18 us (2%)
    ppermute x20, starting transfers between devices, exchange(): lax.ppermute(block, 'wide', [(i, i ^ masks[i & 1]) for i in range(count)])  26.7 us
    ppermute x20, waiting for transfers between devices, exchange(): lax.ppermute(block, 'wide', [(i, i ^ masks[i & 1]) for i in range(count)])  21.9 us
    unnamed x18, local copies, waits for them, and re-layouts  7.82 us
    pallas_call x1, Pallas kernels, experts(): pl.pallas_call(functools.partial(experts_kernel, axis_width, tile), out_s...  5.46 us
    pallas_call x1, Pallas kernels, attend(): pl.pallas_call(functools.partial(attend_kernel, axis_width), out_shape=[k...  3.01 us
  transfers between devices with their start and end apart: 20, of which 14 were waited for; matrix products, arithmetic and copies ran while one was open for 1% of the time, Pallas kernels for 0%

profile of v1, /device:TPU:0, one launch (start us, length us, event | category | flops | bytes accessed | tf_op | source)
XLA Modules:
  0.0 66.4 jit_solution(2228235935711402109)
XLA Ops:
  1.5 1.6 %copy-done.1 = bf16[512,2048]{1,0:T(8,128)(2,1)S(1)} copy-done((bf16[512,2048]{1,0:T(8,128)(2,1)S(1)}, bf16[512,2048]{1,0:T(8,128)(2,1)}, u32[]{:S(2)}) %copy-start.1) | copy-done | bytes 2097176
  7.8 3.0 %attend.1 = (f32[64,1024]{1,0:T(8,128)S(1)}, bf16[64,1024]{1,0:T(8,128)(2,1)S(1)}, f32[64,1024]{1,0:T(8,128)S(1)}, bf16[64,1024]{1,0:T(8,128)(2,1)S(1)}, bf16[32,128]{1,0:T(8,128)(2,1)S(1)}) custom-call(s32[4,4]{1,0:T(4,128)S(1)} %copy-done.5, s32[1,4]{1,0:T(1,128)S(1)} %copy-done.7, bf16[128,512]{1,0:T(8,128)(2,1)S(1)} %copy-done.3, ...), custom_call_target="tpu_custom_call" | custom-call | tf_op jit(solution)/shard_map/attend/pallas_call | solution.py:154
  10.8 3.0 %collective-permute-start = (bf16[64,1024]{1,0:T(8,128)(2,1)S(1)}, bf16[64,1024]{1,0:T(8,128)(2,1)S(1)}, u32[]{:S(2)}, u32[]{:S(2)}) collective-permute-start(bf16[64,1024]{1,0:T(8,128)(2,1)S(1)} %get-tuple-element.15), channel_id=1, source_target_pairs={{0,2},{1,5},{2,0},{3,7},{4,6},{5,1},{6,4},{7,3},{8,10},{9,13},{10,... | collective-permute-start | bytes 393224 | tf_op jit(solution)/shard_map/ppermute | solution.py:21
  14.0 2.9 %collective-permute-done = bf16[64,1024]{1,0:T(8,128)(2,1)S(1)} collective-permute-done((bf16[64,1024]{1,0:T(8,128)(2,1)S(1)}, bf16[64,1024]{1,0:T(8,128)(2,1)S(1)}, u32[]{:S(2)}, u32[]{:S(2)}) %collective-permute-start) | collective-permute-done | bytes 131104 | tf_op jit(solution)/shard_map/ppermute | solution.py:21
  16.9 2.1 %collective-permute-start.1 = (bf16[32,1024]{1,0:T(8,128)(2,1)S(1)}, bf16[32,1024]{1,0:T(8,128)(2,1)S(1)}, u32[]{:S(2)}, u32[]{:S(2)}) collective-permute-start(bf16[32,1024]{1,0:T(8,128)(2,1)S(1)} %slice.137), channel_id=1, source_target_pairs={{0,4},{1,3},{2,6},{3,1},{4,0},{5,7},{6,2},{7,5},{8,12},{9,11},{10,... | collective-permute-start | bytes 196616 | tf_op jit(solution)/shard_map/ppermute | solution.py:21
  19.1 1.5 %collective-permute-start.7 = (bf16[32,1024]{1,0:T(8,128)(2,1)S(1)}, bf16[32,1024]{1,0:T(8,128)(2,1)S(1)}, u32[]{:S(2)}, u32[]{:S(2)}) collective-permute-start(bf16[32,1024]{1,0:T(8,128)(2,1)S(1)} %slice.136), channel_id=1, source_target_pairs={{0,4},{1,3},{2,6},{3,1},{4,0},{5,7},{6,2},{7,5},{8,12},{9,11},{10,... | collective-permute-start | bytes 196616 | tf_op jit(solution)/shard_map/ppermute | solution.py:21
  21.3 3.1 %collective-permute-start.2 = (bf16[32,1024]{1,0:T(8,128)(2,1)S(1)}, bf16[32,1024]{1,0:T(8,128)(2,1)S(1)}, u32[]{:S(2)}, u32[]{:S(2)}) collective-permute-start(bf16[32,1024]{1,0:T(8,128)(2,1)S(1)} %fusion.3), channel_id=1, source_target_pairs={{0,8},{1,9},{2,10},{3,11},{4,12},{5,13},{6,14},{7,15},{8,0},{9,1},... | collective-permute-start | bytes 196616 | tf_op jit(solution)/shard_map/ppermute | solution.py:21
  24.4 1.8 %collective-permute-start.8 = (bf16[32,1152]{1,0:T(8,128)(2,1)S(1)}, bf16[32,1152]{1,0:T(8,128)(2,1)S(1)}, u32[]{:S(2)}, u32[]{:S(2)}) collective-permute-start(bf16[32,1152]{1,0:T(8,128)(2,1)S(1)} %fusion.2), channel_id=1, source_target_pairs={{0,8},{1,9},{2,10},{3,11},{4,12},{5,13},{6,14},{7,15},{8,0},{9,1},... | collective-permute-start | bytes 221192 | tf_op jit(solution)/shard_map/ppermute | solution.py:21
  26.2 2.3 %collective-permute-done.2 = bf16[32,1024]{1,0:T(8,128)(2,1)S(1)} collective-permute-done((bf16[32,1024]{1,0:T(8,128)(2,1)S(1)}, bf16[32,1024]{1,0:T(8,128)(2,1)S(1)}, u32[]{:S(2)}, u32[]{:S(2)}) %collective-permute-start.2) | collective-permute-done | bytes 65568 | tf_op jit(solution)/shard_map/ppermute | solution.py:21
  29.8 1.6 %collective-permute-start.9 = (bf16[32,1152]{1,0:T(8,128)(2,1)S(1)}, bf16[32,1152]{1,0:T(8,128)(2,1)S(1)}, u32[]{:S(2)}, u32[]{:S(2)}) collective-permute-start(bf16[32,1152]{1,0:T(8,128)(2,1)S(1)} %fusion), channel_id=1, source_target_pairs={{0,4},{1,3},{2,6},{3,1},{4,0},{5,7},{6,2},{7,5},{8,12},{9,11},{10,... | collective-permute-start | bytes 221192 | tf_op jit(solution)/shard_map/ppermute | solution.py:21
  31.4 1.9 %collective-permute-done.3 = bf16[32,1024]{1,0:T(8,128)(2,1)S(1)} collective-permute-done((bf16[32,1024]{1,0:T(8,128)(2,1)S(1)}, bf16[32,1024]{1,0:T(8,128)(2,1)S(1)}, u32[]{:S(2)}, u32[]{:S(2)}) %collective-permute-start.3) | collective-permute-done | bytes 65568 | tf_op jit(solution)/shard_map/ppermute | solution.py:21
  33.3 1.8 %collective-permute-start.4 = (bf16[64,1024]{1,0:T(8,128)(2,1)S(1)}, bf16[64,1024]{1,0:T(8,128)(2,1)S(1)}, u32[]{:S(2)}, u32[]{:S(2)}) collective-permute-start(bf16[64,1024]{1,0:T(8,128)(2,1)S(1)} %pad_maximum_fusion.6), channel_id=1, source_target_pairs={{0,2},{1,5},{2,0},{3,7},{4,6},{5,1},{6,4},{7,3},{8,10},{9,13},{10,... | collective-permute-start | bytes 393224 | tf_op jit(solution)/shard_map/ppermute | solution.py:21
  35.2 1.6 %collective-permute-start.10 = (bf16[64,1152]{1,0:T(8,128)(2,1)S(1)}, bf16[64,1152]{1,0:T(8,128)(2,1)S(1)}, u32[]{:S(2)}, u32[]{:S(2)}) collective-permute-start(bf16[64,1152]{1,0:T(8,128)(2,1)S(1)} %pad_maximum_fusion.5), channel_id=1, source_target_pairs={{0,2},{1,5},{2,0},{3,7},{4,6},{5,1},{6,4},{7,3},{8,10},{9,13},{10,... | collective-permute-start | bytes 442376 | tf_op jit(solution)/shard_map/ppermute | solution.py:21
  36.7 1.6 %collective-permute-done.4 = bf16[64,1024]{1,0:T(8,128)(2,1)S(1)} collective-permute-done((bf16[64,1024]{1,0:T(8,128)(2,1)S(1)}, bf16[64,1024]{1,0:T(8,128)(2,1)S(1)}, u32[]{:S(2)}, u32[]{:S(2)}) %collective-permute-start.4) | collective-permute-done | bytes 131104 | tf_op jit(solution)/shard_map/ppermute | solution.py:21
  38.5 1.9 %collective-permute-done.10 = bf16[64,1152]{1,0:T(8,128)(2,1)S(1)} collective-permute-done((bf16[64,1152]{1,0:T(8,128)(2,1)S(1)}, bf16[64,1152]{1,0:T(8,128)(2,1)S(1)}, u32[]{:S(2)}, u32[]{:S(2)}) %collective-permute-start.10) | collective-permute-done | bytes 147488 | tf_op jit(solution)/shard_map/ppermute | solution.py:21
  40.5 1.5 %collective-permute-done.11 = bf16[128,1152]{1,0:T(8,128)(2,1)S(1)} collective-permute-done((bf16[128,1152]{1,0:T(8,128)(2,1)S(1)}, bf16[128,1152]{1,0:T(8,128)(2,1)S(1)}, u32[]{:S(2)}, u32[]{:S(2)}) %collective-permute-start.11) | collective-permute-done | bytes 294944 | tf_op jit(solution)/shard_map/ppermute | solution.py:21
  42.1 5.5 %experts.1 = (f32[128,1024]{1,0:T(8,128)S(1)}, bf16[128,1024]{1,0:T(8,128)(2,1)S(1)}, f32[128,1024]{1,0:T(8,128)S(1)}, bf16[128,1024]{1,0:T(8,128)(2,1)S(1)}) custom-call(bf16[256,1024]{1,0:T(8,128)(2,1)S(1)} %pad_maximum_fusion.1.refs_0_, bf16[256,1152]{1,0:T(8,128)(2,1)S(1)} %pad_maximum_fusion.refs_1_, bf16[1,2048,768]{2,1,0:T(8,128)(2,1)S(1)} %copy-done, ...), custom_call_target="tpu_custom_call" | custom-call | tf_op jit(solution)/shard_map/experts/pallas_call | solution.py:208
  49.3 1.6 %collective-permute-start.13 = (bf16[64,1024]{1,0:T(8,128)(2,1)S(1)}, bf16[64,1024]{1,0:T(8,128)(2,1)S(1)}, u32[]{:S(2)}, u32[]{:S(2)}) collective-permute-start(bf16[64,1024]{1,0:T(8,128)(2,1)S(1)} %slice.133), channel_id=1, source_target_pairs={{0,2},{1,5},{2,0},{3,7},{4,6},{5,1},{6,4},{7,3},{8,10},{9,13},{10,... | collective-permute-start | bytes 393224 | tf_op jit(solution)/shard_map/ppermute | solution.py:21
  51.5 2.8 %collective-permute-done.13 = bf16[64,1024]{1,0:T(8,128)(2,1)S(1)} collective-permute-done((bf16[64,1024]{1,0:T(8,128)(2,1)S(1)}, bf16[64,1024]{1,0:T(8,128)(2,1)S(1)}, u32[]{:S(2)}, u32[]{:S(2)}) %collective-permute-start.13) | collective-permute-done | bytes 131104 | tf_op jit(solution)/shard_map/ppermute | solution.py:21
  54.4 1.5 %collective-permute-start.14 = (bf16[32,1024]{1,0:T(8,128)(2,1)S(1)}, bf16[32,1024]{1,0:T(8,128)(2,1)S(1)}, u32[]{:S(2)}, u32[]{:S(2)}) collective-permute-start(bf16[32,1024]{1,0:T(8,128)(2,1)S(1)} %slice.135), channel_id=1, source_target_pairs={{0,4},{1,3},{2,6},{3,1},{4,0},{5,7},{6,2},{7,5},{8,12},{9,11},{10,... | collective-permute-start | bytes 196616 | tf_op jit(solution)/shard_map/ppermute | solution.py:21
  56.0 1.4 %collective-permute-start.18 = (bf16[32,1024]{1,0:T(8,128)(2,1)S(1)}, bf16[32,1024]{1,0:T(8,128)(2,1)S(1)}, u32[]{:S(2)}, u32[]{:S(2)}) collective-permute-start(bf16[32,1024]{1,0:T(8,128)(2,1)S(1)} %slice.134), channel_id=1, source_target_pairs={{0,4},{1,3},{2,6},{3,1},{4,0},{5,7},{6,2},{7,5},{8,12},{9,11},{10,... | collective-permute-start | bytes 196616 | tf_op jit(solution)/shard_map/ppermute | solution.py:21
  58.7 2.1 %collective-permute-start.15 = (bf16[16,1024]{1,0:T(8,128)(2,1)S(1)}, bf16[16,1024]{1,0:T(8,128)(2,1)S(1)}, u32[]{:S(2)}, u32[]{:S(2)}) collective-permute-start(bf16[16,1024]{1,0:T(8,128)(2,1)S(1)} %slice.139), channel_id=1, source_target_pairs={{0,8},{1,9},{2,10},{3,11},{4,12},{5,13},{6,14},{7,15},{8,0},{9,1},... | collective-permute-start | bytes 98312 | tf_op jit(solution)/shard_map/ppermute | solution.py:21
  60.9 2.0 %collective-permute-start.19 = (bf16[16,1024]{1,0:T(8,128)(2,1)S(1)}, bf16[16,1024]{1,0:T(8,128)(2,1)S(1)}, u32[]{:S(2)}, u32[]{:S(2)}) collective-permute-start(bf16[16,1024]{1,0:T(8,128)(2,1)S(1)} %slice.138), channel_id=1, source_target_pairs={{0,8},{1,9},{2,10},{3,11},{4,12},{5,13},{6,14},{7,15},{8,0},{9,1},... | collective-permute-start | bytes 98312 | tf_op jit(solution)/shard_map/ppermute | solution.py:21
  64.0 1.8 %collective-permute-done.19 = bf16[16,1024]{1,0:T(8,128)(2,1)S(1)} collective-permute-done((bf16[16,1024]{1,0:T(8,128)(2,1)S(1)}, bf16[16,1024]{1,0:T(8,128)(2,1)S(1)}, u32[]{:S(2)}, u32[]{:S(2)}) %collective-permute-start.19) | collective-permute-done | bytes 32800 | tf_op jit(solution)/shard_map/ppermute | solution.py:21
  (69 shorter events, 14.3 us)
Async XLA Ops:
  1.5 1.6 %copy-start.1 = (bf16[512,2048]{1,0:T(8,128)(2,1)S(1)}, bf16[512,2048]{1,0:T(8,128)(2,1)}, u32[]{:S(2)}) copy-start(bf16[512,2048]{1,0:T(8,128)(2,1)} %w_out.1) | copy-start | bytes 6291460
  3.1 0.9 %copy-start.2 = (bf16[2,16,32,128]{3,2,1,0:T(8,128)(2,1)S(1)}, bf16[2,16,32,128]{3,2,1,0:T(8,128)(2,1)}, u32[]{:S(2)}) copy-start(bf16[2,16,32,128]{3,2,1,0:T(8,128)(2,1)} %kv_cache.1) | copy-start | bytes 786436
  4.1 0.9 %copy-start.3 = (bf16[128,512]{1,0:T(8,128)(2,1)S(1)}, bf16[128,512]{1,0:T(8,128)(2,1)}, u32[]{:S(2)}) copy-start(bf16[128,512]{1,0:T(8,128)(2,1)} %queries.1) | copy-start | bytes 393220
  10.8 6.0 %collective-permute-start = (bf16[64,1024]{1,0:T(8,128)(2,1)S(1)}, bf16[64,1024]{1,0:T(8,128)(2,1)S(1)}, u32[]{:S(2)}, u32[]{:S(2)}) collective-permute-start(bf16[64,1024]{1,0:T(8,128)(2,1)S(1)} %get-tuple-element.15), channel_id=1, source_target_pairs={{0,2},{1,5},{2,0},{3,7},{4,6},{5,1},{6,4},{7,3},{8,10},{9,13},{10,... | collective-permute-start | bytes 393224 | tf_op jit(solution)/shard_map/ppermute | solution.py:21
  13.9 5.1 %collective-permute-start.6 = (bf16[64,1024]{1,0:T(8,128)(2,1)S(1)}, bf16[64,1024]{1,0:T(8,128)(2,1)S(1)}, u32[]{:S(2)}, u32[]{:S(2)}) collective-permute-start(bf16[64,1024]{1,0:T(8,128)(2,1)S(1)} %get-tuple-element.17), channel_id=1, source_target_pairs={{0,2},{1,5},{2,0},{3,7},{4,6},{5,1},{6,4},{7,3},{8,10},{9,13},{10,... | collective-permute-start | bytes 393224 | tf_op jit(solution)/shard_map/ppermute | solution.py:21
  16.9 4.4 %collective-permute-start.1 = (bf16[32,1024]{1,0:T(8,128)(2,1)S(1)}, bf16[32,1024]{1,0:T(8,128)(2,1)S(1)}, u32[]{:S(2)}, u32[]{:S(2)}) collective-permute-start(bf16[32,1024]{1,0:T(8,128)(2,1)S(1)} %slice.137), channel_id=1, source_target_pairs={{0,4},{1,3},{2,6},{3,1},{4,0},{5,7},{6,2},{7,5},{8,12},{9,11},{10,... | collective-permute-start | bytes 196616 | tf_op jit(solution)/shard_map/ppermute | solution.py:21
  19.1 5.3 %collective-permute-start.7 = (bf16[32,1024]{1,0:T(8,128)(2,1)S(1)}, bf16[32,1024]{1,0:T(8,128)(2,1)S(1)}, u32[]{:S(2)}, u32[]{:S(2)}) collective-permute-start(bf16[32,1024]{1,0:T(8,128)(2,1)S(1)} %slice.136), channel_id=1, source_target_pairs={{0,4},{1,3},{2,6},{3,1},{4,0},{5,7},{6,2},{7,5},{8,12},{9,11},{10,... | collective-permute-start | bytes 196616 | tf_op jit(solution)/shard_map/ppermute | solution.py:21
  21.3 7.2 %collective-permute-start.2 = (bf16[32,1024]{1,0:T(8,128)(2,1)S(1)}, bf16[32,1024]{1,0:T(8,128)(2,1)S(1)}, u32[]{:S(2)}, u32[]{:S(2)}) collective-permute-start(bf16[32,1024]{1,0:T(8,128)(2,1)S(1)} %fusion.3), channel_id=1, source_target_pairs={{0,8},{1,9},{2,10},{3,11},{4,12},{5,13},{6,14},{7,15},{8,0},{9,1},... | collective-permute-start | bytes 196616 | tf_op jit(solution)/shard_map/ppermute | solution.py:21
  24.4 5.3 %collective-permute-start.8 = (bf16[32,1152]{1,0:T(8,128)(2,1)S(1)}, bf16[32,1152]{1,0:T(8,128)(2,1)S(1)}, u32[]{:S(2)}, u32[]{:S(2)}) collective-permute-start(bf16[32,1152]{1,0:T(8,128)(2,1)S(1)} %fusion.2), channel_id=1, source_target_pairs={{0,8},{1,9},{2,10},{3,11},{4,12},{5,13},{6,14},{7,15},{8,0},{9,1},... | collective-permute-start | bytes 221192 | tf_op jit(solution)/shard_map/ppermute | solution.py:21
  28.6 4.8 %collective-permute-start.3 = (bf16[32,1024]{1,0:T(8,128)(2,1)S(1)}, bf16[32,1024]{1,0:T(8,128)(2,1)S(1)}, u32[]{:S(2)}, u32[]{:S(2)}) collective-permute-start(bf16[32,1024]{1,0:T(8,128)(2,1)S(1)} %fusion.1), channel_id=1, source_target_pairs={{0,4},{1,3},{2,6},{3,1},{4,0},{5,7},{6,2},{7,5},{8,12},{9,11},{10,... | collective-permute-start | bytes 196616 | tf_op jit(solution)/shard_map/ppermute | solution.py:21
  29.8 5.4 %collective-permute-start.9 = (bf16[32,1152]{1,0:T(8,128)(2,1)S(1)}, bf16[32,1152]{1,0:T(8,128)(2,1)S(1)}, u32[]{:S(2)}, u32[]{:S(2)}) collective-permute-start(bf16[32,1152]{1,0:T(8,128)(2,1)S(1)} %fusion), channel_id=1, source_target_pairs={{0,4},{1,3},{2,6},{3,1},{4,0},{5,7},{6,2},{7,5},{8,12},{9,11},{10,... | collective-permute-start | bytes 221192 | tf_op jit(solution)/shard_map/ppermute | solution.py:21
  33.3 5.0 %collective-permute-start.4 = (bf16[64,1024]{1,0:T(8,128)(2,1)S(1)}, bf16[64,1024]{1,0:T(8,128)(2,1)S(1)}, u32[]{:S(2)}, u32[]{:S(2)}) collective-permute-start(bf16[64,1024]{1,0:T(8,128)(2,1)S(1)} %pad_maximum_fusion.6), channel_id=1, source_target_pairs={{0,2},{1,5},{2,0},{3,7},{4,6},{5,1},{6,4},{7,3},{8,10},{9,13},{10,... | collective-permute-start | bytes 393224 | tf_op jit(solution)/shard_map/ppermute | solution.py:21
  35.2 5.2 %collective-permute-start.10 = (bf16[64,1152]{1,0:T(8,128)(2,1)S(1)}, bf16[64,1152]{1,0:T(8,128)(2,1)S(1)}, u32[]{:S(2)}, u32[]{:S(2)}) collective-permute-start(bf16[64,1152]{1,0:T(8,128)(2,1)S(1)} %pad_maximum_fusion.5), channel_id=1, source_target_pairs={{0,2},{1,5},{2,0},{3,7},{4,6},{5,1},{6,4},{7,3},{8,10},{9,13},{10,... | collective-permute-start | bytes 442376 | tf_op jit(solution)/shard_map/ppermute | solution.py:21
  38.4 3.7 %copy-start = (bf16[1,2048,768]{2,1,0:T(8,128)(2,1)S(1)}, bf16[1,2048,768]{2,1,0:T(8,128)(2,1)}, u32[]{:S(2)}) copy-start(bf16[1,2048,768]{2,1,0:T(8,128)(2,1)} %refs_2_.1) | copy-start | bytes 9437188
  38.4 2.1 %collective-permute-start.5 = (bf16[128,1024]{1,0:T(8,128)(2,1)S(1)}, bf16[128,1024]{1,0:T(8,128)(2,1)S(1)}, u32[]{:S(2)}, u32[]{:S(2)}) collective-permute-start(bf16[128,1024]{1,0:T(8,128)(2,1)S(1)} %pad_maximum_fusion.3), channel_id=1, source_target_pairs={{0,1},{1,0},{2,3},{3,2},{4,5},{5,4},{6,7},{7,6},{8,9},{9,8},{10,11... | collective-permute-start | bytes 786440 | tf_op jit(solution)/shard_map/ppermute | solution.py:21
  40.4 1.6 %collective-permute-start.11 = (bf16[128,1152]{1,0:T(8,128)(2,1)S(1)}, bf16[128,1152]{1,0:T(8,128)(2,1)S(1)}, u32[]{:S(2)}, u32[]{:S(2)}) collective-permute-start(bf16[128,1152]{1,0:T(8,128)(2,1)S(1)} %pad_maximum_fusion.2), channel_id=1, source_target_pairs={{0,1},{1,0},{2,3},{3,2},{4,5},{5,4},{6,7},{7,6},{8,9},{9,8},{10,11... | collective-permute-start | bytes 884744 | tf_op jit(solution)/shard_map/ppermute | solution.py:21
  47.6 1.6 %collective-permute-start.12 = (bf16[128,1024]{1,0:T(8,128)(2,1)S(1)}, bf16[128,1024]{1,0:T(8,128)(2,1)S(1)}, u32[]{:S(2)}, u32[]{:S(2)}) collective-permute-start(bf16[128,1024]{1,0:T(8,128)(2,1)S(1)} %get-tuple-element.20), channel_id=1, source_target_pairs={{0,1},{1,0},{2,3},{3,2},{4,5},{5,4},{6,7},{7,6},{8,9},{9,8},{10,11... | collective-permute-start | bytes 786440 | tf_op jit(solution)/shard_map/ppermute | solution.py:21
  47.8 3.1 %collective-permute-start.16 = (bf16[128,1024]{1,0:T(8,128)(2,1)S(1)}, bf16[128,1024]{1,0:T(8,128)(2,1)S(1)}, u32[]{:S(2)}, u32[]{:S(2)}) collective-permute-start(bf16[128,1024]{1,0:T(8,128)(2,1)S(1)} %get-tuple-element.22), channel_id=1, source_target_pairs={{0,1},{1,0},{2,3},{3,2},{4,5},{5,4},{6,7},{7,6},{8,9},{9,8},{10,11... | collective-permute-start | bytes 786440 | tf_op jit(solution)/shard_map/ppermute | solution.py:21
  49.3 5.0 %collective-permute-start.13 = (bf16[64,1024]{1,0:T(8,128)(2,1)S(1)}, bf16[64,1024]{1,0:T(8,128)(2,1)S(1)}, u32[]{:S(2)}, u32[]{:S(2)}) collective-permute-start(bf16[64,1024]{1,0:T(8,128)(2,1)S(1)} %slice.133), channel_id=1, source_target_pairs={{0,2},{1,5},{2,0},{3,7},{4,6},{5,1},{6,4},{7,3},{8,10},{9,13},{10,... | collective-permute-start | bytes 393224 | tf_op jit(solution)/shard_map/ppermute | solution.py:21
  50.9 5.0 %collective-permute-start.17 = (bf16[64,1024]{1,0:T(8,128)(2,1)S(1)}, bf16[64,1024]{1,0:T(8,128)(2,1)S(1)}, u32[]{:S(2)}, u32[]{:S(2)}) collective-permute-start(bf16[64,1024]{1,0:T(8,128)(2,1)S(1)} %slice.132), channel_id=1, source_target_pairs={{0,2},{1,5},{2,0},{3,7},{4,6},{5,1},{6,4},{7,3},{8,10},{9,13},{10,... | collective-permute-start | bytes 393224 | tf_op jit(solution)/shard_map/ppermute | solution.py:21
  54.4 4.3 %collective-permute-start.14 = (bf16[32,1024]{1,0:T(8,128)(2,1)S(1)}, bf16[32,1024]{1,0:T(8,128)(2,1)S(1)}, u32[]{:S(2)}, u32[]{:S(2)}) collective-permute-start(bf16[32,1024]{1,0:T(8,128)(2,1)S(1)} %slice.135), channel_id=1, source_target_pairs={{0,4},{1,3},{2,6},{3,1},{4,0},{5,7},{6,2},{7,5},{8,12},{9,11},{10,... | collective-permute-start | bytes 196616 | tf_op jit(solution)/shard_map/ppermute | solution.py:21
  56.0 4.8 %collective-permute-start.18 = (bf16[32,1024]{1,0:T(8,128)(2,1)S(1)}, bf16[32,1024]{1,0:T(8,128)(2,1)S(1)}, u32[]{:S(2)}, u32[]{:S(2)}) collective-permute-start(bf16[32,1024]{1,0:T(8,128)(2,1)S(1)} %slice.134), channel_id=1, source_target_pairs={{0,4},{1,3},{2,6},{3,1},{4,0},{5,7},{6,2},{7,5},{8,12},{9,11},{10,... | collective-permute-start | bytes 196616 | tf_op jit(solution)/shard_map/ppermute | solution.py:21
  58.7 5.2 %collective-permute-start.15 = (bf16[16,1024]{1,0:T(8,128)(2,1)S(1)}, bf16[16,1024]{1,0:T(8,128)(2,1)S(1)}, u32[]{:S(2)}, u32[]{:S(2)}) collective-permute-start(bf16[16,1024]{1,0:T(8,128)(2,1)S(1)} %slice.139), channel_id=1, source_target_pairs={{0,8},{1,9},{2,10},{3,11},{4,12},{5,13},{6,14},{7,15},{8,0},{9,1},... | collective-permute-start | bytes 98312 | tf_op jit(solution)/shard_map/ppermute | solution.py:21
  60.9 4.9 %collective-permute-start.19 = (bf16[16,1024]{1,0:T(8,128)(2,1)S(1)}, bf16[16,1024]{1,0:T(8,128)(2,1)S(1)}, u32[]{:S(2)}, u32[]{:S(2)}) collective-permute-start(bf16[16,1024]{1,0:T(8,128)(2,1)S(1)} %slice.138), channel_id=1, source_target_pairs={{0,8},{1,9},{2,10},{3,11},{4,12},{5,13},{6,14},{7,15},{8,0},{9,1},... | collective-permute-start | bytes 98312 | tf_op jit(solution)/shard_map/ppermute | solution.py:21
  (4 other events, 2.9 us)

commit v2 on v1

--- a/solution.py
+++ b/solution.py
@@ -8,12 +8,18 @@
 from jax.sharding import PartitionSpec as P
 
 ATT_TP = 8
-CHUNKS = 2
+PIECES = (8, 8)
+CHUNKS = len(PIECES)
 LANES = 128
 
 
 def bits_of(count):
     return count.bit_length() - 1
+
+
+def column_cuts(features):
+    ends = [features * sum(PIECES[: c + 1]) // sum(PIECES) for c in range(CHUNKS)]
+    return list(zip([0] + ends[:-1], ends))
 
 
 def exchange(block, masks):
@@ -40,22 +46,20 @@
     return masks
 
 
-def attend_kernel(
-    axis_width,
-    table,
-    lengths,
-    queries,
-    tree_kv,
-    kv_cache,
-    parents,
-    expert_ids,
-    gate_weights,
-    w_out,
-    *refs,
-):
-    outs, (extra, attended, weights_in, weights_sem) = refs[:-4], refs[-4:]
-    copy = pltpu.make_async_copy(w_out, weights_in, weights_sem)
-    copy.start()
+def attend_kernel(axis_width, *refs):
+    sources, outs, scratch = refs[:9], refs[9 : 10 + 2 * CHUNKS], refs[10 + 2 * CHUNKS :]
+    *inputs, attended, sems = scratch
+    copies = [
+        pltpu.make_async_copy(source, target, sems.at[n])
+        for n, (source, target) in enumerate(zip(sources, inputs))
+    ]
+    for copy in copies:
+        copy.start()
+    for copy in copies[:-1]:
+        copy.wait()
+    table, lengths, parents, expert_ids, gate_weights = inputs[:5]
+    queries, tree_kv, kv_cache, weights_in = inputs[5:]
+    *outs, extra = outs
     seq_count, node_count = parents.shape
     head_dim = tree_kv.shape[-1]
     head_count = queries.shape[1] // head_dim
@@ -109,17 +113,20 @@
                 h * node_count : (h + 1) * node_count
             ]
 
-    row_count, listed = expert_ids.shape
-    lane = lax.broadcasted_iota(jnp.int32, (row_count, extra.shape[1]), 1)
-    weight = jnp.zeros((row_count, extra.shape[1]), f32)
+    listed, row_count = expert_ids.shape
+    spread_width = extra.shape[1]
+    expert = lax.broadcasted_iota(jnp.int32, (spread_width, row_count), 0)
+    weight = jnp.zeros((spread_width, row_count), f32)
     for k in range(listed):
         weight += jnp.where(
-            expert_ids[:, k : k + 1] == lane % axis_width, gate_weights[:, k : k + 1], 0.0
+            expert_ids[k : k + 1, :] == expert % axis_width, gate_weights[k : k + 1, :], 0.0
         )
     upper = weight.astype(bf16).astype(f32)
-    parts = jnp.where(lane < axis_width, upper, jnp.where(lane < 2 * axis_width, weight - upper, 0.0))
-    extra[:row_count] = parts.astype(bf16)
-    extra[row_count:] = jnp.zeros((row_count, extra.shape[1]), bf16)
+    parts = jnp.where(
+        expert < axis_width, upper, jnp.where(expert < 2 * axis_width, weight - upper, 0.0)
+    )
+    extra[:row_count] = parts.T.astype(bf16)
+    extra[row_count:] = jnp.zeros((row_count, spread_width), bf16)
 
     device = lax.axis_index("wide")
     groups = axis_width // ATT_TP
@@ -130,15 +137,20 @@
         target = (device ^ jnp.where(device & 1 == 0, one, other)) // groups
         picked.append(attended[pl.ds(pl.multiple_of(target * block, block), block), :])
     ordered = jnp.concatenate(picked, axis=0)
-    copy.wait()
+    copies[-1].wait()
     half = all_nodes // 2
-    width = outs[0].shape[1]
-    for c in range(len(outs) // 2):
-        projected = jnp.dot(
-            ordered, weights_in[:, c * width : (c + 1) * width], preferred_element_type=f32
-        )
+    for c, (low, high) in enumerate(column_cuts(weights_in.shape[1])):
+        projected = jnp.dot(ordered, weights_in[:, low:high], preferred_element_type=f32)
         outs[2 * c][...] = projected[:half]
         outs[2 * c + 1][...] = projected[half:].astype(bf16)
+
+
+def kept_and_sent(rows, cuts):
+    shapes = []
+    for low, high in cuts:
+        shapes.append(pltpu.VMEM((rows // 2, high - low), jnp.float32))
+        shapes.append(pltpu.VMEM((rows // 2, high - low), jnp.bfloat16))
+    return shapes
 
 
 def attend(queries, tree_kv, kv_cache, table, lengths, parents, w_out, expert_ids, gate_weights):
@@ -147,73 +159,122 @@
     rows = queries.shape[0]
     own_rows = expert_ids.shape[0]
     extra_width = -(-2 * axis_width // LANES) * LANES
-    smem = pl.BlockSpec(memory_space=pltpu.SMEM)
-    vmem = pl.BlockSpec(memory_space=pltpu.VMEM)
-    half = (rows // 2, features // CHUNKS)
-    kept, sent = jax.ShapeDtypeStruct(half, jnp.float32), jax.ShapeDtypeStruct(half, jnp.bfloat16)
+    halves = kept_and_sent(rows, column_cuts(features))
+    given = [table, lengths, parents, expert_ids.T, gate_weights.T, queries, tree_kv, kv_cache, w_out]
+    spaces = [pltpu.SMEM] * 2 + [pltpu.VMEM] * (len(given) - 2)
+    given = [pltpu.with_memory_space_constraint(x, pltpu.HBM) for x in given]
     return pl.pallas_call(
         functools.partial(attend_kernel, axis_width),
-        out_shape=[kept, sent] * CHUNKS
-        + [jax.ShapeDtypeStruct((2 * own_rows, extra_width), jnp.bfloat16)],
-        in_specs=[smem, smem] + [vmem] * 6 + [pl.BlockSpec(memory_space=pl.ANY)],
-        out_specs=[vmem] * (2 * CHUNKS + 1),
-        scratch_shapes=[
-            pltpu.VMEM(queries.shape, jnp.bfloat16),
-            pltpu.VMEM(w_out.shape, jnp.bfloat16),
-            pltpu.SemaphoreType.DMA,
-        ],
+        out_shape=halves
+        + [pltpu.VMEM((2 * own_rows, extra_width), jnp.bfloat16)],
+        in_specs=[pl.BlockSpec(memory_space=pltpu.HBM)] * len(given),
+        out_specs=[pl.BlockSpec(memory_space=pltpu.VMEM)] * (2 * CHUNKS + 1),
+        scratch_shapes=[space(x.shape, x.dtype) for space, x in zip(spaces, given)]
+        + [pltpu.VMEM(queries.shape, jnp.bfloat16), pltpu.SemaphoreType.DMA((len(given),))],
         compiler_params=pltpu.CompilerParams(vmem_limit_bytes=16 * 1024 * 1024),
         name="attend",
-    )(table, lengths, queries, tree_kv, kv_cache, parents, expert_ids, gate_weights, w_out)
-
-
-def experts_kernel(axis_width, tile, *refs):
-    hidden, (w_gate, w_up, w_down) = refs[:CHUNKS], refs[CHUNKS : CHUNKS + 3]
-    outs, activated = refs[CHUNKS + 3 : -1], refs[-1]
+    )(*given)
+
+
+def feed_kernel(cut, tile, first, *refs):
+    hidden, w_gate, w_up = refs[:3]
+    before, after = ((), refs[3:]) if first else (refs[3:5], refs[5:])
+    width = cut[1] - cut[0]
+    for n in range(w_gate.shape[2] // tile):
+        columns = slice(n * tile, (n + 1) * tile)
+        for m, weights in enumerate((w_gate, w_up)):
+            share = jnp.dot(
+                hidden[:, :width],
+                weights[0, cut[0] : cut[1], columns],
+                preferred_element_type=jnp.float32,
+            )
+            after[m][:, columns] = share if first else before[m][:, columns] + share
+
+
+def finish_kernel(axis_width, cut, out_cut, tile, hidden, w_gate, w_up, w_down, gate, up, *outs):
+    kept, sent, activated, row_weight = outs
     f32, bf16 = jnp.float32, jnp.bfloat16
-    width = outs[0].shape[1]
+    width = cut[1] - cut[0]
     device = lax.axis_index("wide")
-    parts = hidden[-1][:, width:]
+    parts = hidden[:, width:]
     lane = lax.broadcasted_iota(jnp.int32, parts.shape, 1)
     mine = (lane == device) | (lane == device + axis_width)
     weight = jnp.sum(jnp.where(mine, parts.astype(f32), 0.0), axis=1, keepdims=True)
-    hidden_width = activated.shape[1]
-    half = activated.shape[0] // 2
-    for n in range(hidden_width // tile):
-        cut = slice(n * tile, (n + 1) * tile)
-        gate_part = up_part = 0.0
-        for c in range(CHUNKS):
-            rows = hidden[c][:, :width]
-            down = slice(c * width, (c + 1) * width)
-            gate_part += jnp.dot(rows, w_gate[0, down, cut], preferred_element_type=f32)
-            up_part += jnp.dot(rows, w_up[0, down, cut], preferred_element_type=f32)
-        activated[:, cut] = (gate_part / (1.0 + jnp.exp(-gate_part)) * up_part).astype(bf16)
-    for c in range(CHUNKS):
-        for n in range(width // tile):
-            cut = slice(c * width + n * tile, c * width + (n + 1) * tile)
-            produced = jnp.dot(activated[...], w_down[0, :, cut], preferred_element_type=f32)
-            weighted = produced * weight
-            outs[2 * c][:, n * tile : (n + 1) * tile] = weighted[:half]
-            outs[2 * c + 1][:, n * tile : (n + 1) * tile] = weighted[half:].astype(bf16)
+    row_weight[...] = weight
+    for n in range(w_gate.shape[2] // tile):
+        columns = slice(n * tile, (n + 1) * tile)
+        rows = hidden[:, :width]
+        piece = slice(*cut)
+        gate_part = gate[:, columns] + jnp.dot(
+            rows, w_gate[0, piece, columns], preferred_element_type=f32
+        )
+        up_part = up[:, columns] + jnp.dot(
+            rows, w_up[0, piece, columns], preferred_element_type=f32
+        )
+        activated[:, columns] = (gate_part / (1.0 + jnp.exp(-gate_part)) * up_part).astype(bf16)
+    produce(activated, w_down.at[0, :, slice(*out_cut)], weight, kept, sent, tile)
+
+
+def down_kernel(cut, tile, activated, row_weight, w_down, kept, sent):
+    produce(activated, w_down.at[0, :, slice(*cut)], row_weight[...], kept, sent, tile)
+
+
+def produce(activated, w_down, weight, kept, sent, tile):
+    half, width = kept.shape
+    for start in range(0, width, tile):
+        columns = slice(start, min(start + tile, width))
+        produced = jnp.dot(
+            activated[...], w_down[:, columns], preferred_element_type=jnp.float32
+        )
+        weighted = produced * weight
+        kept[:, columns] = weighted[:half]
+        sent[:, columns] = weighted[half:].astype(jnp.bfloat16)
+
+
+def local_call(kernel, name, out_shape, given):
+    return pl.pallas_call(
+        kernel,
+        out_shape=out_shape,
+        in_specs=[pl.BlockSpec(memory_space=pltpu.VMEM)] * len(given),
+        out_specs=[pl.BlockSpec(memory_space=pltpu.VMEM)] * len(out_shape),
+        compiler_params=pltpu.CompilerParams(vmem_limit_bytes=16 * 1024 * 1024),
+        name=name,
+    )(*given)
 
 
 def experts(hidden, w_gate, w_up, w_down):
     axis_width = lax.axis_size("wide")
     rows = hidden[0].shape[0]
     hidden_width, features = w_down.shape[1:]
-    vmem = pl.BlockSpec(memory_space=pltpu.VMEM)
+    cuts = column_cuts(features)
     tile = 256 if hidden_width % 256 == 0 else LANES
-    half = (rows // 2, features // CHUNKS)
-    kept, sent = jax.ShapeDtypeStruct(half, jnp.float32), jax.ShapeDtypeStruct(half, jnp.bfloat16)
-    return pl.pallas_call(
-        functools.partial(experts_kernel, axis_width, tile),
-        out_shape=[kept, sent] * CHUNKS,
-        in_specs=[vmem] * (CHUNKS + 3),
-        out_specs=[vmem] * (2 * CHUNKS),
-        scratch_shapes=[pltpu.VMEM((rows, hidden_width), jnp.bfloat16)],
-        compiler_params=pltpu.CompilerParams(vmem_limit_bytes=48 * 1024 * 1024),
-        name="experts",
-    )(*hidden, w_gate, w_up, w_down)
+    wide = pltpu.VMEM((rows, hidden_width), jnp.float32)
+    sums = []
+    for c in range(CHUNKS - 1):
+        given = [hidden[c], w_gate, w_up, *sums]
+        kernel = functools.partial(feed_kernel, cuts[c], tile, c == 0)
+        sums = local_call(kernel, "feed", [wide, wide], given)
+    kept, sent, activated, row_weight = local_call(
+        functools.partial(finish_kernel, axis_width, cuts[-1], cuts[0], tile),
+        "finish",
+        kept_and_sent(rows, cuts[:1])
+        + [
+            pltpu.VMEM((rows, hidden_width), jnp.bfloat16),
+            pltpu.VMEM((rows, 1), jnp.float32),
+        ],
+        [hidden[-1], w_gate, w_up, w_down, *sums],
+    )
+    produced = [(kept, sent)]
+    for c in range(1, CHUNKS):
+        produced.append(
+            local_call(
+                functools.partial(down_kernel, cuts[c], tile),
+                "down",
+                kept_and_sent(rows, cuts[c : c + 1]),
+                [activated, row_weight, w_down],
+            )
+        )
+    return produced
 
 
 def halved(block):
@@ -261,7 +322,7 @@
     produced = experts(hidden, w_gate, w_up, w_down)
     results = []
     for c in range(CHUNKS):
-        kept, sent = produced[2 * c], produced[2 * c + 1]
+        kept, sent = produced[c]
         last = len(group_steps) + len(steps) - 1
         for number, masks in enumerate(group_steps[::-1] + steps):
             kept = kept + exchange(sent, masks).astype(jnp.float32)

time: 66.8 us -> 55.7 us (0.83)
  local copies, waits for them, and re-layouts: 7.92 us -> 0.46 us
  Pallas kernels: 8.47 us -> 6.41 us
  waiting for transfers between devices: 21.9 us -> 20 us
    unnamed x18 -> x6, local copies, waits for them, and re-layouts: 7.82 us -> 0.36 us
    pallas_call x2 -> x4, Pallas kernels: 8.47 us -> 6.41 us  [the longest x1 3.46 us: attend(): pl.pallas_call(functools.partial(attend_kernel, axis_width), out_shape=ha...]
    ppermute x20, waiting for transfers between devices: 21.9 us -> 20 us  [exchange(): lax.ppermute(block, 'wide', [(i, i ^ masks[i & 1]) for i in range(count)])]
  transfers between devices with their start and end apart: 20 -> 20, of which waited for: 14 -> 14; matrix products, arithmetic and copies ran while one was open for 1% -> 1% of each run, Pallas kernels for 0% -> 3%
where the time goes in v2:
time: 55.7 us; the launch traced here: 55.5 us
  starting transfers between devices  27.2 us (49%)
  waiting for transfers between devices  20 us (36%)
  Pallas kernels  6.41 us (12%)
  other arithmetic  1.16 us (2%)
    ppermute x20, starting transfers between devices, exchange(): lax.ppermute(block, 'wide', [(i, i ^ masks[i & 1]) for i in range(count)])  27.2 us
    ppermute x20, waiting for transfers between devices, exchange(): lax.ppermute(block, 'wide', [(i, i ^ masks[i & 1]) for i in range(count)])  20 us
    pallas_call x1, Pallas kernels, attend(): pl.pallas_call(functools.partial(attend_kernel, axis_width), out_shape=ha...  3.46 us
    pallas_call x3, Pallas kernels, local_call(): pl.pallas_call(kernel, out_shape=out_shape, in_specs=[pl.BlockSpec(memory...  2.95 us
  transfers between devices with their start and end apart: 20, of which 14 were waited for; matrix products, arithmetic and copies ran while one was open for 1% of the time, Pallas kernels for 3%

profile of v2, /device:TPU:0, one launch (start us, length us, event | category | flops | bytes accessed | tf_op | source)
XLA Modules:
  0.0 55.5 jit_solution(1841886394664155992)
XLA Ops:
  0.0 3.5 %attend.1 = (f32[64,1024]{1,0:T(8,128)S(1)}, bf16[64,1024]{1,0:T(8,128)(2,1)S(1)}, f32[64,1024]{1,0:T(8,128)S(1)}, bf16[64,1024]{1,0:T(8,128)(2,1)S(1)}, bf16[32,128]{1,0:T(8,128)(2,1)S(1)}) custom-call(s32[4,4]{1,0:T(4,128)} %refs_0_.1, s32[1,4]{1,0:T(1,128)} %refs_1_.2, s32[4,32]{1,0:T(4,128)} %refs_2_.2, s32[8,16]{1,0:T(8,128)} %bitcast.2, ...), custom_call_target="tpu_custom_call" | custom-call | tf_op jit(solution)/shard_map/attend/pallas_call | solution.py:166
  3.5 3.0 %collective-permute-start.6 = (bf16[64,1024]{1,0:T(8,128)(2,1)S(1)}, bf16[64,1024]{1,0:T(8,128)(2,1)S(1)}, u32[]{:S(2)}, u32[]{:S(2)}) collective-permute-start(bf16[64,1024]{1,0:T(8,128)(2,1)S(1)} %get-tuple-element.22), channel_id=1, source_target_pairs={{0,2},{1,5},{2,0},{3,7},{4,6},{5,1},{6,4},{7,3},{8,10},{9,13},{10,... | collective-permute-start | bytes 393224 | tf_op jit(solution)/shard_map/ppermute | solution.py:27
  6.6 2.9 %collective-permute-done.6 = bf16[64,1024]{1,0:T(8,128)(2,1)S(1)} collective-permute-done((bf16[64,1024]{1,0:T(8,128)(2,1)S(1)}, bf16[64,1024]{1,0:T(8,128)(2,1)S(1)}, u32[]{:S(2)}, u32[]{:S(2)}) %collective-permute-start.6) | collective-permute-done | bytes 131104 | tf_op jit(solution)/shard_map/ppermute | solution.py:27
  9.5 2.1 %collective-permute-start.7 = (bf16[32,1024]{1,0:T(8,128)(2,1)S(1)}, bf16[32,1024]{1,0:T(8,128)(2,1)S(1)}, u32[]{:S(2)}, u32[]{:S(2)}) collective-permute-start(bf16[32,1024]{1,0:T(8,128)(2,1)S(1)} %slice.136), channel_id=1, source_target_pairs={{0,4},{1,3},{2,6},{3,1},{4,0},{5,7},{6,2},{7,5},{8,12},{9,11},{10,... | collective-permute-start | bytes 196616 | tf_op jit(solution)/shard_map/ppermute | solution.py:27
  11.7 1.5 %collective-permute-start.1 = (bf16[32,1024]{1,0:T(8,128)(2,1)S(1)}, bf16[32,1024]{1,0:T(8,128)(2,1)S(1)}, u32[]{:S(2)}, u32[]{:S(2)}) collective-permute-start(bf16[32,1024]{1,0:T(8,128)(2,1)S(1)} %slice.137), channel_id=1, source_target_pairs={{0,4},{1,3},{2,6},{3,1},{4,0},{5,7},{6,2},{7,5},{8,12},{9,11},{10,... | collective-permute-start | bytes 196616 | tf_op jit(solution)/shard_map/ppermute | solution.py:27
  13.9 3.1 %collective-permute-start.8 = (bf16[32,1024]{1,0:T(8,128)(2,1)S(1)}, bf16[32,1024]{1,0:T(8,128)(2,1)S(1)}, u32[]{:S(2)}, u32[]{:S(2)}) collective-permute-start(bf16[32,1024]{1,0:T(8,128)(2,1)S(1)} %fusion.3), channel_id=1, source_target_pairs={{0,8},{1,9},{2,10},{3,11},{4,12},{5,13},{6,14},{7,15},{8,0},{9,1},... | collective-permute-start | bytes 196616 | tf_op jit(solution)/shard_map/ppermute | solution.py:27
  17.1 1.8 %collective-permute-start.2 = (bf16[32,1152]{1,0:T(8,128)(2,1)S(1)}, bf16[32,1152]{1,0:T(8,128)(2,1)S(1)}, u32[]{:S(2)}, u32[]{:S(2)}) collective-permute-start(bf16[32,1152]{1,0:T(8,128)(2,1)S(1)} %fusion.2), channel_id=1, source_target_pairs={{0,8},{1,9},{2,10},{3,11},{4,12},{5,13},{6,14},{7,15},{8,0},{9,1},... | collective-permute-start | bytes 221192 | tf_op jit(solution)/shard_map/ppermute | solution.py:27
  18.8 2.3 %collective-permute-done.8 = bf16[32,1024]{1,0:T(8,128)(2,1)S(1)} collective-permute-done((bf16[32,1024]{1,0:T(8,128)(2,1)S(1)}, bf16[32,1024]{1,0:T(8,128)(2,1)S(1)}, u32[]{:S(2)}, u32[]{:S(2)}) %collective-permute-start.8) | collective-permute-done | bytes 65568 | tf_op jit(solution)/shard_map/ppermute | solution.py:27
  22.4 1.6 %collective-permute-start.3 = (bf16[32,1152]{1,0:T(8,128)(2,1)S(1)}, bf16[32,1152]{1,0:T(8,128)(2,1)S(1)}, u32[]{:S(2)}, u32[]{:S(2)}) collective-permute-start(bf16[32,1152]{1,0:T(8,128)(2,1)S(1)} %fusion), channel_id=1, source_target_pairs={{0,4},{1,3},{2,6},{3,1},{4,0},{5,7},{6,2},{7,5},{8,12},{9,11},{10,... | collective-permute-start | bytes 221192 | tf_op jit(solution)/shard_map/ppermute | solution.py:27
  24.1 1.9 %collective-permute-done.9 = bf16[32,1024]{1,0:T(8,128)(2,1)S(1)} collective-permute-done((bf16[32,1024]{1,0:T(8,128)(2,1)S(1)}, bf16[32,1024]{1,0:T(8,128)(2,1)S(1)}, u32[]{:S(2)}, u32[]{:S(2)}) %collective-permute-start.9) | collective-permute-done | bytes 65568 | tf_op jit(solution)/shard_map/ppermute | solution.py:27
  26.0 1.8 %collective-permute-start.10 = (bf16[64,1024]{1,0:T(8,128)(2,1)S(1)}, bf16[64,1024]{1,0:T(8,128)(2,1)S(1)}, u32[]{:S(2)}, u32[]{:S(2)}) collective-permute-start(bf16[64,1024]{1,0:T(8,128)(2,1)S(1)} %pad_maximum_fusion.6), channel_id=1, source_target_pairs={{0,2},{1,5},{2,0},{3,7},{4,6},{5,1},{6,4},{7,3},{8,10},{9,13},{10,... | collective-permute-start | bytes 393224 | tf_op jit(solution)/shard_map/ppermute | solution.py:27
  27.8 1.6 %collective-permute-start.4 = (bf16[64,1152]{1,0:T(8,128)(2,1)S(1)}, bf16[64,1152]{1,0:T(8,128)(2,1)S(1)}, u32[]{:S(2)}, u32[]{:S(2)}) collective-permute-start(bf16[64,1152]{1,0:T(8,128)(2,1)S(1)} %pad_maximum_fusion.5), channel_id=1, source_target_pairs={{0,2},{1,5},{2,0},{3,7},{4,6},{5,1},{6,4},{7,3},{8,10},{9,13},{10,... | collective-permute-start | bytes 442376 | tf_op jit(solution)/shard_map/ppermute | solution.py:27
  29.4 1.6 %collective-permute-done.10 = bf16[64,1024]{1,0:T(8,128)(2,1)S(1)} collective-permute-done((bf16[64,1024]{1,0:T(8,128)(2,1)S(1)}, bf16[64,1024]{1,0:T(8,128)(2,1)S(1)}, u32[]{:S(2)}, u32[]{:S(2)}) %collective-permute-start.10) | collective-permute-done | bytes 131104 | tf_op jit(solution)/shard_map/ppermute | solution.py:27
  31.1 1.9 %collective-permute-done.4 = bf16[64,1152]{1,0:T(8,128)(2,1)S(1)} collective-permute-done((bf16[64,1152]{1,0:T(8,128)(2,1)S(1)}, bf16[64,1152]{1,0:T(8,128)(2,1)S(1)}, u32[]{:S(2)}, u32[]{:S(2)}) %collective-permute-start.4) | collective-permute-done | bytes 147488 | tf_op jit(solution)/shard_map/ppermute | solution.py:27
  33.2 1.0 %feed.1 = (f32[256,768]{1,0:T(8,128)S(1)}, f32[256,768]{1,0:T(8,128)S(1)}) custom-call(bf16[256,1024]{1,0:T(8,128)(2,1)S(1)} %pad_maximum_fusion.1.refs_0_, bf16[1,2048,768]{2,1,0:T(8,128)(2,1)S(1)} %copy-done.1, bf16[1,2048,768]{2,1,0:T(8,128)(2,1)S(1)} %copy-done.2), custom_call_target="tpu_custom_call" | custom-call | tf_op jit(solution)/shard_map/feed/pallas_call | solution.py:235
  35.1 1.4 %finish.1 = (f32[128,1024]{1,0:T(8,128)S(1)}, bf16[128,1024]{1,0:T(8,128)(2,1)S(1)}, bf16[256,768]{1,0:T(8,128)(2,1)S(1)}, f32[256,1]{1,0:T(8,128)S(1)}) custom-call(bf16[256,1152]{1,0:T(8,128)(2,1)S(1)} %pad_maximum_fusion.hidden, bf16[1,2048,768]{2,1,0:T(8,128)(2,1)S(1)} %copy-done.1, bf16[1,2048,768]{2,1,0:T(8,128)(2,1)S(1)} %copy-done.2, ...), custom_call_target="tpu_custom_call" | custom-call | tf_op jit(solution)/shard_map/finish/pallas_call | solution.py:235
  38.3 1.6 %collective-permute-start.13 = (bf16[64,1024]{1,0:T(8,128)(2,1)S(1)}, bf16[64,1024]{1,0:T(8,128)(2,1)S(1)}, u32[]{:S(2)}, u32[]{:S(2)}) collective-permute-start(bf16[64,1024]{1,0:T(8,128)(2,1)S(1)} %slice.133), channel_id=1, source_target_pairs={{0,2},{1,5},{2,0},{3,7},{4,6},{5,1},{6,4},{7,3},{8,10},{9,13},{10,... | collective-permute-start | bytes 393224 | tf_op jit(solution)/shard_map/ppermute | solution.py:27
  40.9 2.5 %collective-permute-done.13 = bf16[64,1024]{1,0:T(8,128)(2,1)S(1)} collective-permute-done((bf16[64,1024]{1,0:T(8,128)(2,1)S(1)}, bf16[64,1024]{1,0:T(8,128)(2,1)S(1)}, u32[]{:S(2)}, u32[]{:S(2)}) %collective-permute-start.13) | collective-permute-done | bytes 131104 | tf_op jit(solution)/shard_map/ppermute | solution.py:27
  43.4 1.5 %collective-permute-start.14 = (bf16[32,1024]{1,0:T(8,128)(2,1)S(1)}, bf16[32,1024]{1,0:T(8,128)(2,1)S(1)}, u32[]{:S(2)}, u32[]{:S(2)}) collective-permute-start(bf16[32,1024]{1,0:T(8,128)(2,1)S(1)} %slice.135), channel_id=1, source_target_pairs={{0,4},{1,3},{2,6},{3,1},{4,0},{5,7},{6,2},{7,5},{8,12},{9,11},{10,... | collective-permute-start | bytes 196616 | tf_op jit(solution)/shard_map/ppermute | solution.py:27
  45.0 1.4 %collective-permute-start.18 = (bf16[32,1024]{1,0:T(8,128)(2,1)S(1)}, bf16[32,1024]{1,0:T(8,128)(2,1)S(1)}, u32[]{:S(2)}, u32[]{:S(2)}) collective-permute-start(bf16[32,1024]{1,0:T(8,128)(2,1)S(1)} %slice.134), channel_id=1, source_target_pairs={{0,4},{1,3},{2,6},{3,1},{4,0},{5,7},{6,2},{7,5},{8,12},{9,11},{10,... | collective-permute-start | bytes 196616 | tf_op jit(solution)/shard_map/ppermute | solution.py:27
  46.4 1.3 %collective-permute-done.14 = bf16[32,1024]{1,0:T(8,128)(2,1)S(1)} collective-permute-done((bf16[32,1024]{1,0:T(8,128)(2,1)S(1)}, bf16[32,1024]{1,0:T(8,128)(2,1)S(1)}, u32[]{:S(2)}, u32[]{:S(2)}) %collective-permute-start.14) | collective-permute-done | bytes 65568 | tf_op jit(solution)/shard_map/ppermute | solution.py:27
  47.7 2.2 %collective-permute-start.15 = (bf16[16,1024]{1,0:T(8,128)(2,1)S(1)}, bf16[16,1024]{1,0:T(8,128)(2,1)S(1)}, u32[]{:S(2)}, u32[]{:S(2)}) collective-permute-start(bf16[16,1024]{1,0:T(8,128)(2,1)S(1)} %slice.139), channel_id=1, source_target_pairs={{0,8},{1,9},{2,10},{3,11},{4,12},{5,13},{6,14},{7,15},{8,0},{9,1},... | collective-permute-start | bytes 98312 | tf_op jit(solution)/shard_map/ppermute | solution.py:27
  50.0 2.0 %collective-permute-start.19 = (bf16[16,1024]{1,0:T(8,128)(2,1)S(1)}, bf16[16,1024]{1,0:T(8,128)(2,1)S(1)}, u32[]{:S(2)}, u32[]{:S(2)}) collective-permute-start(bf16[16,1024]{1,0:T(8,128)(2,1)S(1)} %slice.138), channel_id=1, source_target_pairs={{0,8},{1,9},{2,10},{3,11},{4,12},{5,13},{6,14},{7,15},{8,0},{9,1},... | collective-permute-start | bytes 98312 | tf_op jit(solution)/shard_map/ppermute | solution.py:27
  52.6 2.2 %collective-permute-done.19 = bf16[16,1024]{1,0:T(8,128)(2,1)S(1)} collective-permute-done((bf16[16,1024]{1,0:T(8,128)(2,1)S(1)}, bf16[16,1024]{1,0:T(8,128)(2,1)S(1)}, u32[]{:S(2)}, u32[]{:S(2)}) %collective-permute-start.19) | collective-permute-done | bytes 32800 | tf_op jit(solution)/shard_map/ppermute | solution.py:27
  (59 shorter events, 7.7 us)
Async XLA Ops:
  3.5 6.0 %collective-permute-start.6 = (bf16[64,1024]{1,0:T(8,128)(2,1)S(1)}, bf16[64,1024]{1,0:T(8,128)(2,1)S(1)}, u32[]{:S(2)}, u32[]{:S(2)}) collective-permute-start(bf16[64,1024]{1,0:T(8,128)(2,1)S(1)} %get-tuple-element.22), channel_id=1, source_target_pairs={{0,2},{1,5},{2,0},{3,7},{4,6},{5,1},{6,4},{7,3},{8,10},{9,13},{10,... | collective-permute-start | bytes 393224 | tf_op jit(solution)/shard_map/ppermute | solution.py:27
  6.5 5.1 %collective-permute-start = (bf16[64,1024]{1,0:T(8,128)(2,1)S(1)}, bf16[64,1024]{1,0:T(8,128)(2,1)S(1)}, u32[]{:S(2)}, u32[]{:S(2)}) collective-permute-start(bf16[64,1024]{1,0:T(8,128)(2,1)S(1)} %get-tuple-element.19), channel_id=1, source_target_pairs={{0,2},{1,5},{2,0},{3,7},{4,6},{5,1},{6,4},{7,3},{8,10},{9,13},{10,... | collective-permute-start | bytes 393224 | tf_op jit(solution)/shard_map/ppermute | solution.py:27
  9.5 23.7 %copy-start.2 = (bf16[1,2048,768]{2,1,0:T(8,128)(2,1)S(1)}, bf16[1,2048,768]{2,1,0:T(8,128)(2,1)}, u32[]{:S(2)}) copy-start(bf16[1,2048,768]{2,1,0:T(8,128)(2,1)} %w_up.1) | copy-start | bytes 9437188
  9.5 4.4 %collective-permute-start.7 = (bf16[32,1024]{1,0:T(8,128)(2,1)S(1)}, bf16[32,1024]{1,0:T(8,128)(2,1)S(1)}, u32[]{:S(2)}, u32[]{:S(2)}) collective-permute-start(bf16[32,1024]{1,0:T(8,128)(2,1)S(1)} %slice.136), channel_id=1, source_target_pairs={{0,4},{1,3},{2,6},{3,1},{4,0},{5,7},{6,2},{7,5},{8,12},{9,11},{10,... | collective-permute-start | bytes 196616 | tf_op jit(solution)/shard_map/ppermute | solution.py:27
  11.7 5.3 %collective-permute-start.1 = (bf16[32,1024]{1,0:T(8,128)(2,1)S(1)}, bf16[32,1024]{1,0:T(8,128)(2,1)S(1)}, u32[]{:S(2)}, u32[]{:S(2)}) collective-permute-start(bf16[32,1024]{1,0:T(8,128)(2,1)S(1)} %slice.137), channel_id=1, source_target_pairs={{0,4},{1,3},{2,6},{3,1},{4,0},{5,7},{6,2},{7,5},{8,12},{9,11},{10,... | collective-permute-start | bytes 196616 | tf_op jit(solution)/shard_map/ppermute | solution.py:27
  13.9 7.2 %collective-permute-start.8 = (bf16[32,1024]{1,0:T(8,128)(2,1)S(1)}, bf16[32,1024]{1,0:T(8,128)(2,1)S(1)}, u32[]{:S(2)}, u32[]{:S(2)}) collective-permute-start(bf16[32,1024]{1,0:T(8,128)(2,1)S(1)} %fusion.3), channel_id=1, source_target_pairs={{0,8},{1,9},{2,10},{3,11},{4,12},{5,13},{6,14},{7,15},{8,0},{9,1},... | collective-permute-start | bytes 196616 | tf_op jit(solution)/shard_map/ppermute | solution.py:27
  17.1 5.3 %collective-permute-start.2 = (bf16[32,1152]{1,0:T(8,128)(2,1)S(1)}, bf16[32,1152]{1,0:T(8,128)(2,1)S(1)}, u32[]{:S(2)}, u32[]{:S(2)}) collective-permute-start(bf16[32,1152]{1,0:T(8,128)(2,1)S(1)} %fusion.2), channel_id=1, source_target_pairs={{0,8},{1,9},{2,10},{3,11},{4,12},{5,13},{6,14},{7,15},{8,0},{9,1},... | collective-permute-start | bytes 221192 | tf_op jit(solution)/shard_map/ppermute | solution.py:27
  21.2 4.8 %collective-permute-start.9 = (bf16[32,1024]{1,0:T(8,128)(2,1)S(1)}, bf16[32,1024]{1,0:T(8,128)(2,1)S(1)}, u32[]{:S(2)}, u32[]{:S(2)}) collective-permute-start(bf16[32,1024]{1,0:T(8,128)(2,1)S(1)} %fusion.1), channel_id=1, source_target_pairs={{0,4},{1,3},{2,6},{3,1},{4,0},{5,7},{6,2},{7,5},{8,12},{9,11},{10,... | collective-permute-start | bytes 196616 | tf_op jit(solution)/shard_map/ppermute | solution.py:27
  22.4 10.8 %copy-start.1 = (bf16[1,2048,768]{2,1,0:T(8,128)(2,1)S(1)}, bf16[1,2048,768]{2,1,0:T(8,128)(2,1)}, u32[]{:S(2)}) copy-start(bf16[1,2048,768]{2,1,0:T(8,128)(2,1)} %w_gate.1) | copy-start | bytes 9437188
  22.4 5.4 %collective-permute-start.3 = (bf16[32,1152]{1,0:T(8,128)(2,1)S(1)}, bf16[32,1152]{1,0:T(8,128)(2,1)S(1)}, u32[]{:S(2)}, u32[]{:S(2)}) collective-permute-start(bf16[32,1152]{1,0:T(8,128)(2,1)S(1)} %fusion), channel_id=1, source_target_pairs={{0,4},{1,3},{2,6},{3,1},{4,0},{5,7},{6,2},{7,5},{8,12},{9,11},{10,... | collective-permute-start | bytes 221192 | tf_op jit(solution)/shard_map/ppermute | solution.py:27
  26.0 5.0 %collective-permute-start.10 = (bf16[64,1024]{1,0:T(8,128)(2,1)S(1)}, bf16[64,1024]{1,0:T(8,128)(2,1)S(1)}, u32[]{:S(2)}, u32[]{:S(2)}) collective-permute-start(bf16[64,1024]{1,0:T(8,128)(2,1)S(1)} %pad_maximum_fusion.6), channel_id=1, source_target_pairs={{0,2},{1,5},{2,0},{3,7},{4,6},{5,1},{6,4},{7,3},{8,10},{9,13},{10,... | collective-permute-start | bytes 393224 | tf_op jit(solution)/shard_map/ppermute | solution.py:27
  27.8 5.2 %collective-permute-start.4 = (bf16[64,1152]{1,0:T(8,128)(2,1)S(1)}, bf16[64,1152]{1,0:T(8,128)(2,1)S(1)}, u32[]{:S(2)}, u32[]{:S(2)}) collective-permute-start(bf16[64,1152]{1,0:T(8,128)(2,1)S(1)} %pad_maximum_fusion.5), channel_id=1, source_target_pairs={{0,2},{1,5},{2,0},{3,7},{4,6},{5,1},{6,4},{7,3},{8,10},{9,13},{10,... | collective-permute-start | bytes 442376 | tf_op jit(solution)/shard_map/ppermute | solution.py:27
  31.0 2.1 %collective-permute-start.11 = (bf16[128,1024]{1,0:T(8,128)(2,1)S(1)}, bf16[128,1024]{1,0:T(8,128)(2,1)S(1)}, u32[]{:S(2)}, u32[]{:S(2)}) collective-permute-start(bf16[128,1024]{1,0:T(8,128)(2,1)S(1)} %pad_maximum_fusion.3), channel_id=1, source_target_pairs={{0,1},{1,0},{2,3},{3,2},{4,5},{5,4},{6,7},{7,6},{8,9},{9,8},{10,11... | collective-permute-start | bytes 786440 | tf_op jit(solution)/shard_map/ppermute | solution.py:27
  33.1 1.6 %collective-permute-start.5 = (bf16[128,1152]{1,0:T(8,128)(2,1)S(1)}, bf16[128,1152]{1,0:T(8,128)(2,1)S(1)}, u32[]{:S(2)}, u32[]{:S(2)}) collective-permute-start(bf16[128,1152]{1,0:T(8,128)(2,1)S(1)} %pad_maximum_fusion.2), channel_id=1, source_target_pairs={{0,1},{1,0},{2,3},{3,2},{4,5},{5,4},{6,7},{7,6},{8,9},{9,8},{10,11... | collective-permute-start | bytes 884744 | tf_op jit(solution)/shard_map/ppermute | solution.py:27
  33.2 1.9 %copy-start = (bf16[1,768,2048]{2,1,0:T(8,128)(2,1)S(1)}, bf16[1,768,2048]{2,1,0:T(8,128)(2,1)}, u32[]{:S(2)}) copy-start(bf16[1,768,2048]{2,1,0:T(8,128)(2,1)} %w_down.3) | copy-start | bytes 9437188
  36.5 1.7 %collective-permute-start.12 = (bf16[128,1024]{1,0:T(8,128)(2,1)S(1)}, bf16[128,1024]{1,0:T(8,128)(2,1)S(1)}, u32[]{:S(2)}, u32[]{:S(2)}) collective-permute-start(bf16[128,1024]{1,0:T(8,128)(2,1)S(1)} %get-tuple-element.26), channel_id=1, source_target_pairs={{0,1},{1,0},{2,3},{3,2},{4,5},{5,4},{6,7},{7,6},{8,9},{9,8},{10,11... | collective-permute-start | bytes 786440 | tf_op jit(solution)/shard_map/ppermute | solution.py:27
  37.6 2.2 %collective-permute-start.16 = (bf16[128,1024]{1,0:T(8,128)(2,1)S(1)}, bf16[128,1024]{1,0:T(8,128)(2,1)S(1)}, u32[]{:S(2)}, u32[]{:S(2)}) collective-permute-start(bf16[128,1024]{1,0:T(8,128)(2,1)S(1)} %get-tuple-element.30), channel_id=1, source_target_pairs={{0,1},{1,0},{2,3},{3,2},{4,5},{5,4},{6,7},{7,6},{8,9},{9,8},{10,11... | collective-permute-start | bytes 786440 | tf_op jit(solution)/shard_map/ppermute | solution.py:27
  38.3 5.0 %collective-permute-start.13 = (bf16[64,1024]{1,0:T(8,128)(2,1)S(1)}, bf16[64,1024]{1,0:T(8,128)(2,1)S(1)}, u32[]{:S(2)}, u32[]{:S(2)}) collective-permute-start(bf16[64,1024]{1,0:T(8,128)(2,1)S(1)} %slice.133), channel_id=1, source_target_pairs={{0,2},{1,5},{2,0},{3,7},{4,6},{5,1},{6,4},{7,3},{8,10},{9,13},{10,... | collective-permute-start | bytes 393224 | tf_op jit(solution)/shard_map/ppermute | solution.py:27
  40.0 5.0 %collective-permute-start.17 = (bf16[64,1024]{1,0:T(8,128)(2,1)S(1)}, bf16[64,1024]{1,0:T(8,128)(2,1)S(1)}, u32[]{:S(2)}, u32[]{:S(2)}) collective-permute-start(bf16[64,1024]{1,0:T(8,128)(2,1)S(1)} %slice.132), channel_id=1, source_target_pairs={{0,2},{1,5},{2,0},{3,7},{4,6},{5,1},{6,4},{7,3},{8,10},{9,13},{10,... | collective-permute-start | bytes 393224 | tf_op jit(solution)/shard_map/ppermute | solution.py:27
  43.4 4.3 %collective-permute-start.14 = (bf16[32,1024]{1,0:T(8,128)(2,1)S(1)}, bf16[32,1024]{1,0:T(8,128)(2,1)S(1)}, u32[]{:S(2)}, u32[]{:S(2)}) collective-permute-start(bf16[32,1024]{1,0:T(8,128)(2,1)S(1)} %slice.135), channel_id=1, source_target_pairs={{0,4},{1,3},{2,6},{3,1},{4,0},{5,7},{6,2},{7,5},{8,12},{9,11},{10,... | collective-permute-start | bytes 196616 | tf_op jit(solution)/shard_map/ppermute | solution.py:27
  45.0 4.9 %collective-permute-start.18 = (bf16[32,1024]{1,0:T(8,128)(2,1)S(1)}, bf16[32,1024]{1,0:T(8,128)(2,1)S(1)}, u32[]{:S(2)}, u32[]{:S(2)}) collective-permute-start(bf16[32,1024]{1,0:T(8,128)(2,1)S(1)} %slice.134), channel_id=1, source_target_pairs={{0,4},{1,3},{2,6},{3,1},{4,0},{5,7},{6,2},{7,5},{8,12},{9,11},{10,... | collective-permute-start | bytes 196616 | tf_op jit(solution)/shard_map/ppermute | solution.py:27
  47.7 4.9 %collective-permute-start.15 = (bf16[16,1024]{1,0:T(8,128)(2,1)S(1)}, bf16[16,1024]{1,0:T(8,128)(2,1)S(1)}, u32[]{:S(2)}, u32[]{:S(2)}) collective-permute-start(bf16[16,1024]{1,0:T(8,128)(2,1)S(1)} %slice.139), channel_id=1, source_target_pairs={{0,8},{1,9},{2,10},{3,11},{4,12},{5,13},{6,14},{7,15},{8,0},{9,1},... | collective-permute-start | bytes 98312 | tf_op jit(solution)/shard_map/ppermute | solution.py:27
  50.0 4.9 %collective-permute-start.19 = (bf16[16,1024]{1,0:T(8,128)(2,1)S(1)}, bf16[16,1024]{1,0:T(8,128)(2,1)S(1)}, u32[]{:S(2)}, u32[]{:S(2)}) collective-permute-start(bf16[16,1024]{1,0:T(8,128)(2,1)S(1)} %slice.138), channel_id=1, source_target_pairs={{0,8},{1,9},{2,10},{3,11},{4,12},{5,13},{6,14},{7,15},{8,0},{9,1},... | collective-permute-start | bytes 98312 | tf_op jit(solution)/shard_map/ppermute | solution.py:27

commit v3 on v2

--- a/solution.py
+++ b/solution.py
@@ -10,6 +10,7 @@
 ATT_TP = 8
 PIECES = (8, 8)
 CHUNKS = len(PIECES)
+CARRIER = 0
 LANES = 128
 
 
@@ -20,6 +21,10 @@
 def column_cuts(features):
     ends = [features * sum(PIECES[: c + 1]) // sum(PIECES) for c in range(CHUNKS)]
     return list(zip([0] + ends[:-1], ends))
+
+
+def spare_width(axis_width):
+    return -(-2 * axis_width // LANES) * LANES
 
 
 def exchange(block, masks):
@@ -47,19 +52,19 @@
 
 
 def attend_kernel(axis_width, *refs):
-    sources, outs, scratch = refs[:9], refs[9 : 10 + 2 * CHUNKS], refs[10 + 2 * CHUNKS :]
+    sources, outs, scratch = refs[:10], refs[10 : 12 + 2 * CHUNKS], refs[12 + 2 * CHUNKS :]
     *inputs, attended, sems = scratch
     copies = [
         pltpu.make_async_copy(source, target, sems.at[n])
-        for n, (source, target) in enumerate(zip(sources, inputs))
+        for n, (source, target) in enumerate(zip(sources, [*inputs, outs[-1]]))
     ]
     for copy in copies:
         copy.start()
-    for copy in copies[:-1]:
+    for copy in copies[:-2]:
         copy.wait()
     table, lengths, parents, expert_ids, gate_weights = inputs[:5]
     queries, tree_kv, kv_cache, weights_in = inputs[5:]
-    *outs, extra = outs
+    *outs, extra, w_down = outs
     seq_count, node_count = parents.shape
     head_dim = tree_kv.shape[-1]
     head_count = queries.shape[1] // head_dim
@@ -137,12 +142,13 @@
         target = (device ^ jnp.where(device & 1 == 0, one, other)) // groups
         picked.append(attended[pl.ds(pl.multiple_of(target * block, block), block), :])
     ordered = jnp.concatenate(picked, axis=0)
-    copies[-1].wait()
+    copies[-2].wait()
     half = all_nodes // 2
     for c, (low, high) in enumerate(column_cuts(weights_in.shape[1])):
         projected = jnp.dot(ordered, weights_in[:, low:high], preferred_element_type=f32)
         outs[2 * c][...] = projected[:half]
         outs[2 * c + 1][...] = projected[half:].astype(bf16)
+    copies[-1].wait()
 
 
 def kept_and_sent(rows, cuts):
@@ -153,82 +159,92 @@
     return shapes
 
 
-def attend(queries, tree_kv, kv_cache, table, lengths, parents, w_out, expert_ids, gate_weights):
+def attend(
+    queries, tree_kv, kv_cache, table, lengths, parents, w_out, w_down, expert_ids, gate_weights
+):
     axis_width = lax.axis_size("wide")
     features = w_out.shape[1]
     rows = queries.shape[0]
     own_rows = expert_ids.shape[0]
-    extra_width = -(-2 * axis_width // LANES) * LANES
+    extra_width = spare_width(axis_width)
     halves = kept_and_sent(rows, column_cuts(features))
-    given = [table, lengths, parents, expert_ids.T, gate_weights.T, queries, tree_kv, kv_cache, w_out]
+    given = [table, lengths, parents, expert_ids.T, gate_weights.T, queries, tree_kv, kv_cache, w_out, w_down]
     spaces = [pltpu.SMEM] * 2 + [pltpu.VMEM] * (len(given) - 2)
     given = [pltpu.with_memory_space_constraint(x, pltpu.HBM) for x in given]
     return pl.pallas_call(
         functools.partial(attend_kernel, axis_width),
         out_shape=halves
-        + [pltpu.VMEM((2 * own_rows, extra_width), jnp.bfloat16)],
+        + [pltpu.VMEM((2 * own_rows, extra_width), jnp.bfloat16), pltpu.VMEM(w_down.shape, w_down.dtype)],
         in_specs=[pl.BlockSpec(memory_space=pltpu.HBM)] * len(given),
-        out_specs=[pl.BlockSpec(memory_space=pltpu.VMEM)] * (2 * CHUNKS + 1),
-        scratch_shapes=[space(x.shape, x.dtype) for space, x in zip(spaces, given)]
+        out_specs=[pl.BlockSpec(memory_space=pltpu.VMEM)] * (2 * CHUNKS + 2),
+        scratch_shapes=[space(x.shape, x.dtype) for space, x in zip(spaces, given[:-1])]
         + [pltpu.VMEM(queries.shape, jnp.bfloat16), pltpu.SemaphoreType.DMA((len(given),))],
         compiler_params=pltpu.CompilerParams(vmem_limit_bytes=16 * 1024 * 1024),
         name="attend",
     )(*given)
 
 
-def feed_kernel(cut, tile, first, *refs):
-    hidden, w_gate, w_up = refs[:3]
-    before, after = ((), refs[3:]) if first else (refs[3:5], refs[5:])
-    width = cut[1] - cut[0]
-    for n in range(w_gate.shape[2] // tile):
-        columns = slice(n * tile, (n + 1) * tile)
-        for m, weights in enumerate((w_gate, w_up)):
+def feed_kernel(cut, tile, pairs, first, *refs):
+    hidden, weights, refs = refs[:2], refs[2 : 2 + pairs], refs[2 + pairs :]
+    before, after = (None, refs) if first else (refs[:pairs], refs[pairs:])
+    rows = jnp.concatenate([half[:, : cut[1] - cut[0]] for half in hidden], axis=0)
+    for m in range(pairs):
+        for n in range(weights[m].shape[2] // tile):
+            columns = slice(n * tile, (n + 1) * tile)
             share = jnp.dot(
-                hidden[:, :width],
-                weights[0, cut[0] : cut[1], columns],
-                preferred_element_type=jnp.float32,
+                rows, weights[m][0, cut[0] : cut[1], columns], preferred_element_type=jnp.float32
             )
             after[m][:, columns] = share if first else before[m][:, columns] + share
 
 
-def finish_kernel(axis_width, cut, out_cut, tile, hidden, w_gate, w_up, w_down, gate, up, *outs):
-    kept, sent, activated, row_weight = outs
+def finish_kernel(axis_width, spare, cut, out_cut, tile, owners, *refs):
+    count = len(owners)
+    hidden, carrier, refs = refs[:2], refs[2:4], refs[4:]
+    feeds, downs, sums = refs[: 2 * count], refs[2 * count : 3 * count], refs[3 * count : 5 * count]
+    kept, sent = refs[5 * count : 5 * count + 2]
+    activated, row_weight = refs[5 * count + 2 : 6 * count + 2], refs[6 * count + 2 :]
     f32, bf16 = jnp.float32, jnp.bfloat16
     width = cut[1] - cut[0]
     device = lax.axis_index("wide")
-    parts = hidden[:, width:]
+    rows = jnp.concatenate([half[:, :width] for half in hidden], axis=0)
+    parts = jnp.concatenate([half[:, -spare:] for half in carrier], axis=0)
     lane = lax.broadcasted_iota(jnp.int32, parts.shape, 1)
-    mine = (lane == device) | (lane == device + axis_width)
-    weight = jnp.sum(jnp.where(mine, parts.astype(f32), 0.0), axis=1, keepdims=True)
-    row_weight[...] = weight
-    for n in range(w_gate.shape[2] // tile):
-        columns = slice(n * tile, (n + 1) * tile)
-        rows = hidden[:, :width]
-        piece = slice(*cut)
-        gate_part = gate[:, columns] + jnp.dot(
-            rows, w_gate[0, piece, columns], preferred_element_type=f32
-        )
-        up_part = up[:, columns] + jnp.dot(
-            rows, w_up[0, piece, columns], preferred_element_type=f32
-        )
-        activated[:, columns] = (gate_part / (1.0 + jnp.exp(-gate_part)) * up_part).astype(bf16)
-    produce(activated, w_down.at[0, :, slice(*out_cut)], weight, kept, sent, tile)
-
-
-def down_kernel(cut, tile, activated, row_weight, w_down, kept, sent):
-    produce(activated, w_down.at[0, :, slice(*cut)], row_weight[...], kept, sent, tile)
-
-
-def produce(activated, w_down, weight, kept, sent, tile):
+    piece = slice(*cut)
+    for m, owner in enumerate(owners):
+        expert = device ^ owner
+        mine = (lane == expert) | (lane == expert + axis_width)
+        row_weight[m][...] = jnp.sum(jnp.where(mine, parts.astype(f32), 0.0), axis=1, keepdims=True)
+        for n in range(feeds[2 * m].shape[2] // tile):
+            columns = slice(n * tile, (n + 1) * tile)
+            gate_part, up_part = [
+                sums[2 * m + k][:, columns]
+                + jnp.dot(rows, feeds[2 * m + k][0, piece, columns], preferred_element_type=f32)
+                for k in range(2)
+            ]
+            activated[m][:, columns] = (
+                gate_part / (1.0 + jnp.exp(-gate_part)) * up_part
+            ).astype(bf16)
+    produce(activated, downs, row_weight, out_cut, kept, sent, tile)
+
+
+def down_kernel(cut, tile, count, *refs):
+    activated, row_weight, downs = [refs[k * count : (k + 1) * count] for k in range(3)]
+    produce(activated, downs, row_weight, cut, *refs[3 * count :], tile)
+
+
+def produce(activated, downs, row_weight, cut, kept, sent, tile):
     half, width = kept.shape
     for start in range(0, width, tile):
-        columns = slice(start, min(start + tile, width))
-        produced = jnp.dot(
-            activated[...], w_down[:, columns], preferred_element_type=jnp.float32
-        )
-        weighted = produced * weight
-        kept[:, columns] = weighted[:half]
-        sent[:, columns] = weighted[half:].astype(jnp.bfloat16)
+        size = min(tile, width - start)
+        columns = slice(cut[0] + start, cut[0] + start + size)
+        weighted = 0.0
+        for rows, w_down, weight in zip(activated, downs, row_weight):
+            weighted += (
+                jnp.dot(rows[...], w_down[0, :, columns], preferred_element_type=jnp.float32)
+                * weight[...]
+            )
+        kept[:, start : start + size] = weighted[:half]
+        sent[:, start : start + size] = weighted[half:].astype(jnp.bfloat16)
 
 
 def local_call(kernel, name, out_shape, given):
@@ -242,44 +258,71 @@
     )(*given)
 
 
-def experts(hidden, w_gate, w_up, w_down):
+def experts(hidden, owners, feeds, downs):
     axis_width = lax.axis_size("wide")
-    rows = hidden[0].shape[0]
-    hidden_width, features = w_down.shape[1:]
+    rows = 2 * hidden[0][0].shape[0]
+    hidden_width, features = downs[0].shape[1:]
     cuts = column_cuts(features)
+    spare = spare_width(axis_width)
+    count = len(owners)
     tile = 256 if hidden_width % 256 == 0 else LANES
     wide = pltpu.VMEM((rows, hidden_width), jnp.float32)
     sums = []
     for c in range(CHUNKS - 1):
-        given = [hidden[c], w_gate, w_up, *sums]
-        kernel = functools.partial(feed_kernel, cuts[c], tile, c == 0)
-        sums = local_call(kernel, "feed", [wide, wide], given)
-    kept, sent, activated, row_weight = local_call(
-        functools.partial(finish_kernel, axis_width, cuts[-1], cuts[0], tile),
+        kernel = functools.partial(feed_kernel, cuts[c], tile, 2 * count, c == 0)
+        sums = local_call(kernel, "feed", [wide] * (2 * count), [*hidden[c], *feeds, *sums])
+    kept, sent, *rest = local_call(
+        functools.partial(finish_kernel, axis_width, spare, cuts[-1], cuts[0], tile, owners),
         "finish",
         kept_and_sent(rows, cuts[:1])
-        + [
-            pltpu.VMEM((rows, hidden_width), jnp.bfloat16),
-            pltpu.VMEM((rows, 1), jnp.float32),
-        ],
-        [hidden[-1], w_gate, w_up, w_down, *sums],
+        + [pltpu.VMEM((rows, hidden_width), jnp.bfloat16)] * count
+        + [pltpu.VMEM((rows, 1), jnp.float32)] * count,
+        [*hidden[-1], *hidden[CARRIER], *feeds, *downs, *sums],
     )
     produced = [(kept, sent)]
     for c in range(1, CHUNKS):
-        produced.append(
-            local_call(
-                functools.partial(down_kernel, cuts[c], tile),
-                "down",
-                kept_and_sent(rows, cuts[c : c + 1]),
-                [activated, row_weight, w_down],
-            )
-        )
+        kernel = functools.partial(down_kernel, cuts[c], tile, count)
+        shapes = kept_and_sent(rows, cuts[c : c + 1])
+        produced.append(local_call(kernel, "down", shapes, [*rest, *downs]))
     return produced
 
 
 def halved(block):
     half = block.shape[0] // 2
     return block[:half], block[half:].astype(jnp.bfloat16)
+
+
+def ordered_after(value, earlier):
+    return value if earlier is None else lax.optimization_barrier((value, earlier))[0]
+
+
+def reduce_and_gather(halves, extra, steps, gathers):
+    f32, bf16 = jnp.float32, jnp.bfloat16
+    parts = [list(halves[2 * c : 2 * c + 2]) for c in range(CHUNKS)]
+    for number, masks in enumerate(steps[:-1]):
+        earlier = None
+        for c, part in enumerate(parts):
+            kept, sent = part
+            kept = kept + ordered_after(exchange(sent, masks), earlier).astype(f32)
+            if number < len(steps) - 2:
+                part[:] = halved(kept)
+            else:
+                if c == CARRIER:
+                    kept = jnp.concatenate([kept, extra.astype(f32)], axis=1)
+                part[:] = kept, kept.astype(bf16)
+            earlier = part[1]
+    blocks, earlier = [], None
+    for kept, sent in parts:
+        half = kept.shape[0] // 2
+        other = ordered_after(exchange(sent, steps[-1]), earlier).astype(f32)
+        blocks.append((kept + jnp.concatenate([other[half:], other[:half]], axis=0)).astype(bf16))
+        earlier = blocks[-1]
+    for masks in gathers[:-1]:
+        earlier = None
+        for c, block in enumerate(blocks):
+            other = ordered_after(exchange(block, masks), earlier)
+            blocks[c] = earlier = jnp.concatenate([block, other], axis=0)
+    return [(block, exchange(block, gathers[-1])) for block in blocks]
 
 
 def body(
@@ -298,37 +341,33 @@
 ):
     axis_width = lax.axis_size("wide")
     steps = list(zip(*slice_orders(axis_width)))
-    group_steps = [(1 << k, 1 << k) for k in range(bits_of(axis_width // ATT_TP))]
-    *halves, extra = attend(
-        queries, tree_kv, kv_cache, block_table, cache_lengths, parents, w_out,
+    group_steps = [(1 << k, 1 << k) for k in range(1, bits_of(axis_width // ATT_TP))]
+    pair = (1, 1)
+    owners = (0, 1)
+    feeds = [w_gate, w_up, exchange(w_gate, pair), exchange(w_up, pair)]
+    *halves, extra, fetched = attend(
+        queries, tree_kv, kv_cache, block_table, cache_lengths, parents, w_out, w_down,
         expert_ids, gate_weights,
     )
-    hidden = []
-    for c in range(CHUNKS):
-        kept, sent = halves[2 * c], halves[2 * c + 1]
-        for number, masks in enumerate(steps[:-1]):
-            kept = kept + exchange(sent, masks).astype(jnp.float32)
-            if number < len(steps) - 2:
-                kept, sent = halved(kept)
-        if c == CHUNKS - 1:
-            kept = jnp.concatenate([kept, extra.astype(jnp.float32)], axis=1)
-        half = kept.shape[0] // 2
-        other = exchange(kept.astype(jnp.bfloat16), steps[-1]).astype(jnp.float32)
-        block = kept + jnp.concatenate([other[half:], other[:half]], axis=0)
-        block = block.astype(jnp.bfloat16)
-        for masks in steps[-2::-1] + group_steps:
-            block = jnp.concatenate([block, exchange(block, masks)], axis=0)
-        hidden.append(block)
-    produced = experts(hidden, w_gate, w_up, w_down)
+    downs = [fetched, exchange(w_down, pair)]
+    gathers = steps[-2::-1] + group_steps
+    hidden = reduce_and_gather(halves, extra, steps, gathers)
+    produced = experts(hidden, owners, feeds, downs)
     results = []
-    for c in range(CHUNKS):
-        kept, sent = produced[c]
-        last = len(group_steps) + len(steps) - 1
-        for number, masks in enumerate(group_steps[::-1] + steps):
-            kept = kept + exchange(sent, masks).astype(jnp.float32)
-            if number < last:
-                kept, sent = halved(kept)
-        results.append(kept.astype(jnp.bfloat16))
+    parts = [list(pair) for pair in produced]
+    hops = group_steps[::-1] + steps
+    for number, masks in enumerate(hops):
+        earlier = None
+        for part in parts:
+            kept, sent = part
+            other = ordered_after(exchange(sent, masks), earlier)
+            kept = kept + other.astype(jnp.float32)
+            if number < len(hops) - 1:
+                part[:] = halved(kept)
+                earlier = part[1]
+            else:
+                results.append(kept.astype(jnp.bfloat16))
+                earlier = results[-1]
     return jnp.concatenate(results, axis=1)
 
 

time: 55.7 us -> 53.2 us (0.955)
  starting transfers between devices: 27.2 us -> 24.1 us
  waiting for transfers between devices: 20 us -> 21.1 us
    ppermute x20 -> x19, starting transfers between devices: 27.2 us -> 24.1 us  [exchange(): lax.ppermute(block, 'wide', [(i, i ^ masks[i & 1]) for i in range(count)])]
    ppermute x20 -> x19, waiting for transfers between devices: 20 us -> 21.1 us  [exchange(): lax.ppermute(block, 'wide', [(i, i ^ masks[i & 1]) for i in range(count)])]
  transfers between devices with their start and end apart: 20 -> 19, of which waited for: 14 -> 12; matrix products, arithmetic and copies ran while one was open for 1% -> 1% of each run, Pallas kernels for 3% -> 10%
where the time goes in v3:
time: 53.2 us; the launch traced here: 53 us
  starting transfers between devices  24.1 us (45%)
  waiting for transfers between devices  21.1 us (40%)
  Pallas kernels  6.71 us (13%)
  other arithmetic  0.93 us (2%)
    ppermute x19, starting transfers between devices, exchange(): lax.ppermute(block, 'wide', [(i, i ^ masks[i & 1]) for i in range(count)])  24.1 us
    ppermute x19, waiting for transfers between devices, exchange(): lax.ppermute(block, 'wide', [(i, i ^ masks[i & 1]) for i in range(count)])  21.1 us
    pallas_call x1, Pallas kernels, attend(): pl.pallas_call(functools.partial(attend_kernel, axis_width), out_shape=ha...  3.63 us
    pallas_call x3, Pallas kernels, local_call(): pl.pallas_call(kernel, out_shape=out_shape, in_specs=[pl.BlockSpec(memory...  3.09 us
  transfers between devices with their start and end apart: 19, of which 12 were waited for; matrix products, arithmetic and copies ran while one was open for 1% of the time, Pallas kernels for 10%

profile of v3, /device:TPU:0, one launch (start us, length us, event | category | flops | bytes accessed | tf_op | source)
XLA Modules:
  0.0 53.0 jit_solution(793087477283801026)
XLA Ops:
  1.0 3.6 %attend.1 = (f32[64,1024]{1,0:T(8,128)S(1)}, bf16[64,1024]{1,0:T(8,128)(2,1)S(1)}, f32[64,1024]{1,0:T(8,128)S(1)}, bf16[64,1024]{1,0:T(8,128)(2,1)S(1)}, bf16[32...) custom-call(s32[4,4]{1,0:T(4,128)} %refs_0_.1, s32[1,4]{1,0:T(1,128)} %refs_1_.1, s32[4,32]{1,0:T(4,128)} %refs_2_.2, ...), custom_call_target="tpu_custom_call" | custom-call | tf_op jit(solution)/shard_map/attend/pallas_call | solution.py:174
  4.6 2.6 %collective-permute-start.1 = (bf16[64,1024]{1,0:T(8,128)(2,1)S(1)}, bf16[64,1024]{1,0:T(8,128)(2,1)S(1)}, u32[]{:S(2)}, u32[]{:S(2)}) collective-permute-start(bf16[64,1024]{1,0:T(8,128)(2,1)S(1)} %get-tuple-element.33), channel_id=1, source_target_pairs={{0,2},{1,5},{2,0},{3,7},{4,6},{5,1},{6,4},{7,3},{8,10},{9,13},{10,... | collective-permute-start | bytes 393224 | tf_op jit(solution)/shard_map/ppermute | solution.py:32
  7.3 2.9 %collective-permute-done.1 = bf16[64,1024]{1,0:T(8,128)(2,1)S(1)} collective-permute-done((bf16[64,1024]{1,0:T(8,128)(2,1)S(1)}, bf16[64,1024]{1,0:T(8,128)(2,1)S(1)}, u32[]{:S(2)}, u32[]{:S(2)}) %collective-permute-start.1) | collective-permute-done | bytes 131104 | tf_op jit(solution)/shard_map/ppermute | solution.py:32
  10.2 2.1 %collective-permute-start.3 = (bf16[32,1024]{1,0:T(8,128)(2,1)S(1)}, bf16[32,1024]{1,0:T(8,128)(2,1)S(1)}, u32[]{:S(2)}, u32[]{:S(2)}) collective-permute-start(bf16[32,1024]{1,0:T(8,128)(2,1)S(1)} %slice.109), channel_id=1, source_target_pairs={{0,4},{1,3},{2,6},{3,1},{4,0},{5,7},{6,2},{7,5},{8,12},{9,11},{10,... | collective-permute-start | bytes 196616 | tf_op jit(solution)/shard_map/ppermute | solution.py:32
  12.4 1.5 %collective-permute-start.2 = (bf16[32,1024]{1,0:T(8,128)(2,1)S(1)}, bf16[32,1024]{1,0:T(8,128)(2,1)S(1)}, u32[]{:S(2)}, u32[]{:S(2)}) collective-permute-start(bf16[32,1024]{1,0:T(8,128)(2,1)S(1)} %slice.108), channel_id=1, source_target_pairs={{0,4},{1,3},{2,6},{3,1},{4,0},{5,7},{6,2},{7,5},{8,12},{9,11},{10,... | collective-permute-start | bytes 196616 | tf_op jit(solution)/shard_map/ppermute | solution.py:32
  14.6 3.1 %collective-permute-start.5 = (bf16[32,1152]{1,0:T(8,128)(2,1)S(1)}, bf16[32,1152]{1,0:T(8,128)(2,1)S(1)}, u32[]{:S(2)}, u32[]{:S(2)}) collective-permute-start(bf16[32,1152]{1,0:T(8,128)(2,1)S(1)} %fusion.2), channel_id=1, source_target_pairs={{0,8},{1,9},{2,10},{3,11},{4,12},{5,13},{6,14},{7,15},{8,0},{9,1},... | collective-permute-start | bytes 221192 | tf_op jit(solution)/shard_map/ppermute | solution.py:32
  17.8 2.3 %collective-permute-start.4 = (bf16[32,1024]{1,0:T(8,128)(2,1)S(1)}, bf16[32,1024]{1,0:T(8,128)(2,1)S(1)}, u32[]{:S(2)}, u32[]{:S(2)}) collective-permute-start(bf16[32,1024]{1,0:T(8,128)(2,1)S(1)} %fusion.3), channel_id=1, source_target_pairs={{0,8},{1,9},{2,10},{3,11},{4,12},{5,13},{6,14},{7,15},{8,0},{9,1},... | collective-permute-start | bytes 196616 | tf_op jit(solution)/shard_map/ppermute | solution.py:32
  20.0 2.4 %collective-permute-done.5 = bf16[32,1152]{1,0:T(8,128)(2,1)S(1)} collective-permute-done((bf16[32,1152]{1,0:T(8,128)(2,1)S(1)}, bf16[32,1152]{1,0:T(8,128)(2,1)S(1)}, u32[]{:S(2)}, u32[]{:S(2)}) %collective-permute-start.5) | collective-permute-done | bytes 73760 | tf_op jit(solution)/shard_map/ppermute | solution.py:32
  23.2 1.4 %collective-permute-start.6 = (bf16[32,1024]{1,0:T(8,128)(2,1)S(1)}, bf16[32,1024]{1,0:T(8,128)(2,1)S(1)}, u32[]{:S(2)}, u32[]{:S(2)}) collective-permute-start(bf16[32,1024]{1,0:T(8,128)(2,1)S(1)} %fusion.1), channel_id=1, source_target_pairs={{0,4},{1,3},{2,6},{3,1},{4,0},{5,7},{6,2},{7,5},{8,12},{9,11},{10,... | collective-permute-start | bytes 196616 | tf_op jit(solution)/shard_map/ppermute | solution.py:32
  24.7 2.6 %collective-permute-done.7 = bf16[32,1152]{1,0:T(8,128)(2,1)S(1)} collective-permute-done((bf16[32,1152]{1,0:T(8,128)(2,1)S(1)}, bf16[32,1152]{1,0:T(8,128)(2,1)S(1)}, u32[]{:S(2)}, u32[]{:S(2)}) %collective-permute-start.7) | collective-permute-done | bytes 73760 | tf_op jit(solution)/shard_map/ppermute | solution.py:32
  27.3 2.0 %collective-permute-start.9 = (bf16[64,1152]{1,0:T(8,128)(2,1)S(1)}, bf16[64,1152]{1,0:T(8,128)(2,1)S(1)}, u32[]{:S(2)}, u32[]{:S(2)}) collective-permute-start(bf16[64,1152]{1,0:T(8,128)(2,1)S(1)} %pad_maximum_fusion.1.refs_0_.refs_2_), channel_id=1, source_target_pairs={{0,2},{1,5},{2,0},{3,7},{4,6},{5,1},{6,4},{7,3},{8,10},{9,13},{10,... | collective-permute-start | bytes 442376 | tf_op jit(solution)/shard_map/ppermute | solution.py:32
  29.3 1.3 %collective-permute-start.8 = (bf16[64,1024]{1,0:T(8,128)(2,1)S(1)}, bf16[64,1024]{1,0:T(8,128)(2,1)S(1)}, u32[]{:S(2)}, u32[]{:S(2)}) collective-permute-start(bf16[64,1024]{1,0:T(8,128)(2,1)S(1)} %pad_maximum_fusion.2.refs_0_), channel_id=1, source_target_pairs={{0,2},{1,5},{2,0},{3,7},{4,6},{5,1},{6,4},{7,3},{8,10},{9,13},{10,... | collective-permute-start | bytes 393224 | tf_op jit(solution)/shard_map/ppermute | solution.py:32
  30.6 1.9 %collective-permute-done.9.refs_1_.refs_3_ = bf16[64,1152]{1,0:T(8,128)(2,1)S(1)} collective-permute-done((bf16[64,1152]{1,0:T(8,128)(2,1)S(1)}, bf16[64,1152]{1,0:T(8,128)(2,1)S(1)}, u32[]{:S(2)}, u32[]{:S(2)}) %collective-permute-start.9) | collective-permute-done | bytes 147488 | tf_op jit(solution)/shard_map/ppermute | solution.py:32
  32.6 1.0 %feed.1 = (f32[128,768]{1,0:T(8,128)S(1)}, f32[128,768]{1,0:T(8,128)S(1)}, f32[128,768]{1,0:T(8,128)S(1)}, f32[128,768]{1,0:T(8,128)S(1)}) custom-call(bf16[64,1152]{1,0:T(8,128)(2,1)S(1)} %pad_maximum_fusion.1.refs_0_.refs_2_, bf16[64,1152]{1,0:T(8,128)(2,1)S(1)} %collective-permute-done.9.refs_1_.refs_3_, bf16[1,2048,768]{2,1,0:T(8,128)(2,1)S(1)} %copy-done, ...), custom_call_target="tpu_custom_call" | custom-call | tf_op jit(solution)/shard_map/feed/pallas_call | solution.py:251
  33.6 0.8 %collective-permute-done.8.refs_1_ = bf16[64,1024]{1,0:T(8,128)(2,1)S(1)} collective-permute-done((bf16[64,1024]{1,0:T(8,128)(2,1)S(1)}, bf16[64,1024]{1,0:T(8,128)(2,1)S(1)}, u32[]{:S(2)}, u32[]{:S(2)}) %collective-permute-start.8) | collective-permute-done | bytes 131104 | tf_op jit(solution)/shard_map/ppermute | solution.py:32
  34.4 1.5 %finish.1 = (f32[64,1024]{1,0:T(8,128)S(1)}, bf16[64,1024]{1,0:T(8,128)(2,1)S(1)}, bf16[128,768]{1,0:T(8,128)(2,1)S(1)}, bf16[128,768]{1,0:T(8,128)(2,1)S(1)}, f...) custom-call(bf16[64,1024]{1,0:T(8,128)(2,1)S(1)} %pad_maximum_fusion.2.refs_0_, ...), custom_call_target="tpu_custom_call" | custom-call | tf_op jit(solution)/shard_map/finish/pallas_call | solution.py:251
  35.9 1.6 %collective-permute-start.13 = (bf16[64,1024]{1,0:T(8,128)(2,1)S(1)}, bf16[64,1024]{1,0:T(8,128)(2,1)S(1)}, u32[]{:S(2)}, u32[]{:S(2)}) collective-permute-start(bf16[64,1024]{1,0:T(8,128)(2,1)S(1)} %get-tuple-element.45), channel_id=1, source_target_pairs={{0,2},{1,5},{2,0},{3,7},{4,6},{5,1},{6,4},{7,3},{8,10},{9,13},{10,... | collective-permute-start | bytes 393224 | tf_op jit(solution)/shard_map/ppermute | solution.py:32
  38.6 3.0 %collective-permute-done.13 = bf16[64,1024]{1,0:T(8,128)(2,1)S(1)} collective-permute-done((bf16[64,1024]{1,0:T(8,128)(2,1)S(1)}, bf16[64,1024]{1,0:T(8,128)(2,1)S(1)}, u32[]{:S(2)}, u32[]{:S(2)}) %collective-permute-start.13) | collective-permute-done | bytes 131104 | tf_op jit(solution)/shard_map/ppermute | solution.py:32
  41.8 1.3 %collective-permute-done.16 = bf16[64,1024]{1,0:T(8,128)(2,1)S(1)} collective-permute-done((bf16[64,1024]{1,0:T(8,128)(2,1)S(1)}, bf16[64,1024]{1,0:T(8,128)(2,1)S(1)}, u32[]{:S(2)}, u32[]{:S(2)}) %collective-permute-start.16) | collective-permute-done | bytes 131104 | tf_op jit(solution)/shard_map/ppermute | solution.py:32
  43.9 2.1 %collective-permute-done.14 = bf16[32,1024]{1,0:T(8,128)(2,1)S(1)} collective-permute-done((bf16[32,1024]{1,0:T(8,128)(2,1)S(1)}, bf16[32,1024]{1,0:T(8,128)(2,1)S(1)}, u32[]{:S(2)}, u32[]{:S(2)}) %collective-permute-start.14) | collective-permute-done | bytes 65568 | tf_op jit(solution)/shard_map/ppermute | solution.py:32
  46.0 1.4 %collective-permute-start.15 = (bf16[16,1024]{1,0:T(8,128)(2,1)S(1)}, bf16[16,1024]{1,0:T(8,128)(2,1)S(1)}, u32[]{:S(2)}, u32[]{:S(2)}) collective-permute-start(bf16[16,1024]{1,0:T(8,128)(2,1)S(1)} %slice.111), channel_id=1, source_target_pairs={{0,8},{1,9},{2,10},{3,11},{4,12},{5,13},{6,14},{7,15},{8,0},{9,1},... | collective-permute-start | bytes 98312 | tf_op jit(solution)/shard_map/ppermute | solution.py:32
  47.5 2.0 %collective-permute-start.18 = (bf16[16,1024]{1,0:T(8,128)(2,1)S(1)}, bf16[16,1024]{1,0:T(8,128)(2,1)S(1)}, u32[]{:S(2)}, u32[]{:S(2)}) collective-permute-start(bf16[16,1024]{1,0:T(8,128)(2,1)S(1)} %slice.110), channel_id=1, source_target_pairs={{0,8},{1,9},{2,10},{3,11},{4,12},{5,13},{6,14},{7,15},{8,0},{9,1},... | collective-permute-start | bytes 98312 | tf_op jit(solution)/shard_map/ppermute | solution.py:32
  49.5 1.6 %collective-permute-done.15 = bf16[16,1024]{1,0:T(8,128)(2,1)S(1)} collective-permute-done((bf16[16,1024]{1,0:T(8,128)(2,1)S(1)}, bf16[16,1024]{1,0:T(8,128)(2,1)S(1)}, u32[]{:S(2)}, u32[]{:S(2)}) %collective-permute-start.15) | collective-permute-done | bytes 32800 | tf_op jit(solution)/shard_map/ppermute | solution.py:32
  51.1 1.3 %collective-permute-done.18 = bf16[16,1024]{1,0:T(8,128)(2,1)S(1)} collective-permute-done((bf16[16,1024]{1,0:T(8,128)(2,1)S(1)}, bf16[16,1024]{1,0:T(8,128)(2,1)S(1)}, u32[]{:S(2)}, u32[]{:S(2)}) %collective-permute-start.18) | collective-permute-done | bytes 32800 | tf_op jit(solution)/shard_map/ppermute | solution.py:32
  (47 shorter events, 5.6 us)
Async XLA Ops:
  0.0 32.5 %collective-permute-start.10 = (bf16[1,2048,768]{2,1,0:T(8,128)(2,1)}, bf16[1,2048,768]{2,1,0:T(8,128)(2,1)S(1)}, u32[]{:S(2)}, u32[]{:S(2)}) collective-permute-start(bf16[1,2048,768]{2,1,0:T(8,128)(2,1)} %refs_4_.1), channel_id=1, source_target_pairs={{0,1},{1,0},{2,3},{3,2},{4,5},{5,4},{6,7},{7,6},{8,9},{9,8},{10,11... | collective-permute-start | bytes 9437192 | tf_op jit(solution)/shard_map/ppermute | solution.py:32
  0.5 32.1 %collective-permute-start.11 = (bf16[1,2048,768]{2,1,0:T(8,128)(2,1)}, bf16[1,2048,768]{2,1,0:T(8,128)(2,1)S(1)}, u32[]{:S(2)}, u32[]{:S(2)}) collective-permute-start(bf16[1,2048,768]{2,1,0:T(8,128)(2,1)} %refs_5_.3), channel_id=1, source_target_pairs={{0,1},{1,0},{2,3},{3,2},{4,5},{5,4},{6,7},{7,6},{8,9},{9,8},{10,11... | collective-permute-start | bytes 9437192 | tf_op jit(solution)/shard_map/ppermute | solution.py:32
  0.5 33.9 %collective-permute-start.12 = (bf16[1,768,2048]{2,1,0:T(8,128)(2,1)}, bf16[1,768,2048]{2,1,0:T(8,128)(2,1)S(1)}, u32[]{:S(2)}, u32[]{:S(2)}) collective-permute-start(bf16[1,768,2048]{2,1,0:T(8,128)(2,1)} %refs_9_.1), channel_id=1, source_target_pairs={{0,1},{1,0},{2,3},{3,2},{4,5},{5,4},{6,7},{7,6},{8,9},{9,8},{10,11... | collective-permute-start | bytes 9437192 | tf_op jit(solution)/shard_map/ppermute | solution.py:32
  1.0 31.6 %copy-start.1 = (bf16[1,2048,768]{2,1,0:T(8,128)(2,1)S(1)}, bf16[1,2048,768]{2,1,0:T(8,128)(2,1)}, u32[]{:S(2)}) copy-start(bf16[1,2048,768]{2,1,0:T(8,128)(2,1)} %refs_5_.3) | copy-start | bytes 9437188
  4.6 28.0 %copy-start = (bf16[1,2048,768]{2,1,0:T(8,128)(2,1)S(1)}, bf16[1,2048,768]{2,1,0:T(8,128)(2,1)}, u32[]{:S(2)}) copy-start(bf16[1,2048,768]{2,1,0:T(8,128)(2,1)} %refs_4_.1) | copy-start | bytes 9437188
  4.6 5.5 %collective-permute-start.1 = (bf16[64,1024]{1,0:T(8,128)(2,1)S(1)}, bf16[64,1024]{1,0:T(8,128)(2,1)S(1)}, u32[]{:S(2)}, u32[]{:S(2)}) collective-permute-start(bf16[64,1024]{1,0:T(8,128)(2,1)S(1)} %get-tuple-element.33), channel_id=1, source_target_pairs={{0,2},{1,5},{2,0},{3,7},{4,6},{5,1},{6,4},{7,3},{8,10},{9,13},{10,... | collective-permute-start | bytes 393224 | tf_op jit(solution)/shard_map/ppermute | solution.py:32
  7.2 5.1 %collective-permute-start = (bf16[64,1024]{1,0:T(8,128)(2,1)S(1)}, bf16[64,1024]{1,0:T(8,128)(2,1)S(1)}, u32[]{:S(2)}, u32[]{:S(2)}) collective-permute-start(bf16[64,1024]{1,0:T(8,128)(2,1)S(1)} %get-tuple-element.31), channel_id=1, source_target_pairs={{0,2},{1,5},{2,0},{3,7},{4,6},{5,1},{6,4},{7,3},{8,10},{9,13},{10,... | collective-permute-start | bytes 393224 | tf_op jit(solution)/shard_map/ppermute | solution.py:32
  10.2 4.4 %collective-permute-start.3 = (bf16[32,1024]{1,0:T(8,128)(2,1)S(1)}, bf16[32,1024]{1,0:T(8,128)(2,1)S(1)}, u32[]{:S(2)}, u32[]{:S(2)}) collective-permute-start(bf16[32,1024]{1,0:T(8,128)(2,1)S(1)} %slice.109), channel_id=1, source_target_pairs={{0,4},{1,3},{2,6},{3,1},{4,0},{5,7},{6,2},{7,5},{8,12},{9,11},{10,... | collective-permute-start | bytes 196616 | tf_op jit(solution)/shard_map/ppermute | solution.py:32
  12.4 5.3 %collective-permute-start.2 = (bf16[32,1024]{1,0:T(8,128)(2,1)S(1)}, bf16[32,1024]{1,0:T(8,128)(2,1)S(1)}, u32[]{:S(2)}, u32[]{:S(2)}) collective-permute-start(bf16[32,1024]{1,0:T(8,128)(2,1)S(1)} %slice.108), channel_id=1, source_target_pairs={{0,4},{1,3},{2,6},{3,1},{4,0},{5,7},{6,2},{7,5},{8,12},{9,11},{10,... | collective-permute-start | bytes 196616 | tf_op jit(solution)/shard_map/ppermute | solution.py:32
  14.6 7.8 %collective-permute-start.5 = (bf16[32,1152]{1,0:T(8,128)(2,1)S(1)}, bf16[32,1152]{1,0:T(8,128)(2,1)S(1)}, u32[]{:S(2)}, u32[]{:S(2)}) collective-permute-start(bf16[32,1152]{1,0:T(8,128)(2,1)S(1)} %fusion.2), channel_id=1, source_target_pairs={{0,8},{1,9},{2,10},{3,11},{4,12},{5,13},{6,14},{7,15},{8,0},{9,1},... | collective-permute-start | bytes 221192 | tf_op jit(solution)/shard_map/ppermute | solution.py:32
  17.8 5.4 %collective-permute-start.4 = (bf16[32,1024]{1,0:T(8,128)(2,1)S(1)}, bf16[32,1024]{1,0:T(8,128)(2,1)S(1)}, u32[]{:S(2)}, u32[]{:S(2)}) collective-permute-start(bf16[32,1024]{1,0:T(8,128)(2,1)S(1)} %fusion.3), channel_id=1, source_target_pairs={{0,8},{1,9},{2,10},{3,11},{4,12},{5,13},{6,14},{7,15},{8,0},{9,1},... | collective-permute-start | bytes 196616 | tf_op jit(solution)/shard_map/ppermute | solution.py:32
  22.5 4.9 %collective-permute-start.7 = (bf16[32,1152]{1,0:T(8,128)(2,1)S(1)}, bf16[32,1152]{1,0:T(8,128)(2,1)S(1)}, u32[]{:S(2)}, u32[]{:S(2)}) collective-permute-start(bf16[32,1152]{1,0:T(8,128)(2,1)S(1)} %fusion), channel_id=1, source_target_pairs={{0,4},{1,3},{2,6},{3,1},{4,0},{5,7},{6,2},{7,5},{8,12},{9,11},{10,... | collective-permute-start | bytes 221192 | tf_op jit(solution)/shard_map/ppermute | solution.py:32
  23.2 6.1 %collective-permute-start.6 = (bf16[32,1024]{1,0:T(8,128)(2,1)S(1)}, bf16[32,1024]{1,0:T(8,128)(2,1)S(1)}, u32[]{:S(2)}, u32[]{:S(2)}) collective-permute-start(bf16[32,1024]{1,0:T(8,128)(2,1)S(1)} %fusion.1), channel_id=1, source_target_pairs={{0,4},{1,3},{2,6},{3,1},{4,0},{5,7},{6,2},{7,5},{8,12},{9,11},{10,... | collective-permute-start | bytes 196616 | tf_op jit(solution)/shard_map/ppermute | solution.py:32
  27.3 5.2 %collective-permute-start.9 = (bf16[64,1152]{1,0:T(8,128)(2,1)S(1)}, bf16[64,1152]{1,0:T(8,128)(2,1)S(1)}, u32[]{:S(2)}, u32[]{:S(2)}) collective-permute-start(bf16[64,1152]{1,0:T(8,128)(2,1)S(1)} %pad_maximum_fusion.1.refs_0_.refs_2_), channel_id=1, source_target_pairs={{0,2},{1,5},{2,0},{3,7},{4,6},{5,1},{6,4},{7,3},{8,10},{9,13},{10,... | collective-permute-start | bytes 442376 | tf_op jit(solution)/shard_map/ppermute | solution.py:32
  29.3 5.0 %collective-permute-start.8 = (bf16[64,1024]{1,0:T(8,128)(2,1)S(1)}, bf16[64,1024]{1,0:T(8,128)(2,1)S(1)}, u32[]{:S(2)}, u32[]{:S(2)}) collective-permute-start(bf16[64,1024]{1,0:T(8,128)(2,1)S(1)} %pad_maximum_fusion.2.refs_0_), channel_id=1, source_target_pairs={{0,2},{1,5},{2,0},{3,7},{4,6},{5,1},{6,4},{7,3},{8,10},{9,13},{10,... | collective-permute-start | bytes 393224 | tf_op jit(solution)/shard_map/ppermute | solution.py:32
  35.9 5.7 %collective-permute-start.13 = (bf16[64,1024]{1,0:T(8,128)(2,1)S(1)}, bf16[64,1024]{1,0:T(8,128)(2,1)S(1)}, u32[]{:S(2)}, u32[]{:S(2)}) collective-permute-start(bf16[64,1024]{1,0:T(8,128)(2,1)S(1)} %get-tuple-element.45), channel_id=1, source_target_pairs={{0,2},{1,5},{2,0},{3,7},{4,6},{5,1},{6,4},{7,3},{8,10},{9,13},{10,... | collective-permute-start | bytes 393224 | tf_op jit(solution)/shard_map/ppermute | solution.py:32
  38.0 5.0 %collective-permute-start.16 = (bf16[64,1024]{1,0:T(8,128)(2,1)S(1)}, bf16[64,1024]{1,0:T(8,128)(2,1)S(1)}, u32[]{:S(2)}, u32[]{:S(2)}) collective-permute-start(bf16[64,1024]{1,0:T(8,128)(2,1)S(1)} %get-tuple-element.51), channel_id=1, source_target_pairs={{0,2},{1,5},{2,0},{3,7},{4,6},{5,1},{6,4},{7,3},{8,10},{9,13},{10,... | collective-permute-start | bytes 393224 | tf_op jit(solution)/shard_map/ppermute | solution.py:32
  41.6 4.3 %collective-permute-start.14 = (bf16[32,1024]{1,0:T(8,128)(2,1)S(1)}, bf16[32,1024]{1,0:T(8,128)(2,1)S(1)}, u32[]{:S(2)}, u32[]{:S(2)}) collective-permute-start(bf16[32,1024]{1,0:T(8,128)(2,1)S(1)} %slice.107), channel_id=1, source_target_pairs={{0,4},{1,3},{2,6},{3,1},{4,0},{5,7},{6,2},{7,5},{8,12},{9,11},{10,... | collective-permute-start | bytes 196616 | tf_op jit(solution)/shard_map/ppermute | solution.py:32
  43.1 4.3 %collective-permute-start.17 = (bf16[32,1024]{1,0:T(8,128)(2,1)S(1)}, bf16[32,1024]{1,0:T(8,128)(2,1)S(1)}, u32[]{:S(2)}, u32[]{:S(2)}) collective-permute-start(bf16[32,1024]{1,0:T(8,128)(2,1)S(1)} %slice.106), channel_id=1, source_target_pairs={{0,4},{1,3},{2,6},{3,1},{4,0},{5,7},{6,2},{7,5},{8,12},{9,11},{10,... | collective-permute-start | bytes 196616 | tf_op jit(solution)/shard_map/ppermute | solution.py:32
  46.0 5.1 %collective-permute-start.15 = (bf16[16,1024]{1,0:T(8,128)(2,1)S(1)}, bf16[16,1024]{1,0:T(8,128)(2,1)S(1)}, u32[]{:S(2)}, u32[]{:S(2)}) collective-permute-start(bf16[16,1024]{1,0:T(8,128)(2,1)S(1)} %slice.111), channel_id=1, source_target_pairs={{0,8},{1,9},{2,10},{3,11},{4,12},{5,13},{6,14},{7,15},{8,0},{9,1},... | collective-permute-start | bytes 98312 | tf_op jit(solution)/shard_map/ppermute | solution.py:32
  47.5 4.9 %collective-permute-start.18 = (bf16[16,1024]{1,0:T(8,128)(2,1)S(1)}, bf16[16,1024]{1,0:T(8,128)(2,1)S(1)}, u32[]{:S(2)}, u32[]{:S(2)}) collective-permute-start(bf16[16,1024]{1,0:T(8,128)(2,1)S(1)} %slice.110), channel_id=1, source_target_pairs={{0,8},{1,9},{2,10},{3,11},{4,12},{5,13},{6,14},{7,15},{8,0},{9,1},... | collective-permute-start | bytes 98312 | tf_op jit(solution)/shard_map/ppermute | solution.py:32

commit v4 on v3

--- a/solution.py
+++ b/solution.py
@@ -12,6 +12,7 @@
 CHUNKS = len(PIECES)
 CARRIER = 0
 LANES = 128
+HINT = 30_000_000_000
 
 
 def bits_of(count):
@@ -27,16 +28,38 @@
     return -(-2 * axis_width // LANES) * LANES
 
 
-def exchange(block, masks):
-    count = lax.axis_size("wide")
-    return lax.ppermute(block, "wide", [(i, i ^ masks[i & 1]) for i in range(count)])
-
-
 def slice_orders(axis_width):
     groups = axis_width // ATT_TP
     first = [groups << step for step in range(bits_of(ATT_TP))]
-    second = [first[1], first[0]] + first[2:] if groups > 1 and len(first) > 2 else first
+    second = [first[1], first[0], *first[2:]]
     return first, second
+
+
+def exchange(block, route):
+    count = lax.axis_size("wide")
+    return lax.ppermute(block, "wide", [(i, route(i)) for i in range(count)])
+
+
+def on_odd_chip():
+    index = lax.axis_index("wide") // (lax.axis_size("wide") // ATT_TP)
+    odd = 0
+    for step in range(bits_of(ATT_TP)):
+        odd ^= index >> step & 1
+    return odd == 1
+
+
+class Routes:
+    def __init__(self, axis_width):
+        groups = axis_width // ATT_TP
+        orders = slice_orders(axis_width)
+        odd = lambda i: (i // groups).bit_count() & 1
+        self.pair = lambda i: i ^ 1
+        self.steps = [
+            lambda i, step=step: i ^ orders[(i & 1) ^ odd(i)][step] ^ 1
+            for step in range(bits_of(ATT_TP))
+        ]
+        self.last = lambda i: i ^ orders[(i & 1) ^ odd(i)][-1] ^ odd(i)
+        self.groups = [lambda i, k=k: i ^ 1 << k for k in range(1, bits_of(groups))]
 
 
 def relative_masks(order):
@@ -51,20 +74,23 @@
     return masks
 
 
-def attend_kernel(axis_width, *refs):
-    sources, outs, scratch = refs[:10], refs[10 : 12 + 2 * CHUNKS], refs[12 + 2 * CHUNKS :]
-    *inputs, attended, sems = scratch
+def started(sources, targets, sems):
     copies = [
         pltpu.make_async_copy(source, target, sems.at[n])
-        for n, (source, target) in enumerate(zip(sources, [*inputs, outs[-1]]))
+        for n, (source, target) in enumerate(zip(sources, targets))
     ]
     for copy in copies:
         copy.start()
+    return copies
+
+
+def attend_kernel(axis_width, *refs):
+    sources, (ordered, w_out, w_down), scratch = refs[:10], refs[10:13], refs[13:]
+    *inputs, attended, sems = scratch
+    copies = started(sources, [*inputs, w_out, w_down], sems)
     for copy in copies[:-2]:
         copy.wait()
-    table, lengths, parents, expert_ids, gate_weights = inputs[:5]
-    queries, tree_kv, kv_cache, weights_in = inputs[5:]
-    *outs, extra, w_down = outs
+    table, lengths, parents, expert_ids, gate_weights, queries, tree_kv, kv_cache = inputs
     seq_count, node_count = parents.shape
     head_dim = tree_kv.shape[-1]
     head_count = queries.shape[1] // head_dim
@@ -74,25 +100,26 @@
     query_count = head_count * node_count
     f32, bf16 = jnp.float32, jnp.bfloat16
 
+    lane = lax.broadcasted_iota(jnp.int32, (8, all_nodes), 1)
     shifted = [
         jnp.where(parents[s : s + 1, :] >= 0, parents[s : s + 1, :] + s * node_count, -1)
         for s in range(seq_count)
     ]
-    parent_row = jnp.concatenate(shifted, axis=1)
-    rows = lax.broadcasted_iota(jnp.int32, (all_nodes, all_nodes), 0)
-    columns = lax.broadcasted_iota(jnp.int32, (all_nodes, all_nodes), 1)
-    reached = ((rows == columns) | (rows == parent_row)).astype(f32).astype(bf16)
+    above = jnp.broadcast_to(jnp.concatenate(shifted, axis=1), lane.shape)
+    above = jnp.where(above >= 0, above, lane)
+    words = jnp.left_shift(1, lane % node_count)
     for repeat in range(max(node_count - 1, 1).bit_length()):
-        squared = jnp.dot(reached, reached, preferred_element_type=f32)
-        reached = jnp.minimum(squared, 1.0).astype(bf16)
-
-    node_rows = lax.broadcasted_iota(jnp.int32, (all_nodes, query_count), 0)
-    query_nodes = lax.broadcasted_iota(jnp.int32, (all_nodes, query_count), 1) % node_count
+        words = words | jnp.take_along_axis(words, above, axis=1)
+        above = jnp.take_along_axis(above, above, axis=1)
+
+    query_nodes = lax.broadcasted_iota(jnp.int32, (8, query_count), 1) % node_count
+    node_rows = lax.broadcasted_iota(jnp.int32, (node_count, query_count), 0)
     positions = lax.broadcasted_iota(jnp.int32, (cached, query_count), 0)
     for s in range(seq_count):
         own = slice(s * node_count, (s + 1) * node_count)
-        spread = (node_rows == query_nodes + s * node_count).astype(f32).astype(bf16)
-        tree_open = jnp.dot(reached[own], spread, preferred_element_type=f32) > 0.5
+        word = jnp.take_along_axis(words, query_nodes + s * node_count, axis=1)
+        word = jnp.broadcast_to(word[:1], node_rows.shape)
+        tree_open = (lax.shift_right_logical(word, node_rows) & 1) == 1
         keys = [kv_cache[0, table[s, p]] for p in range(pages)]
         values = [kv_cache[1, table[s, p]] for p in range(pages)]
         key_rows = jnp.concatenate(keys + [tree_kv[0, own]], axis=0)
@@ -119,7 +146,7 @@
             ]
 
     listed, row_count = expert_ids.shape
-    spread_width = extra.shape[1]
+    spread_width = spare_width(axis_width)
     expert = lax.broadcasted_iota(jnp.int32, (spread_width, row_count), 0)
     weight = jnp.zeros((spread_width, row_count), f32)
     for k in range(listed):
@@ -130,8 +157,9 @@
     parts = jnp.where(
         expert < axis_width, upper, jnp.where(expert < 2 * axis_width, weight - upper, 0.0)
     )
-    extra[:row_count] = parts.T.astype(bf16)
-    extra[row_count:] = jnp.zeros((row_count, spread_width), bf16)
+    ordered[:row_count, -spread_width:] = parts.T.astype(bf16)
+    rest = (all_nodes - row_count, spread_width)
+    ordered[row_count:, -spread_width:] = jnp.zeros(rest, bf16)
 
     device = lax.axis_index("wide")
     groups = axis_width // ATT_TP
@@ -141,14 +169,38 @@
     for one, other in zip(first, second):
         target = (device ^ jnp.where(device & 1 == 0, one, other)) // groups
         picked.append(attended[pl.ds(pl.multiple_of(target * block, block), block), :])
-    ordered = jnp.concatenate(picked, axis=0)
-    copies[-2].wait()
-    half = all_nodes // 2
-    for c, (low, high) in enumerate(column_cuts(weights_in.shape[1])):
-        projected = jnp.dot(ordered, weights_in[:, low:high], preferred_element_type=f32)
-        outs[2 * c][...] = projected[:half]
-        outs[2 * c + 1][...] = projected[half:].astype(bf16)
-    copies[-1].wait()
+    ordered[:, : queries.shape[1]] = jnp.concatenate(picked, axis=0)
+    for copy in copies[-2:]:
+        copy.wait()
+
+
+def project_kernel(own_rows, cut, own, other, w_out, kept, sent, *extra):
+    rows = jnp.where(on_odd_chip(), other[...], own[...])
+    width = w_out.shape[0]
+    if extra:
+        extra[0][...] = rows[: 2 * own_rows, width:]
+    half = rows.shape[0] // 2
+    projected = jnp.dot(
+        rows[:, :width], w_out[:, cut[0] : cut[1]], preferred_element_type=jnp.float32
+    )
+    kept[...] = projected[:half]
+    sent[...] = projected[half:].astype(jnp.bfloat16)
+
+
+def project(own, other, w_out, own_rows):
+    spare = spare_width(lax.axis_size("wide"))
+    halves = []
+    for c, cut in enumerate(column_cuts(w_out.shape[1])):
+        shapes = kept_and_sent(own.shape[0], [cut])
+        last = c == CHUNKS - 1
+        halves += local_call(
+            functools.partial(project_kernel, own_rows, cut),
+            "project",
+            shapes + [pltpu.VMEM((2 * own_rows, spare), jnp.bfloat16)] * last,
+            [own, other, w_out],
+            flops=HINT * c,
+        )
+    return halves
 
 
 def kept_and_sent(rows, cuts):
@@ -163,21 +215,20 @@
     queries, tree_kv, kv_cache, table, lengths, parents, w_out, w_down, expert_ids, gate_weights
 ):
     axis_width = lax.axis_size("wide")
-    features = w_out.shape[1]
-    rows = queries.shape[0]
-    own_rows = expert_ids.shape[0]
-    extra_width = spare_width(axis_width)
-    halves = kept_and_sent(rows, column_cuts(features))
+    rows, width = queries.shape
     given = [table, lengths, parents, expert_ids.T, gate_weights.T, queries, tree_kv, kv_cache, w_out, w_down]
-    spaces = [pltpu.SMEM] * 2 + [pltpu.VMEM] * (len(given) - 2)
+    spaces = [pltpu.SMEM] * 2 + [pltpu.VMEM] * 6
     given = [pltpu.with_memory_space_constraint(x, pltpu.HBM) for x in given]
     return pl.pallas_call(
         functools.partial(attend_kernel, axis_width),
-        out_shape=halves
-        + [pltpu.VMEM((2 * own_rows, extra_width), jnp.bfloat16), pltpu.VMEM(w_down.shape, w_down.dtype)],
+        out_shape=[
+            pltpu.VMEM((rows, width + spare_width(axis_width)), jnp.bfloat16),
+            pltpu.VMEM(w_out.shape, w_out.dtype),
+            pltpu.VMEM(w_down.shape, w_down.dtype),
+        ],
         in_specs=[pl.BlockSpec(memory_space=pltpu.HBM)] * len(given),
-        out_specs=[pl.BlockSpec(memory_space=pltpu.VMEM)] * (2 * CHUNKS + 2),
-        scratch_shapes=[space(x.shape, x.dtype) for space, x in zip(spaces, given[:-1])]
+        out_specs=[pl.BlockSpec(memory_space=pltpu.VMEM)] * 3,
+        scratch_shapes=[space(x.shape, x.dtype) for space, x in zip(spaces, given)]
         + [pltpu.VMEM(queries.shape, jnp.bfloat16), pltpu.SemaphoreType.DMA((len(given),))],
         compiler_params=pltpu.CompilerParams(vmem_limit_bytes=16 * 1024 * 1024),
         name="attend",
@@ -247,13 +298,14 @@
         sent[:, start : start + size] = weighted[half:].astype(jnp.bfloat16)
 
 
-def local_call(kernel, name, out_shape, given):
+def local_call(kernel, name, out_shape, given, flops=0):
     return pl.pallas_call(
         kernel,
         out_shape=out_shape,
         in_specs=[pl.BlockSpec(memory_space=pltpu.VMEM)] * len(given),
         out_specs=[pl.BlockSpec(memory_space=pltpu.VMEM)] * len(out_shape),
         compiler_params=pltpu.CompilerParams(vmem_limit_bytes=16 * 1024 * 1024),
+        cost_estimate=pl.CostEstimate(flops=flops, bytes_accessed=0, transcendentals=0) if flops else None,
         name=name,
     )(*given)
 
@@ -296,15 +348,15 @@
     return value if earlier is None else lax.optimization_barrier((value, earlier))[0]
 
 
-def reduce_and_gather(halves, extra, steps, gathers):
+def reduce_and_gather(halves, extra, routes):
     f32, bf16 = jnp.float32, jnp.bfloat16
     parts = [list(halves[2 * c : 2 * c + 2]) for c in range(CHUNKS)]
-    for number, masks in enumerate(steps[:-1]):
+    for number, route in enumerate(routes.steps[:-1]):
         earlier = None
         for c, part in enumerate(parts):
             kept, sent = part
-            kept = kept + ordered_after(exchange(sent, masks), earlier).astype(f32)
-            if number < len(steps) - 2:
+            kept = kept + ordered_after(exchange(sent, route), earlier).astype(f32)
+            if number < len(routes.steps) - 2:
                 part[:] = halved(kept)
             else:
                 if c == CARRIER:
@@ -314,13 +366,14 @@
     blocks, earlier = [], None
     for kept, sent in parts:
         half = kept.shape[0] // 2
-        other = ordered_after(exchange(sent, steps[-1]), earlier).astype(f32)
+        other = ordered_after(exchange(sent, routes.steps[-1]), earlier).astype(f32)
         blocks.append((kept + jnp.concatenate([other[half:], other[:half]], axis=0)).astype(bf16))
         earlier = blocks[-1]
-    for masks in gathers[:-1]:
+    gathers = routes.steps[-2::-1] + routes.groups
+    for route in gathers[:-1]:
         earlier = None
         for c, block in enumerate(blocks):
-            other = ordered_after(exchange(block, masks), earlier)
+            other = ordered_after(exchange(block, route), earlier)
             blocks[c] = earlier = jnp.concatenate([block, other], axis=0)
     return [(block, exchange(block, gathers[-1])) for block in blocks]
 
@@ -340,35 +393,32 @@
     gate_weights,
 ):
     axis_width = lax.axis_size("wide")
-    steps = list(zip(*slice_orders(axis_width)))
-    group_steps = [(1 << k, 1 << k) for k in range(1, bits_of(axis_width // ATT_TP))]
-    pair = (1, 1)
+    routes = Routes(axis_width)
     owners = (0, 1)
-    feeds = [w_gate, w_up, exchange(w_gate, pair), exchange(w_up, pair)]
-    *halves, extra, fetched = attend(
+    own, fetched_out, fetched_down = attend(
         queries, tree_kv, kv_cache, block_table, cache_lengths, parents, w_out, w_down,
         expert_ids, gate_weights,
     )
-    downs = [fetched, exchange(w_down, pair)]
-    gathers = steps[-2::-1] + group_steps
-    hidden = reduce_and_gather(halves, extra, steps, gathers)
-    produced = experts(hidden, owners, feeds, downs)
-    results = []
-    parts = [list(pair) for pair in produced]
-    hops = group_steps[::-1] + steps
-    for number, masks in enumerate(hops):
+    *halves, extra = project(own, exchange(own, routes.pair), fetched_out, expert_ids.shape[0])
+    others = [exchange(x, routes.pair) for x in (w_gate, w_up, w_down)]
+    feeds = [w_gate, w_up, *others[:2]]
+    downs = [fetched_down, others[2]]
+    hidden = reduce_and_gather(halves, extra, routes)
+    parts = [list(pair) for pair in experts(hidden, owners, feeds, downs)]
+    for route in routes.groups[::-1] + routes.steps[:-1]:
         earlier = None
         for part in parts:
             kept, sent = part
-            other = ordered_after(exchange(sent, masks), earlier)
-            kept = kept + other.astype(jnp.float32)
-            if number < len(hops) - 1:
-                part[:] = halved(kept)
-                earlier = part[1]
-            else:
-                results.append(kept.astype(jnp.bfloat16))
-                earlier = results[-1]
-    return jnp.concatenate(results, axis=1)
+            other = ordered_after(exchange(sent, route), earlier)
+            part[:] = halved(kept + other.astype(jnp.float32))
+            earlier = part[1]
+    results, earlier = [], None
+    for kept, sent in parts:
+        other = ordered_after(exchange(sent, routes.steps[-1]), earlier).astype(jnp.float32)
+        results.append((kept + other).astype(jnp.bfloat16))
+        earlier = results[-1]
+    result = jnp.concatenate(results, axis=1)
+    return jnp.where(on_odd_chip(), exchange(result, routes.pair), result)
 
 
 def solution(mesh):

time: 53.2 us -> 51.5 us (0.968)
  waiting for transfers between devices: 21.1 us -> 15.2 us
  starting transfers between devices: 24.1 us -> 28.1 us
    ppermute x19 -> x21, waiting for transfers between devices: 21.1 us -> 15.2 us  [exchange(): return lax.ppermute(block, 'wide', [(i, route(i)) for i in range(count)])]
    ppermute x19 -> x21, starting transfers between devices: 24.1 us -> 28.1 us  [exchange(): return lax.ppermute(block, 'wide', [(i, route(i)) for i in range(count)])]
    select_n x0 -> x1, other arithmetic: none -> 0.65 us  [body(): return jnp.where(on_odd_chip(), exchange(result, routes.pair), result)]
    pallas_call x1, Pallas kernels: 3.63 us -> 2.98 us  [attend(): pl.pallas_call(functools.partial(attend_kernel, axis_width), out_shape=[p...]
    pallas_call x3 -> x5, Pallas kernels: 3.09 us -> 3.73 us  [local_call(): pl.pallas_call(kernel, out_shape=out_shape, in_specs=[pl.BlockSpec(memory...]
    concatenate x1, other arithmetic: 0.64 us -> 0.01 us  [body(): result = jnp.concatenate(results, axis=1)]
  transfers between devices with their start and end apart: 19 -> 21, of which waited for: 12 -> 14; matrix products, arithmetic and copies ran while one was open for 1% -> 1% of each run, Pallas kernels for 10% -> 4%
where the time goes in v4:
time: 51.5 us; the launch traced here: 51.3 us
  starting transfers between devices  28.1 us (55%)
  waiting for transfers between devices  15.2 us (30%)
  Pallas kernels  6.7 us (13%)
  other arithmetic  0.95 us (2%)
    ppermute x21, starting transfers between devices, exchange(): return lax.ppermute(block, 'wide', [(i, route(i)) for i in range(count)])  28.1 us
    ppermute x21, waiting for transfers between devices, exchange(): return lax.ppermute(block, 'wide', [(i, route(i)) for i in range(count)])  15.2 us
    pallas_call x5, Pallas kernels, local_call(): pl.pallas_call(kernel, out_shape=out_shape, in_specs=[pl.BlockSpec(memory...  3.73 us
    pallas_call x1, Pallas kernels, attend(): pl.pallas_call(functools.partial(attend_kernel, axis_width), out_shape=[p...  2.98 us
  transfers between devices with their start and end apart: 21, of which 14 were waited for; matrix products, arithmetic and copies ran while one was open for 1% of the time, Pallas kernels for 4%

profile of v4, /device:TPU:0, one launch (start us, length us, event | category | flops | bytes accessed | tf_op | source)
XLA Modules:
  0.0 51.3 jit_solution(2056745346359220811)
XLA Ops:
  0.0 3.0 %attend.1 = (bf16[128,640]{1,0:T(8,128)(2,1)S(1)}, bf16[512,2048]{1,0:T(8,128)(2,1)S(1)}, bf16[1,768,2048]{2,1,0:T(8,128)(2,1)S(1)}) custom-call(s32[4,4]{1,0:T(4,128)} %refs_0_.1, s32[1,4]{1,0:T(1,128)} %refs_1_.1, s32[4,32]{1,0:T(4,128)} %refs_2_.2, s32[8,16]{1,0:T(8,128)} %bitcast.2, f32[8,16]{1,0:T(8,128)} %bitcast.3, bf16[128,512]{1,0:T(8,128)(2,1)} %refs_5_.2, ...), custom_call_target="tpu_custom_call" | custom-call | tf_op jit(solution)/shard_map/attend/pallas_call | solution.py:222
  4.9 2.7 %collective-permute-start.2 = (bf16[64,1024]{1,0:T(8,128)(2,1)S(1)}, bf16[64,1024]{1,0:T(8,128)(2,1)S(1)}, u32[]{:S(2)}, u32[]{:S(2)}) collective-permute-start(bf16[64,1024]{1,0:T(8,128)(2,1)S(1)} %get-tuple-element.37), channel_id=1, source_target_pairs={{0,3},{1,4},{2,7},{3,0},{4,1},{5,6},{6,5},{7,2},{8,13},{9,10},{10,... | collective-permute-start | bytes 393224 | tf_op jit(solution)/shard_map/ppermute | solution.py:40
  8.0 2.2 %collective-permute-done.2 = bf16[64,1024]{1,0:T(8,128)(2,1)S(1)} collective-permute-done((bf16[64,1024]{1,0:T(8,128)(2,1)S(1)}, bf16[64,1024]{1,0:T(8,128)(2,1)S(1)}, u32[]{:S(2)}, u32[]{:S(2)}) %collective-permute-start.2) | collective-permute-done | bytes 131104 | tf_op jit(solution)/shard_map/ppermute | solution.py:40
  10.3 2.2 %collective-permute-start.4 = (bf16[32,1024]{1,0:T(8,128)(2,1)S(1)}, bf16[32,1024]{1,0:T(8,128)(2,1)S(1)}, u32[]{:S(2)}, u32[]{:S(2)}) collective-permute-start(bf16[32,1024]{1,0:T(8,128)(2,1)S(1)} %slice.109), channel_id=1, source_target_pairs={{0,5},{1,2},{2,1},{3,6},{4,7},{5,0},{6,3},{7,4},{8,11},{9,12},{10,... | collective-permute-start | bytes 196616 | tf_op jit(solution)/shard_map/ppermute | solution.py:40
  12.5 1.6 %collective-permute-start.3 = (bf16[32,1024]{1,0:T(8,128)(2,1)S(1)}, bf16[32,1024]{1,0:T(8,128)(2,1)S(1)}, u32[]{:S(2)}, u32[]{:S(2)}) collective-permute-start(bf16[32,1024]{1,0:T(8,128)(2,1)S(1)} %slice.108), channel_id=1, source_target_pairs={{0,5},{1,2},{2,1},{3,6},{4,7},{5,0},{6,3},{7,4},{8,11},{9,12},{10,... | collective-permute-start | bytes 196616 | tf_op jit(solution)/shard_map/ppermute | solution.py:40
  14.4 2.5 %collective-permute-start.6 = (bf16[32,1152]{1,0:T(8,128)(2,1)S(1)}, bf16[32,1152]{1,0:T(8,128)(2,1)S(1)}, u32[]{:S(2)}, u32[]{:S(2)}) collective-permute-start(bf16[32,1152]{1,0:T(8,128)(2,1)S(1)} %fusion.2), channel_id=1, source_target_pairs={{0,9},{1,8},{2,11},{3,10},{4,13},{5,12},{6,15},{7,14},{8,1},{9,0},... | collective-permute-start | bytes 221192 | tf_op jit(solution)/shard_map/ppermute | solution.py:40
  16.9 1.9 %collective-permute-start.5 = (bf16[32,1024]{1,0:T(8,128)(2,1)S(1)}, bf16[32,1024]{1,0:T(8,128)(2,1)S(1)}, u32[]{:S(2)}, u32[]{:S(2)}) collective-permute-start(bf16[32,1024]{1,0:T(8,128)(2,1)S(1)} %fusion.3), channel_id=1, source_target_pairs={{0,9},{1,8},{2,11},{3,10},{4,13},{5,12},{6,15},{7,14},{8,1},{9,0},... | collective-permute-start | bytes 196616 | tf_op jit(solution)/shard_map/ppermute | solution.py:40
  18.8 2.4 %collective-permute-done.6 = bf16[32,1152]{1,0:T(8,128)(2,1)S(1)} collective-permute-done((bf16[32,1152]{1,0:T(8,128)(2,1)S(1)}, bf16[32,1152]{1,0:T(8,128)(2,1)S(1)}, u32[]{:S(2)}, u32[]{:S(2)}) %collective-permute-start.6) | collective-permute-done | bytes 73760 | tf_op jit(solution)/shard_map/ppermute | solution.py:40
  21.3 2.2 %collective-permute-start.8 = (bf16[32,1152]{1,0:T(8,128)(2,1)S(1)}, bf16[32,1152]{1,0:T(8,128)(2,1)S(1)}, u32[]{:S(2)}, u32[]{:S(2)}) collective-permute-start(bf16[32,1152]{1,0:T(8,128)(2,1)S(1)} %fusion), channel_id=1, source_target_pairs={{0,5},{1,2},{2,1},{3,6},{4,7},{5,0},{6,3},{7,4},{8,11},{9,12},{10,... | collective-permute-start | bytes 221192 | tf_op jit(solution)/shard_map/ppermute | solution.py:40
  24.1 0.8 %collective-permute-start.7 = (bf16[32,1024]{1,0:T(8,128)(2,1)S(1)}, bf16[32,1024]{1,0:T(8,128)(2,1)S(1)}, u32[]{:S(2)}, u32[]{:S(2)}) collective-permute-start(bf16[32,1024]{1,0:T(8,128)(2,1)S(1)} %fusion.1), channel_id=1, source_target_pairs={{0,5},{1,2},{2,1},{3,6},{4,7},{5,0},{6,3},{7,4},{8,11},{9,12},{10,... | collective-permute-start | bytes 196616 | tf_op jit(solution)/shard_map/ppermute | solution.py:40
  25.5 1.7 %collective-permute-start.10 = (bf16[64,1152]{1,0:T(8,128)(2,1)S(1)}, bf16[64,1152]{1,0:T(8,128)(2,1)S(1)}, u32[]{:S(2)}, u32[]{:S(2)}) collective-permute-start(bf16[64,1152]{1,0:T(8,128)(2,1)S(1)} %pad_maximum_fusion.1.refs_0_.refs_2_), channel_id=1, source_target_pairs={{0,3},{1,4},{2,7},{3,0},{4,1},{5,6},{6,5},{7,2},{8,13},{9,10},{10,... | collective-permute-start | bytes 442376 | tf_op jit(solution)/shard_map/ppermute | solution.py:40
  27.8 1.4 %collective-permute-start.9 = (bf16[64,1024]{1,0:T(8,128)(2,1)S(1)}, bf16[64,1024]{1,0:T(8,128)(2,1)S(1)}, u32[]{:S(2)}, u32[]{:S(2)}) collective-permute-start(bf16[64,1024]{1,0:T(8,128)(2,1)S(1)} %pad_maximum_fusion.2.refs_0_), channel_id=1, source_target_pairs={{0,3},{1,4},{2,7},{3,0},{4,1},{5,6},{6,5},{7,2},{8,13},{9,10},{10,... | collective-permute-start | bytes 393224 | tf_op jit(solution)/shard_map/ppermute | solution.py:40
  29.3 0.9 %collective-permute-done.10.refs_1_.refs_3_ = bf16[64,1152]{1,0:T(8,128)(2,1)S(1)} collective-permute-done((bf16[64,1152]{1,0:T(8,128)(2,1)S(1)}, bf16[64,1152]{1,0:T(8,128)(2,1)S(1)}, u32[]{:S(2)}, u32[]{:S(2)}) %collective-permute-start.10) | collective-permute-done | bytes 147488 | tf_op jit(solution)/shard_map/ppermute | solution.py:40
  30.2 1.0 %feed.1 = (f32[128,768]{1,0:T(8,128)S(1)}, f32[128,768]{1,0:T(8,128)S(1)}, f32[128,768]{1,0:T(8,128)S(1)}, f32[128,768]{1,0:T(8,128)S(1)}) custom-call(bf16[64,1152]{1,0:T(8,128)(2,1)S(1)} %pad_maximum_fusion.1.refs_0_.refs_2_, bf16[64,1152]{1,0:T(8,128)(2,1)S(1)} %collective-permute-done.10.refs_1_.refs_3_, bf16[1,2048,768]{2,1,0:T(8,128)(2,1)S(1)} %copy-done, ...), custom_call_target="tpu_custom_call" | custom-call | tf_op jit(solution)/shard_map/feed/pallas_call | solution.py:302
  31.2 1.1 %collective-permute-done.9.refs_1_ = bf16[64,1024]{1,0:T(8,128)(2,1)S(1)} collective-permute-done((bf16[64,1024]{1,0:T(8,128)(2,1)S(1)}, bf16[64,1024]{1,0:T(8,128)(2,1)S(1)}, u32[]{:S(2)}, u32[]{:S(2)}) %collective-permute-start.9) | collective-permute-done | bytes 131104 | tf_op jit(solution)/shard_map/ppermute | solution.py:40
  32.3 1.5 %finish.1 = (f32[64,1024]{1,0:T(8,128)S(1)}, bf16[64,1024]{1,0:T(8,128)(2,1)S(1)}, bf16[128,768]{1,0:T(8,128)(2,1)S(1)}, bf16[128,768]{1,0:T(8,128)(2,1)S(1)}, f...) custom-call(bf16[64,1024]{1,0:T(8,128)(2,1)S(1)} %pad_maximum_fusion.2.refs_0_, ...), custom_call_target="tpu_custom_call" | custom-call | tf_op jit(solution)/shard_map/finish/pallas_call | solution.py:302
  33.8 1.4 %collective-permute-start.14 = (bf16[64,1024]{1,0:T(8,128)(2,1)S(1)}, bf16[64,1024]{1,0:T(8,128)(2,1)S(1)}, u32[]{:S(2)}, u32[]{:S(2)}) collective-permute-start(bf16[64,1024]{1,0:T(8,128)(2,1)S(1)} %get-tuple-element.49), channel_id=1, source_target_pairs={{0,3},{1,4},{2,7},{3,0},{4,1},{5,6},{6,5},{7,2},{8,13},{9,10},{10,... | collective-permute-start | bytes 393224 | tf_op jit(solution)/shard_map/ppermute | solution.py:40
  36.3 2.0 %collective-permute-done.14 = bf16[64,1024]{1,0:T(8,128)(2,1)S(1)} collective-permute-done((bf16[64,1024]{1,0:T(8,128)(2,1)S(1)}, bf16[64,1024]{1,0:T(8,128)(2,1)S(1)}, u32[]{:S(2)}, u32[]{:S(2)}) %collective-permute-start.14) | collective-permute-done | bytes 131104 | tf_op jit(solution)/shard_map/ppermute | solution.py:40
  38.3 1.5 %collective-permute-start.15 = (bf16[32,1024]{1,0:T(8,128)(2,1)S(1)}, bf16[32,1024]{1,0:T(8,128)(2,1)S(1)}, u32[]{:S(2)}, u32[]{:S(2)}) collective-permute-start(bf16[32,1024]{1,0:T(8,128)(2,1)S(1)} %slice.107), channel_id=1, source_target_pairs={{0,5},{1,2},{2,1},{3,6},{4,7},{5,0},{6,3},{7,4},{8,11},{9,12},{10,... | collective-permute-start | bytes 196616 | tf_op jit(solution)/shard_map/ppermute | solution.py:40
  40.4 1.3 %collective-permute-start.18 = (bf16[32,1024]{1,0:T(8,128)(2,1)S(1)}, bf16[32,1024]{1,0:T(8,128)(2,1)S(1)}, u32[]{:S(2)}, u32[]{:S(2)}) collective-permute-start(bf16[32,1024]{1,0:T(8,128)(2,1)S(1)} %slice.106), channel_id=1, source_target_pairs={{0,5},{1,2},{2,1},{3,6},{4,7},{5,0},{6,3},{7,4},{8,11},{9,12},{10,... | collective-permute-start | bytes 196616 | tf_op jit(solution)/shard_map/ppermute | solution.py:40
  42.1 2.9 %collective-permute-start.16 = (bf16[16,1024]{1,0:T(8,128)(2,1)S(1)}, bf16[16,1024]{1,0:T(8,128)(2,1)S(1)}, u32[]{:S(2)}, u32[]{:S(2)}) collective-permute-start(bf16[16,1024]{1,0:T(8,128)(2,1)S(1)} %slice.111), channel_id=1, source_target_pairs={{0,9},{1,8},{2,11},{3,10},{4,13},{5,12},{6,15},{7,14},{8,1},{9,0},... | collective-permute-start | bytes 98312 | tf_op jit(solution)/shard_map/ppermute | solution.py:40
  45.0 2.0 %collective-permute-start.19 = (bf16[16,1024]{1,0:T(8,128)(2,1)S(1)}, bf16[16,1024]{1,0:T(8,128)(2,1)S(1)}, u32[]{:S(2)}, u32[]{:S(2)}) collective-permute-start(bf16[16,1024]{1,0:T(8,128)(2,1)S(1)} %slice.110), channel_id=1, source_target_pairs={{0,9},{1,8},{2,11},{3,10},{4,13},{5,12},{6,15},{7,14},{8,1},{9,0},... | collective-permute-start | bytes 98312 | tf_op jit(solution)/shard_map/ppermute | solution.py:40
  47.1 2.3 %collective-permute-done.19 = bf16[16,1024]{1,0:T(8,128)(2,1)S(1)} collective-permute-done((bf16[16,1024]{1,0:T(8,128)(2,1)S(1)}, bf16[16,1024]{1,0:T(8,128)(2,1)S(1)}, u32[]{:S(2)}, u32[]{:S(2)}) %collective-permute-start.19) | collective-permute-done | bytes 32800 | tf_op jit(solution)/shard_map/ppermute | solution.py:40
  49.7 1.0 %collective-permute-done.20 = bf16[16,2048]{1,0:T(8,128)(2,1)S(1)} collective-permute-done((bf16[16,2048]{1,0:T(8,128)(2,1)S(1)}, bf16[16,2048]{1,0:T(8,128)(2,1)S(1)}, u32[]{:S(2)}, u32[]{:S(2)}) %collective-permute-start.20) | collective-permute-done | bytes 65568 | tf_op jit(solution)/shard_map/ppermute | solution.py:40
  (54 shorter events, 7.7 us)
Async XLA Ops:
  0.0 3.7 %copy-start = (bf16[1,2048,768]{2,1,0:T(8,128)(2,1)S(1)}, bf16[1,2048,768]{2,1,0:T(8,128)(2,1)}, u32[]{:S(2)}) copy-start(bf16[1,2048,768]{2,1,0:T(8,128)(2,1)} %refs_4_.1) | copy-start | bytes 9437188
  3.0 1.5 %collective-permute-start = (bf16[128,640]{1,0:T(8,128)(2,1)S(1)}, bf16[128,640]{1,0:T(8,128)(2,1)S(1)}, u32[]{:S(2)}, u32[]{:S(2)}) collective-permute-start(bf16[128,640]{1,0:T(8,128)(2,1)S(1)} %get-tuple-element.32.own), channel_id=1, source_target_pairs={{0,1},{1,0},{2,3},{3,2},{4,5},{5,4},{6,7},{7,6},{8,9},{9,8},{10,11... | collective-permute-start | bytes 491528 | tf_op jit(solution)/shard_map/ppermute | solution.py:40
  3.5 28.8 %collective-permute-start.13 = (bf16[1,768,2048]{2,1,0:T(8,128)(2,1)}, bf16[1,768,2048]{2,1,0:T(8,128)(2,1)S(1)}, u32[]{:S(2)}, u32[]{:S(2)}) collective-permute-start(bf16[1,768,2048]{2,1,0:T(8,128)(2,1)} %refs_9_.1), channel_id=1, source_target_pairs={{0,1},{1,0},{2,3},{3,2},{4,5},{5,4},{6,7},{7,6},{8,9},{9,8},{10,11... | collective-permute-start | bytes 9437192 | tf_op jit(solution)/shard_map/ppermute | solution.py:40
  3.7 26.5 %collective-permute-start.11 = (bf16[1,2048,768]{2,1,0:T(8,128)(2,1)S(1)}, bf16[1,2048,768]{2,1,0:T(8,128)(2,1)S(1)}, u32[]{:S(2)}, u32[]{:S(2)}) collective-permute-start(bf16[1,2048,768]{2,1,0:T(8,128)(2,1)S(1)} %copy-done), channel_id=1, source_target_pairs={{0,1},{1,0},{2,3},{3,2},{4,5},{5,4},{6,7},{7,6},{8,9},{9,8},{10,11... | collective-permute-start | bytes 9437192 | tf_op jit(solution)/shard_map/ppermute | solution.py:40
  4.1 26.1 %collective-permute-start.12 = (bf16[1,2048,768]{2,1,0:T(8,128)(2,1)}, bf16[1,2048,768]{2,1,0:T(8,128)(2,1)S(1)}, u32[]{:S(2)}, u32[]{:S(2)}) collective-permute-start(bf16[1,2048,768]{2,1,0:T(8,128)(2,1)} %refs_5_.3), channel_id=1, source_target_pairs={{0,1},{1,0},{2,3},{3,2},{4,5},{5,4},{6,7},{7,6},{8,9},{9,8},{10,11... | collective-permute-start | bytes 9437192 | tf_op jit(solution)/shard_map/ppermute | solution.py:40
  4.9 5.3 %collective-permute-start.2 = (bf16[64,1024]{1,0:T(8,128)(2,1)S(1)}, bf16[64,1024]{1,0:T(8,128)(2,1)S(1)}, u32[]{:S(2)}, u32[]{:S(2)}) collective-permute-start(bf16[64,1024]{1,0:T(8,128)(2,1)S(1)} %get-tuple-element.37), channel_id=1, source_target_pairs={{0,3},{1,4},{2,7},{3,0},{4,1},{5,6},{6,5},{7,2},{8,13},{9,10},{10,... | collective-permute-start | bytes 393224 | tf_op jit(solution)/shard_map/ppermute | solution.py:40
  7.9 22.3 %copy-start.1 = (bf16[1,2048,768]{2,1,0:T(8,128)(2,1)S(1)}, bf16[1,2048,768]{2,1,0:T(8,128)(2,1)}, u32[]{:S(2)}) copy-start(bf16[1,2048,768]{2,1,0:T(8,128)(2,1)} %refs_5_.3) | copy-start | bytes 9437188
  7.9 4.5 %collective-permute-start.1 = (bf16[64,1024]{1,0:T(8,128)(2,1)S(1)}, bf16[64,1024]{1,0:T(8,128)(2,1)S(1)}, u32[]{:S(2)}, u32[]{:S(2)}) collective-permute-start(bf16[64,1024]{1,0:T(8,128)(2,1)S(1)} %get-tuple-element.35), channel_id=1, source_target_pairs={{0,3},{1,4},{2,7},{3,0},{4,1},{5,6},{6,5},{7,2},{8,13},{9,10},{10,... | collective-permute-start | bytes 393224 | tf_op jit(solution)/shard_map/ppermute | solution.py:40
  10.3 4.1 %collective-permute-start.4 = (bf16[32,1024]{1,0:T(8,128)(2,1)S(1)}, bf16[32,1024]{1,0:T(8,128)(2,1)S(1)}, u32[]{:S(2)}, u32[]{:S(2)}) collective-permute-start(bf16[32,1024]{1,0:T(8,128)(2,1)S(1)} %slice.109), channel_id=1, source_target_pairs={{0,5},{1,2},{2,1},{3,6},{4,7},{5,0},{6,3},{7,4},{8,11},{9,12},{10,... | collective-permute-start | bytes 196616 | tf_op jit(solution)/shard_map/ppermute | solution.py:40
  12.5 4.5 %collective-permute-start.3 = (bf16[32,1024]{1,0:T(8,128)(2,1)S(1)}, bf16[32,1024]{1,0:T(8,128)(2,1)S(1)}, u32[]{:S(2)}, u32[]{:S(2)}) collective-permute-start(bf16[32,1024]{1,0:T(8,128)(2,1)S(1)} %slice.108), channel_id=1, source_target_pairs={{0,5},{1,2},{2,1},{3,6},{4,7},{5,0},{6,3},{7,4},{8,11},{9,12},{10,... | collective-permute-start | bytes 196616 | tf_op jit(solution)/shard_map/ppermute | solution.py:40
  14.4 6.8 %collective-permute-start.6 = (bf16[32,1152]{1,0:T(8,128)(2,1)S(1)}, bf16[32,1152]{1,0:T(8,128)(2,1)S(1)}, u32[]{:S(2)}, u32[]{:S(2)}) collective-permute-start(bf16[32,1152]{1,0:T(8,128)(2,1)S(1)} %fusion.2), channel_id=1, source_target_pairs={{0,9},{1,8},{2,11},{3,10},{4,13},{5,12},{6,15},{7,14},{8,1},{9,0},... | collective-permute-start | bytes 221192 | tf_op jit(solution)/shard_map/ppermute | solution.py:40
  16.9 7.1 %collective-permute-start.5 = (bf16[32,1024]{1,0:T(8,128)(2,1)S(1)}, bf16[32,1024]{1,0:T(8,128)(2,1)S(1)}, u32[]{:S(2)}, u32[]{:S(2)}) collective-permute-start(bf16[32,1024]{1,0:T(8,128)(2,1)S(1)} %fusion.3), channel_id=1, source_target_pairs={{0,9},{1,8},{2,11},{3,10},{4,13},{5,12},{6,15},{7,14},{8,1},{9,0},... | collective-permute-start | bytes 196616 | tf_op jit(solution)/shard_map/ppermute | solution.py:40
  21.3 4.3 %collective-permute-start.8 = (bf16[32,1152]{1,0:T(8,128)(2,1)S(1)}, bf16[32,1152]{1,0:T(8,128)(2,1)S(1)}, u32[]{:S(2)}, u32[]{:S(2)}) collective-permute-start(bf16[32,1152]{1,0:T(8,128)(2,1)S(1)} %fusion), channel_id=1, source_target_pairs={{0,5},{1,2},{2,1},{3,6},{4,7},{5,0},{6,3},{7,4},{8,11},{9,12},{10,... | collective-permute-start | bytes 221192 | tf_op jit(solution)/shard_map/ppermute | solution.py:40
  24.1 3.8 %collective-permute-start.7 = (bf16[32,1024]{1,0:T(8,128)(2,1)S(1)}, bf16[32,1024]{1,0:T(8,128)(2,1)S(1)}, u32[]{:S(2)}, u32[]{:S(2)}) collective-permute-start(bf16[32,1024]{1,0:T(8,128)(2,1)S(1)} %fusion.1), channel_id=1, source_target_pairs={{0,5},{1,2},{2,1},{3,6},{4,7},{5,0},{6,3},{7,4},{8,11},{9,12},{10,... | collective-permute-start | bytes 196616 | tf_op jit(solution)/shard_map/ppermute | solution.py:40
  25.5 4.6 %collective-permute-start.10 = (bf16[64,1152]{1,0:T(8,128)(2,1)S(1)}, bf16[64,1152]{1,0:T(8,128)(2,1)S(1)}, u32[]{:S(2)}, u32[]{:S(2)}) collective-permute-start(bf16[64,1152]{1,0:T(8,128)(2,1)S(1)} %pad_maximum_fusion.1.refs_0_.refs_2_), channel_id=1, source_target_pairs={{0,3},{1,4},{2,7},{3,0},{4,1},{5,6},{6,5},{7,2},{8,13},{9,10},{10,... | collective-permute-start | bytes 442376 | tf_op jit(solution)/shard_map/ppermute | solution.py:40
  27.8 4.5 %collective-permute-start.9 = (bf16[64,1024]{1,0:T(8,128)(2,1)S(1)}, bf16[64,1024]{1,0:T(8,128)(2,1)S(1)}, u32[]{:S(2)}, u32[]{:S(2)}) collective-permute-start(bf16[64,1024]{1,0:T(8,128)(2,1)S(1)} %pad_maximum_fusion.2.refs_0_), channel_id=1, source_target_pairs={{0,3},{1,4},{2,7},{3,0},{4,1},{5,6},{6,5},{7,2},{8,13},{9,10},{10,... | collective-permute-start | bytes 393224 | tf_op jit(solution)/shard_map/ppermute | solution.py:40
  33.8 4.5 %collective-permute-start.14 = (bf16[64,1024]{1,0:T(8,128)(2,1)S(1)}, bf16[64,1024]{1,0:T(8,128)(2,1)S(1)}, u32[]{:S(2)}, u32[]{:S(2)}) collective-permute-start(bf16[64,1024]{1,0:T(8,128)(2,1)S(1)} %get-tuple-element.49), channel_id=1, source_target_pairs={{0,3},{1,4},{2,7},{3,0},{4,1},{5,6},{6,5},{7,2},{8,13},{9,10},{10,... | collective-permute-start | bytes 393224 | tf_op jit(solution)/shard_map/ppermute | solution.py:40
  35.9 4.5 %collective-permute-start.17 = (bf16[64,1024]{1,0:T(8,128)(2,1)S(1)}, bf16[64,1024]{1,0:T(8,128)(2,1)S(1)}, u32[]{:S(2)}, u32[]{:S(2)}) collective-permute-start(bf16[64,1024]{1,0:T(8,128)(2,1)S(1)} %get-tuple-element.55), channel_id=1, source_target_pairs={{0,3},{1,4},{2,7},{3,0},{4,1},{5,6},{6,5},{7,2},{8,13},{9,10},{10,... | collective-permute-start | bytes 393224 | tf_op jit(solution)/shard_map/ppermute | solution.py:40
  38.3 3.8 %collective-permute-start.15 = (bf16[32,1024]{1,0:T(8,128)(2,1)S(1)}, bf16[32,1024]{1,0:T(8,128)(2,1)S(1)}, u32[]{:S(2)}, u32[]{:S(2)}) collective-permute-start(bf16[32,1024]{1,0:T(8,128)(2,1)S(1)} %slice.107), channel_id=1, source_target_pairs={{0,5},{1,2},{2,1},{3,6},{4,7},{5,0},{6,3},{7,4},{8,11},{9,12},{10,... | collective-permute-start | bytes 196616 | tf_op jit(solution)/shard_map/ppermute | solution.py:40
  40.4 4.7 %collective-permute-start.18 = (bf16[32,1024]{1,0:T(8,128)(2,1)S(1)}, bf16[32,1024]{1,0:T(8,128)(2,1)S(1)}, u32[]{:S(2)}, u32[]{:S(2)}) collective-permute-start(bf16[32,1024]{1,0:T(8,128)(2,1)S(1)} %slice.106), channel_id=1, source_target_pairs={{0,5},{1,2},{2,1},{3,6},{4,7},{5,0},{6,3},{7,4},{8,11},{9,12},{10,... | collective-permute-start | bytes 196616 | tf_op jit(solution)/shard_map/ppermute | solution.py:40
  42.1 5.0 %collective-permute-start.16 = (bf16[16,1024]{1,0:T(8,128)(2,1)S(1)}, bf16[16,1024]{1,0:T(8,128)(2,1)S(1)}, u32[]{:S(2)}, u32[]{:S(2)}) collective-permute-start(bf16[16,1024]{1,0:T(8,128)(2,1)S(1)} %slice.111), channel_id=1, source_target_pairs={{0,9},{1,8},{2,11},{3,10},{4,13},{5,12},{6,15},{7,14},{8,1},{9,0},... | collective-permute-start | bytes 98312 | tf_op jit(solution)/shard_map/ppermute | solution.py:40
  45.0 4.3 %collective-permute-start.19 = (bf16[16,1024]{1,0:T(8,128)(2,1)S(1)}, bf16[16,1024]{1,0:T(8,128)(2,1)S(1)}, u32[]{:S(2)}, u32[]{:S(2)}) collective-permute-start(bf16[16,1024]{1,0:T(8,128)(2,1)S(1)} %slice.110), channel_id=1, source_target_pairs={{0,9},{1,8},{2,11},{3,10},{4,13},{5,12},{6,15},{7,14},{8,1},{9,0},... | collective-permute-start | bytes 98312 | tf_op jit(solution)/shard_map/ppermute | solution.py:40
  49.4 1.3 %collective-permute-start.20 = (bf16[16,2048]{1,0:T(8,128)(2,1)S(1)}, bf16[16,2048]{1,0:T(8,128)(2,1)S(1)}, u32[]{:S(2)}, u32[]{:S(2)}) collective-permute-start(bf16[16,2048]{1,0:T(8,128)(2,1)S(1)} %pad_maximum_fusion.3), channel_id=1, source_target_pairs={{0,1},{1,0},{2,3},{3,2},{4,5},{5,4},{6,7},{7,6},{8,9},{9,8},{10,11... | collective-permute-start | bytes 196616 | tf_op jit(solution)/shard_map/ppermute | solution.py:40

commit v5 on v4

--- a/solution.py
+++ b/solution.py
@@ -85,12 +85,10 @@
 
 
 def attend_kernel(axis_width, *refs):
-    sources, (ordered, w_out, w_down), scratch = refs[:10], refs[10:13], refs[13:]
+    sources, (ordered, w_out), scratch = refs[:9], refs[9:11], refs[11:]
     *inputs, attended, sems = scratch
-    copies = started(sources, [*inputs, w_out, w_down], sems)
-    for copy in copies[:-2]:
-        copy.wait()
-    table, lengths, parents, expert_ids, gate_weights, queries, tree_kv, kv_cache = inputs
+    copies = started(sources, [*inputs, w_out], sems)
+    parents, table, lengths, expert_ids, gate_weights, queries, tree_kv, kv_cache = inputs
     seq_count, node_count = parents.shape
     head_dim = tree_kv.shape[-1]
     head_count = queries.shape[1] // head_dim
@@ -100,6 +98,7 @@
     query_count = head_count * node_count
     f32, bf16 = jnp.float32, jnp.bfloat16
 
+    copies[0].wait()
     lane = lax.broadcasted_iota(jnp.int32, (8, all_nodes), 1)
     shifted = [
         jnp.where(parents[s : s + 1, :] >= 0, parents[s : s + 1, :] + s * node_count, -1)
@@ -109,9 +108,12 @@
     above = jnp.where(above >= 0, above, lane)
     words = jnp.left_shift(1, lane % node_count)
     for repeat in range(max(node_count - 1, 1).bit_length()):
+        if repeat:
+            above = jnp.take_along_axis(above, above, axis=1)
         words = words | jnp.take_along_axis(words, above, axis=1)
-        above = jnp.take_along_axis(above, above, axis=1)
-
+
+    for copy in copies[1:-1]:
+        copy.wait()
     query_nodes = lax.broadcasted_iota(jnp.int32, (8, query_count), 1) % node_count
     node_rows = lax.broadcasted_iota(jnp.int32, (node_count, query_count), 0)
     positions = lax.broadcasted_iota(jnp.int32, (cached, query_count), 0)
@@ -170,8 +172,7 @@
         target = (device ^ jnp.where(device & 1 == 0, one, other)) // groups
         picked.append(attended[pl.ds(pl.multiple_of(target * block, block), block), :])
     ordered[:, : queries.shape[1]] = jnp.concatenate(picked, axis=0)
-    for copy in copies[-2:]:
-        copy.wait()
+    copies[-1].wait()
 
 
 def project_kernel(own_rows, cut, own, other, w_out, kept, sent, *extra):
@@ -212,22 +213,21 @@
 
 
 def attend(
-    queries, tree_kv, kv_cache, table, lengths, parents, w_out, w_down, expert_ids, gate_weights
+    queries, tree_kv, kv_cache, table, lengths, parents, w_out, expert_ids, gate_weights
 ):
     axis_width = lax.axis_size("wide")
     rows, width = queries.shape
-    given = [table, lengths, parents, expert_ids.T, gate_weights.T, queries, tree_kv, kv_cache, w_out, w_down]
-    spaces = [pltpu.SMEM] * 2 + [pltpu.VMEM] * 6
+    given = [parents, table, lengths, expert_ids.T, gate_weights.T, queries, tree_kv, kv_cache, w_out]
+    spaces = [pltpu.VMEM, pltpu.SMEM, pltpu.SMEM] + [pltpu.VMEM] * 5
     given = [pltpu.with_memory_space_constraint(x, pltpu.HBM) for x in given]
     return pl.pallas_call(
         functools.partial(attend_kernel, axis_width),
         out_shape=[
             pltpu.VMEM((rows, width + spare_width(axis_width)), jnp.bfloat16),
             pltpu.VMEM(w_out.shape, w_out.dtype),
-            pltpu.VMEM(w_down.shape, w_down.dtype),
         ],
         in_specs=[pl.BlockSpec(memory_space=pltpu.HBM)] * len(given),
-        out_specs=[pl.BlockSpec(memory_space=pltpu.VMEM)] * 3,
+        out_specs=[pl.BlockSpec(memory_space=pltpu.VMEM)] * 2,
         scratch_shapes=[space(x.shape, x.dtype) for space, x in zip(spaces, given)]
         + [pltpu.VMEM(queries.shape, jnp.bfloat16), pltpu.SemaphoreType.DMA((len(given),))],
         compiler_params=pltpu.CompilerParams(vmem_limit_bytes=16 * 1024 * 1024),
@@ -395,14 +395,14 @@
     axis_width = lax.axis_size("wide")
     routes = Routes(axis_width)
     owners = (0, 1)
-    own, fetched_out, fetched_down = attend(
-        queries, tree_kv, kv_cache, block_table, cache_lengths, parents, w_out, w_down,
-        expert_ids, gate_weights,
-    )
-    *halves, extra = project(own, exchange(own, routes.pair), fetched_out, expert_ids.shape[0])
+    own, fetched = attend(
+        queries, tree_kv, kv_cache, block_table, cache_lengths, parents, w_out, expert_ids,
+        gate_weights,
+    )
+    *halves, extra = project(own, exchange(own, routes.pair), fetched, expert_ids.shape[0])
     others = [exchange(x, routes.pair) for x in (w_gate, w_up, w_down)]
     feeds = [w_gate, w_up, *others[:2]]
-    downs = [fetched_down, others[2]]
+    downs = [w_down, others[2]]
     hidden = reduce_and_gather(halves, extra, routes)
     parts = [list(pair) for pair in experts(hidden, owners, feeds, downs)]
     for route in routes.groups[::-1] + routes.steps[:-1]:

time: 51.5 us -> 51 us (level)
    pallas_call x1, Pallas kernels: 2.98 us -> 2.39 us  [attend(): pl.pallas_call(functools.partial(attend_kernel, axis_width), out_shape=[p...]
where the time goes in v5:
time: 51 us; the launch traced here: 50.9 us
  starting transfers between devices  28 us (55%)
  waiting for transfers between devices  15.4 us (30%)
  Pallas kernels  6.24 us (12%)
  other arithmetic  0.94 us (2%)
    ppermute x21, starting transfers between devices, exchange(): return lax.ppermute(block, 'wide', [(i, route(i)) for i in range(count)])  28 us
    ppermute x21, waiting for transfers between devices, exchange(): return lax.ppermute(block, 'wide', [(i, route(i)) for i in range(count)])  15.4 us
    pallas_call x5, Pallas kernels, local_call(): pl.pallas_call(kernel, out_shape=out_shape, in_specs=[pl.BlockSpec(memory...  3.85 us
    pallas_call x1, Pallas kernels, attend(): pl.pallas_call(functools.partial(attend_kernel, axis_width), out_shape=[p...  2.39 us
  transfers between devices with their start and end apart: 21, of which 14 were waited for; matrix products, arithmetic and copies ran while one was open for 1% of the time, Pallas kernels for 4%

profile of v5, /device:TPU:0, one launch (start us, length us, event | category | flops | bytes accessed | tf_op | source)
XLA Modules:
  0.0 50.9 jit_solution(3764065263565252779)
XLA Ops:
  0.0 2.4 %attend.1 = (bf16[128,640]{1,0:T(8,128)(2,1)S(1)}, bf16[512,2048]{1,0:T(8,128)(2,1)S(1)}) custom-call(s32[4,32]{1,0:T(4,128)} %refs_0_.1, s32[4,4]{1,0:T(4,128)} %refs_1_.1, s32[1,4]{1,0:T(1,128)} %refs_2_.2, s32[8,16]{1,0:T(8,128)} %bitcast.2, f32[8,16]{1,0:T(8,128)} %bitcast.3, bf16[128,512]{1,0:T(8,128)(2,1)} %refs_5_.2, bf16[2,128,128]{2,1,0:T(8,128)(2,1)} %refs_6_.1, ...), custom_call_target="tpu_custom_call" | custom-call | tf_op jit(solution)/shard_map/attend/pallas_call | solution.py:223
  4.3 2.7 %collective-permute-start.2 = (bf16[64,1024]{1,0:T(8,128)(2,1)S(1)}, bf16[64,1024]{1,0:T(8,128)(2,1)S(1)}, u32[]{:S(2)}, u32[]{:S(2)}) collective-permute-start(bf16[64,1024]{1,0:T(8,128)(2,1)S(1)} %get-tuple-element.36), channel_id=1, source_target_pairs={{0,3},{1,4},{2,7},{3,0},{4,1},{5,6},{6,5},{7,2},{8,13},{9,10},{10,... | collective-permute-start | bytes 393224 | tf_op jit(solution)/shard_map/ppermute | solution.py:40
  7.4 2.2 %collective-permute-done.2 = bf16[64,1024]{1,0:T(8,128)(2,1)S(1)} collective-permute-done((bf16[64,1024]{1,0:T(8,128)(2,1)S(1)}, bf16[64,1024]{1,0:T(8,128)(2,1)S(1)}, u32[]{:S(2)}, u32[]{:S(2)}) %collective-permute-start.2) | collective-permute-done | bytes 131104 | tf_op jit(solution)/shard_map/ppermute | solution.py:40
  9.7 2.2 %collective-permute-start.4 = (bf16[32,1024]{1,0:T(8,128)(2,1)S(1)}, bf16[32,1024]{1,0:T(8,128)(2,1)S(1)}, u32[]{:S(2)}, u32[]{:S(2)}) collective-permute-start(bf16[32,1024]{1,0:T(8,128)(2,1)S(1)} %slice.109), channel_id=1, source_target_pairs={{0,5},{1,2},{2,1},{3,6},{4,7},{5,0},{6,3},{7,4},{8,11},{9,12},{10,... | collective-permute-start | bytes 196616 | tf_op jit(solution)/shard_map/ppermute | solution.py:40
  11.9 1.5 %collective-permute-start.3 = (bf16[32,1024]{1,0:T(8,128)(2,1)S(1)}, bf16[32,1024]{1,0:T(8,128)(2,1)S(1)}, u32[]{:S(2)}, u32[]{:S(2)}) collective-permute-start(bf16[32,1024]{1,0:T(8,128)(2,1)S(1)} %slice.108), channel_id=1, source_target_pairs={{0,5},{1,2},{2,1},{3,6},{4,7},{5,0},{6,3},{7,4},{8,11},{9,12},{10,... | collective-permute-start | bytes 196616 | tf_op jit(solution)/shard_map/ppermute | solution.py:40
  13.8 2.5 %collective-permute-start.6 = (bf16[32,1152]{1,0:T(8,128)(2,1)S(1)}, bf16[32,1152]{1,0:T(8,128)(2,1)S(1)}, u32[]{:S(2)}, u32[]{:S(2)}) collective-permute-start(bf16[32,1152]{1,0:T(8,128)(2,1)S(1)} %fusion.2), channel_id=1, source_target_pairs={{0,9},{1,8},{2,11},{3,10},{4,13},{5,12},{6,15},{7,14},{8,1},{9,0},... | collective-permute-start | bytes 221192 | tf_op jit(solution)/shard_map/ppermute | solution.py:40
  16.4 1.9 %collective-permute-start.5 = (bf16[32,1024]{1,0:T(8,128)(2,1)S(1)}, bf16[32,1024]{1,0:T(8,128)(2,1)S(1)}, u32[]{:S(2)}, u32[]{:S(2)}) collective-permute-start(bf16[32,1024]{1,0:T(8,128)(2,1)S(1)} %fusion.3), channel_id=1, source_target_pairs={{0,9},{1,8},{2,11},{3,10},{4,13},{5,12},{6,15},{7,14},{8,1},{9,0},... | collective-permute-start | bytes 196616 | tf_op jit(solution)/shard_map/ppermute | solution.py:40
  18.2 2.4 %collective-permute-done.6 = bf16[32,1152]{1,0:T(8,128)(2,1)S(1)} collective-permute-done((bf16[32,1152]{1,0:T(8,128)(2,1)S(1)}, bf16[32,1152]{1,0:T(8,128)(2,1)S(1)}, u32[]{:S(2)}, u32[]{:S(2)}) %collective-permute-start.6) | collective-permute-done | bytes 73760 | tf_op jit(solution)/shard_map/ppermute | solution.py:40
  20.7 2.2 %collective-permute-start.8 = (bf16[32,1152]{1,0:T(8,128)(2,1)S(1)}, bf16[32,1152]{1,0:T(8,128)(2,1)S(1)}, u32[]{:S(2)}, u32[]{:S(2)}) collective-permute-start(bf16[32,1152]{1,0:T(8,128)(2,1)S(1)} %fusion), channel_id=1, source_target_pairs={{0,5},{1,2},{2,1},{3,6},{4,7},{5,0},{6,3},{7,4},{8,11},{9,12},{10,... | collective-permute-start | bytes 221192 | tf_op jit(solution)/shard_map/ppermute | solution.py:40
  23.5 0.8 %collective-permute-start.7 = (bf16[32,1024]{1,0:T(8,128)(2,1)S(1)}, bf16[32,1024]{1,0:T(8,128)(2,1)S(1)}, u32[]{:S(2)}, u32[]{:S(2)}) collective-permute-start(bf16[32,1024]{1,0:T(8,128)(2,1)S(1)} %fusion.1), channel_id=1, source_target_pairs={{0,5},{1,2},{2,1},{3,6},{4,7},{5,0},{6,3},{7,4},{8,11},{9,12},{10,... | collective-permute-start | bytes 196616 | tf_op jit(solution)/shard_map/ppermute | solution.py:40
  24.9 1.7 %collective-permute-start.10 = (bf16[64,1152]{1,0:T(8,128)(2,1)S(1)}, bf16[64,1152]{1,0:T(8,128)(2,1)S(1)}, u32[]{:S(2)}, u32[]{:S(2)}) collective-permute-start(bf16[64,1152]{1,0:T(8,128)(2,1)S(1)} %pad_maximum_fusion.1.refs_0_.refs_2_), channel_id=1, source_target_pairs={{0,3},{1,4},{2,7},{3,0},{4,1},{5,6},{6,5},{7,2},{8,13},{9,10},{10,... | collective-permute-start | bytes 442376 | tf_op jit(solution)/shard_map/ppermute | solution.py:40
  27.3 1.4 %collective-permute-start.9 = (bf16[64,1024]{1,0:T(8,128)(2,1)S(1)}, bf16[64,1024]{1,0:T(8,128)(2,1)S(1)}, u32[]{:S(2)}, u32[]{:S(2)}) collective-permute-start(bf16[64,1024]{1,0:T(8,128)(2,1)S(1)} %pad_maximum_fusion.2.refs_0_), channel_id=1, source_target_pairs={{0,3},{1,4},{2,7},{3,0},{4,1},{5,6},{6,5},{7,2},{8,13},{9,10},{10,... | collective-permute-start | bytes 393224 | tf_op jit(solution)/shard_map/ppermute | solution.py:40
  28.7 0.9 %collective-permute-done.10.refs_1_.refs_3_ = bf16[64,1152]{1,0:T(8,128)(2,1)S(1)} collective-permute-done((bf16[64,1152]{1,0:T(8,128)(2,1)S(1)}, bf16[64,1152]{1,0:T(8,128)(2,1)S(1)}, u32[]{:S(2)}, u32[]{:S(2)}) %collective-permute-start.10) | collective-permute-done | bytes 147488 | tf_op jit(solution)/shard_map/ppermute | solution.py:40
  29.6 1.0 %feed.1 = (f32[128,768]{1,0:T(8,128)S(1)}, f32[128,768]{1,0:T(8,128)S(1)}, f32[128,768]{1,0:T(8,128)S(1)}, f32[128,768]{1,0:T(8,128)S(1)}) custom-call(bf16[64,1152]{1,0:T(8,128)(2,1)S(1)} %pad_maximum_fusion.1.refs_0_.refs_2_, bf16[64,1152]{1,0:T(8,128)(2,1)S(1)} %collective-permute-done.10.refs_1_.refs_3_, bf16[1,2048,768]{2,1,0:T(8,128)(2,1)S(1)} %copy-done, ...), custom_call_target="tpu_custom_call" | custom-call | tf_op jit(solution)/shard_map/feed/pallas_call | solution.py:302
  30.6 1.1 %collective-permute-done.9.refs_1_ = bf16[64,1024]{1,0:T(8,128)(2,1)S(1)} collective-permute-done((bf16[64,1024]{1,0:T(8,128)(2,1)S(1)}, bf16[64,1024]{1,0:T(8,128)(2,1)S(1)}, u32[]{:S(2)}, u32[]{:S(2)}) %collective-permute-start.9) | collective-permute-done | bytes 131104 | tf_op jit(solution)/shard_map/ppermute | solution.py:40
  31.8 1.6 %finish.1 = (f32[64,1024]{1,0:T(8,128)S(1)}, bf16[64,1024]{1,0:T(8,128)(2,1)S(1)}, bf16[128,768]{1,0:T(8,128)(2,1)S(1)}, bf16[128,768]{1,0:T(8,128)(2,1)S(1)}, f...) custom-call(bf16[64,1024]{1,0:T(8,128)(2,1)S(1)} %pad_maximum_fusion.2.refs_0_, ...), custom_call_target="tpu_custom_call" | custom-call | tf_op jit(solution)/shard_map/finish/pallas_call | solution.py:302
  33.4 1.4 %collective-permute-start.14 = (bf16[64,1024]{1,0:T(8,128)(2,1)S(1)}, bf16[64,1024]{1,0:T(8,128)(2,1)S(1)}, u32[]{:S(2)}, u32[]{:S(2)}) collective-permute-start(bf16[64,1024]{1,0:T(8,128)(2,1)S(1)} %get-tuple-element.47), channel_id=1, source_target_pairs={{0,3},{1,4},{2,7},{3,0},{4,1},{5,6},{6,5},{7,2},{8,13},{9,10},{10,... | collective-permute-start | bytes 393224 | tf_op jit(solution)/shard_map/ppermute | solution.py:40
  35.9 2.0 %collective-permute-done.14 = bf16[64,1024]{1,0:T(8,128)(2,1)S(1)} collective-permute-done((bf16[64,1024]{1,0:T(8,128)(2,1)S(1)}, bf16[64,1024]{1,0:T(8,128)(2,1)S(1)}, u32[]{:S(2)}, u32[]{:S(2)}) %collective-permute-start.14) | collective-permute-done | bytes 131104 | tf_op jit(solution)/shard_map/ppermute | solution.py:40
  37.9 1.5 %collective-permute-start.15 = (bf16[32,1024]{1,0:T(8,128)(2,1)S(1)}, bf16[32,1024]{1,0:T(8,128)(2,1)S(1)}, u32[]{:S(2)}, u32[]{:S(2)}) collective-permute-start(bf16[32,1024]{1,0:T(8,128)(2,1)S(1)} %slice.107), channel_id=1, source_target_pairs={{0,5},{1,2},{2,1},{3,6},{4,7},{5,0},{6,3},{7,4},{8,11},{9,12},{10,... | collective-permute-start | bytes 196616 | tf_op jit(solution)/shard_map/ppermute | solution.py:40
  39.9 1.3 %collective-permute-start.18 = (bf16[32,1024]{1,0:T(8,128)(2,1)S(1)}, bf16[32,1024]{1,0:T(8,128)(2,1)S(1)}, u32[]{:S(2)}, u32[]{:S(2)}) collective-permute-start(bf16[32,1024]{1,0:T(8,128)(2,1)S(1)} %slice.106), channel_id=1, source_target_pairs={{0,5},{1,2},{2,1},{3,6},{4,7},{5,0},{6,3},{7,4},{8,11},{9,12},{10,... | collective-permute-start | bytes 196616 | tf_op jit(solution)/shard_map/ppermute | solution.py:40
  41.7 2.9 %collective-permute-start.16 = (bf16[16,1024]{1,0:T(8,128)(2,1)S(1)}, bf16[16,1024]{1,0:T(8,128)(2,1)S(1)}, u32[]{:S(2)}, u32[]{:S(2)}) collective-permute-start(bf16[16,1024]{1,0:T(8,128)(2,1)S(1)} %slice.111), channel_id=1, source_target_pairs={{0,9},{1,8},{2,11},{3,10},{4,13},{5,12},{6,15},{7,14},{8,1},{9,0},... | collective-permute-start | bytes 98312 | tf_op jit(solution)/shard_map/ppermute | solution.py:40
  44.6 2.0 %collective-permute-start.19 = (bf16[16,1024]{1,0:T(8,128)(2,1)S(1)}, bf16[16,1024]{1,0:T(8,128)(2,1)S(1)}, u32[]{:S(2)}, u32[]{:S(2)}) collective-permute-start(bf16[16,1024]{1,0:T(8,128)(2,1)S(1)} %slice.110), channel_id=1, source_target_pairs={{0,9},{1,8},{2,11},{3,10},{4,13},{5,12},{6,15},{7,14},{8,1},{9,0},... | collective-permute-start | bytes 98312 | tf_op jit(solution)/shard_map/ppermute | solution.py:40
  46.6 2.3 %collective-permute-done.19 = bf16[16,1024]{1,0:T(8,128)(2,1)S(1)} collective-permute-done((bf16[16,1024]{1,0:T(8,128)(2,1)S(1)}, bf16[16,1024]{1,0:T(8,128)(2,1)S(1)}, u32[]{:S(2)}, u32[]{:S(2)}) %collective-permute-start.19) | collective-permute-done | bytes 32800 | tf_op jit(solution)/shard_map/ppermute | solution.py:40
  49.2 1.0 %collective-permute-done.20 = bf16[16,2048]{1,0:T(8,128)(2,1)S(1)} collective-permute-done((bf16[16,2048]{1,0:T(8,128)(2,1)S(1)}, bf16[16,2048]{1,0:T(8,128)(2,1)S(1)}, u32[]{:S(2)}, u32[]{:S(2)}) %collective-permute-start.20) | collective-permute-done | bytes 65568 | tf_op jit(solution)/shard_map/ppermute | solution.py:40
  (56 shorter events, 7.8 us)
Async XLA Ops:
  2.4 1.5 %collective-permute-start = (bf16[128,640]{1,0:T(8,128)(2,1)S(1)}, bf16[128,640]{1,0:T(8,128)(2,1)S(1)}, u32[]{:S(2)}, u32[]{:S(2)}) collective-permute-start(bf16[128,640]{1,0:T(8,128)(2,1)S(1)} %get-tuple-element.31.own), channel_id=1, source_target_pairs={{0,1},{1,0},{2,3},{3,2},{4,5},{5,4},{6,7},{7,6},{8,9},{9,8},{10,11... | collective-permute-start | bytes 491528 | tf_op jit(solution)/shard_map/ppermute | solution.py:40
  2.9 26.7 %collective-permute-start.11 = (bf16[1,2048,768]{2,1,0:T(8,128)(2,1)}, bf16[1,2048,768]{2,1,0:T(8,128)(2,1)S(1)}, u32[]{:S(2)}, u32[]{:S(2)}) collective-permute-start(bf16[1,2048,768]{2,1,0:T(8,128)(2,1)} %refs_4_.2), channel_id=1, source_target_pairs={{0,1},{1,0},{2,3},{3,2},{4,5},{5,4},{6,7},{7,6},{8,9},{9,8},{10,11... | collective-permute-start | bytes 9437192 | tf_op jit(solution)/shard_map/ppermute | solution.py:40
  3.0 26.6 %collective-permute-start.12 = (bf16[1,2048,768]{2,1,0:T(8,128)(2,1)}, bf16[1,2048,768]{2,1,0:T(8,128)(2,1)S(1)}, u32[]{:S(2)}, u32[]{:S(2)}) collective-permute-start(bf16[1,2048,768]{2,1,0:T(8,128)(2,1)} %refs_5_.3), channel_id=1, source_target_pairs={{0,1},{1,0},{2,3},{3,2},{4,5},{5,4},{6,7},{7,6},{8,9},{9,8},{10,11... | collective-permute-start | bytes 9437192 | tf_op jit(solution)/shard_map/ppermute | solution.py:40
  3.4 28.3 %collective-permute-start.13 = (bf16[1,768,2048]{2,1,0:T(8,128)(2,1)}, bf16[1,768,2048]{2,1,0:T(8,128)(2,1)S(1)}, u32[]{:S(2)}, u32[]{:S(2)}) collective-permute-start(bf16[1,768,2048]{2,1,0:T(8,128)(2,1)} %refs_4_.3), channel_id=1, source_target_pairs={{0,1},{1,0},{2,3},{3,2},{4,5},{5,4},{6,7},{7,6},{8,9},{9,8},{10,11... | collective-permute-start | bytes 9437192 | tf_op jit(solution)/shard_map/ppermute | solution.py:40
  4.3 5.3 %collective-permute-start.2 = (bf16[64,1024]{1,0:T(8,128)(2,1)S(1)}, bf16[64,1024]{1,0:T(8,128)(2,1)S(1)}, u32[]{:S(2)}, u32[]{:S(2)}) collective-permute-start(bf16[64,1024]{1,0:T(8,128)(2,1)S(1)} %get-tuple-element.36), channel_id=1, source_target_pairs={{0,3},{1,4},{2,7},{3,0},{4,1},{5,6},{6,5},{7,2},{8,13},{9,10},{10,... | collective-permute-start | bytes 393224 | tf_op jit(solution)/shard_map/ppermute | solution.py:40
  7.0 22.6 %copy-start.1 = (bf16[1,2048,768]{2,1,0:T(8,128)(2,1)S(1)}, bf16[1,2048,768]{2,1,0:T(8,128)(2,1)}, u32[]{:S(2)}) copy-start(bf16[1,2048,768]{2,1,0:T(8,128)(2,1)} %refs_5_.3) | copy-start | bytes 9437188
  7.3 22.3 %copy-start = (bf16[1,2048,768]{2,1,0:T(8,128)(2,1)S(1)}, bf16[1,2048,768]{2,1,0:T(8,128)(2,1)}, u32[]{:S(2)}) copy-start(bf16[1,2048,768]{2,1,0:T(8,128)(2,1)} %refs_4_.2) | copy-start | bytes 9437188
  7.3 4.5 %collective-permute-start.1 = (bf16[64,1024]{1,0:T(8,128)(2,1)S(1)}, bf16[64,1024]{1,0:T(8,128)(2,1)S(1)}, u32[]{:S(2)}, u32[]{:S(2)}) collective-permute-start(bf16[64,1024]{1,0:T(8,128)(2,1)S(1)} %get-tuple-element.34), channel_id=1, source_target_pairs={{0,3},{1,4},{2,7},{3,0},{4,1},{5,6},{6,5},{7,2},{8,13},{9,10},{10,... | collective-permute-start | bytes 393224 | tf_op jit(solution)/shard_map/ppermute | solution.py:40
  9.7 4.1 %collective-permute-start.4 = (bf16[32,1024]{1,0:T(8,128)(2,1)S(1)}, bf16[32,1024]{1,0:T(8,128)(2,1)S(1)}, u32[]{:S(2)}, u32[]{:S(2)}) collective-permute-start(bf16[32,1024]{1,0:T(8,128)(2,1)S(1)} %slice.109), channel_id=1, source_target_pairs={{0,5},{1,2},{2,1},{3,6},{4,7},{5,0},{6,3},{7,4},{8,11},{9,12},{10,... | collective-permute-start | bytes 196616 | tf_op jit(solution)/shard_map/ppermute | solution.py:40
  11.9 4.5 %collective-permute-start.3 = (bf16[32,1024]{1,0:T(8,128)(2,1)S(1)}, bf16[32,1024]{1,0:T(8,128)(2,1)S(1)}, u32[]{:S(2)}, u32[]{:S(2)}) collective-permute-start(bf16[32,1024]{1,0:T(8,128)(2,1)S(1)} %slice.108), channel_id=1, source_target_pairs={{0,5},{1,2},{2,1},{3,6},{4,7},{5,0},{6,3},{7,4},{8,11},{9,12},{10,... | collective-permute-start | bytes 196616 | tf_op jit(solution)/shard_map/ppermute | solution.py:40
  13.8 6.8 %collective-permute-start.6 = (bf16[32,1152]{1,0:T(8,128)(2,1)S(1)}, bf16[32,1152]{1,0:T(8,128)(2,1)S(1)}, u32[]{:S(2)}, u32[]{:S(2)}) collective-permute-start(bf16[32,1152]{1,0:T(8,128)(2,1)S(1)} %fusion.2), channel_id=1, source_target_pairs={{0,9},{1,8},{2,11},{3,10},{4,13},{5,12},{6,15},{7,14},{8,1},{9,0},... | collective-permute-start | bytes 221192 | tf_op jit(solution)/shard_map/ppermute | solution.py:40
  16.4 7.1 %collective-permute-start.5 = (bf16[32,1024]{1,0:T(8,128)(2,1)S(1)}, bf16[32,1024]{1,0:T(8,128)(2,1)S(1)}, u32[]{:S(2)}, u32[]{:S(2)}) collective-permute-start(bf16[32,1024]{1,0:T(8,128)(2,1)S(1)} %fusion.3), channel_id=1, source_target_pairs={{0,9},{1,8},{2,11},{3,10},{4,13},{5,12},{6,15},{7,14},{8,1},{9,0},... | collective-permute-start | bytes 196616 | tf_op jit(solution)/shard_map/ppermute | solution.py:40
  20.7 4.2 %collective-permute-start.8 = (bf16[32,1152]{1,0:T(8,128)(2,1)S(1)}, bf16[32,1152]{1,0:T(8,128)(2,1)S(1)}, u32[]{:S(2)}, u32[]{:S(2)}) collective-permute-start(bf16[32,1152]{1,0:T(8,128)(2,1)S(1)} %fusion), channel_id=1, source_target_pairs={{0,5},{1,2},{2,1},{3,6},{4,7},{5,0},{6,3},{7,4},{8,11},{9,12},{10,... | collective-permute-start | bytes 221192 | tf_op jit(solution)/shard_map/ppermute | solution.py:40
  23.5 3.8 %collective-permute-start.7 = (bf16[32,1024]{1,0:T(8,128)(2,1)S(1)}, bf16[32,1024]{1,0:T(8,128)(2,1)S(1)}, u32[]{:S(2)}, u32[]{:S(2)}) collective-permute-start(bf16[32,1024]{1,0:T(8,128)(2,1)S(1)} %fusion.1), channel_id=1, source_target_pairs={{0,5},{1,2},{2,1},{3,6},{4,7},{5,0},{6,3},{7,4},{8,11},{9,12},{10,... | collective-permute-start | bytes 196616 | tf_op jit(solution)/shard_map/ppermute | solution.py:40
  24.9 4.6 %collective-permute-start.10 = (bf16[64,1152]{1,0:T(8,128)(2,1)S(1)}, bf16[64,1152]{1,0:T(8,128)(2,1)S(1)}, u32[]{:S(2)}, u32[]{:S(2)}) collective-permute-start(bf16[64,1152]{1,0:T(8,128)(2,1)S(1)} %pad_maximum_fusion.1.refs_0_.refs_2_), channel_id=1, source_target_pairs={{0,3},{1,4},{2,7},{3,0},{4,1},{5,6},{6,5},{7,2},{8,13},{9,10},{10,... | collective-permute-start | bytes 442376 | tf_op jit(solution)/shard_map/ppermute | solution.py:40
  27.3 4.5 %copy-start.2 = (bf16[1,768,2048]{2,1,0:T(8,128)(2,1)S(1)}, bf16[1,768,2048]{2,1,0:T(8,128)(2,1)}, u32[]{:S(2)}) copy-start(bf16[1,768,2048]{2,1,0:T(8,128)(2,1)} %refs_4_.3) | copy-start | bytes 9437188
  27.3 4.5 %collective-permute-start.9 = (bf16[64,1024]{1,0:T(8,128)(2,1)S(1)}, bf16[64,1024]{1,0:T(8,128)(2,1)S(1)}, u32[]{:S(2)}, u32[]{:S(2)}) collective-permute-start(bf16[64,1024]{1,0:T(8,128)(2,1)S(1)} %pad_maximum_fusion.2.refs_0_), channel_id=1, source_target_pairs={{0,3},{1,4},{2,7},{3,0},{4,1},{5,6},{6,5},{7,2},{8,13},{9,10},{10,... | collective-permute-start | bytes 393224 | tf_op jit(solution)/shard_map/ppermute | solution.py:40
  33.4 4.5 %collective-permute-start.14 = (bf16[64,1024]{1,0:T(8,128)(2,1)S(1)}, bf16[64,1024]{1,0:T(8,128)(2,1)S(1)}, u32[]{:S(2)}, u32[]{:S(2)}) collective-permute-start(bf16[64,1024]{1,0:T(8,128)(2,1)S(1)} %get-tuple-element.47), channel_id=1, source_target_pairs={{0,3},{1,4},{2,7},{3,0},{4,1},{5,6},{6,5},{7,2},{8,13},{9,10},{10,... | collective-permute-start | bytes 393224 | tf_op jit(solution)/shard_map/ppermute | solution.py:40
  35.4 4.5 %collective-permute-start.17 = (bf16[64,1024]{1,0:T(8,128)(2,1)S(1)}, bf16[64,1024]{1,0:T(8,128)(2,1)S(1)}, u32[]{:S(2)}, u32[]{:S(2)}) collective-permute-start(bf16[64,1024]{1,0:T(8,128)(2,1)S(1)} %get-tuple-element.53), channel_id=1, source_target_pairs={{0,3},{1,4},{2,7},{3,0},{4,1},{5,6},{6,5},{7,2},{8,13},{9,10},{10,... | collective-permute-start | bytes 393224 | tf_op jit(solution)/shard_map/ppermute | solution.py:40
  37.9 3.8 %collective-permute-start.15 = (bf16[32,1024]{1,0:T(8,128)(2,1)S(1)}, bf16[32,1024]{1,0:T(8,128)(2,1)S(1)}, u32[]{:S(2)}, u32[]{:S(2)}) collective-permute-start(bf16[32,1024]{1,0:T(8,128)(2,1)S(1)} %slice.107), channel_id=1, source_target_pairs={{0,5},{1,2},{2,1},{3,6},{4,7},{5,0},{6,3},{7,4},{8,11},{9,12},{10,... | collective-permute-start | bytes 196616 | tf_op jit(solution)/shard_map/ppermute | solution.py:40
  39.9 4.7 %collective-permute-start.18 = (bf16[32,1024]{1,0:T(8,128)(2,1)S(1)}, bf16[32,1024]{1,0:T(8,128)(2,1)S(1)}, u32[]{:S(2)}, u32[]{:S(2)}) collective-permute-start(bf16[32,1024]{1,0:T(8,128)(2,1)S(1)} %slice.106), channel_id=1, source_target_pairs={{0,5},{1,2},{2,1},{3,6},{4,7},{5,0},{6,3},{7,4},{8,11},{9,12},{10,... | collective-permute-start | bytes 196616 | tf_op jit(solution)/shard_map/ppermute | solution.py:40
  41.7 4.9 %collective-permute-start.16 = (bf16[16,1024]{1,0:T(8,128)(2,1)S(1)}, bf16[16,1024]{1,0:T(8,128)(2,1)S(1)}, u32[]{:S(2)}, u32[]{:S(2)}) collective-permute-start(bf16[16,1024]{1,0:T(8,128)(2,1)S(1)} %slice.111), channel_id=1, source_target_pairs={{0,9},{1,8},{2,11},{3,10},{4,13},{5,12},{6,15},{7,14},{8,1},{9,0},... | collective-permute-start | bytes 98312 | tf_op jit(solution)/shard_map/ppermute | solution.py:40
  44.6 4.3 %collective-permute-start.19 = (bf16[16,1024]{1,0:T(8,128)(2,1)S(1)}, bf16[16,1024]{1,0:T(8,128)(2,1)S(1)}, u32[]{:S(2)}, u32[]{:S(2)}) collective-permute-start(bf16[16,1024]{1,0:T(8,128)(2,1)S(1)} %slice.110), channel_id=1, source_target_pairs={{0,9},{1,8},{2,11},{3,10},{4,13},{5,12},{6,15},{7,14},{8,1},{9,0},... | collective-permute-start | bytes 98312 | tf_op jit(solution)/shard_map/ppermute | solution.py:40
  48.9 1.3 %collective-permute-start.20 = (bf16[16,2048]{1,0:T(8,128)(2,1)S(1)}, bf16[16,2048]{1,0:T(8,128)(2,1)S(1)}, u32[]{:S(2)}, u32[]{:S(2)}) collective-permute-start(bf16[16,2048]{1,0:T(8,128)(2,1)S(1)} %pad_maximum_fusion.3), channel_id=1, source_target_pairs={{0,1},{1,0},{2,3},{3,2},{4,5},{5,4},{6,7},{7,6},{8,9},{9,8},{10,11... | collective-permute-start | bytes 196616 | tf_op jit(solution)/shard_map/ppermute | solution.py:40

commit v6 on v5

--- a/solution.py
+++ b/solution.py
@@ -31,8 +31,12 @@
 def slice_orders(axis_width):
     groups = axis_width // ATT_TP
     first = [groups << step for step in range(bits_of(ATT_TP))]
-    second = [first[1], first[0], *first[2:]]
-    return first, second
+    return [*first[1:], first[0]], first
+
+
+def return_orders(axis_width):
+    second, first = slice_orders(axis_width)
+    return [second[0], second[-1], *second[1:-1]], first
 
 
 def exchange(block, route):
@@ -54,11 +58,11 @@
         orders = slice_orders(axis_width)
         odd = lambda i: (i // groups).bit_count() & 1
         self.pair = lambda i: i ^ 1
-        self.steps = [
-            lambda i, step=step: i ^ orders[(i & 1) ^ odd(i)][step] ^ 1
-            for step in range(bits_of(ATT_TP))
+        steps = range(bits_of(ATT_TP))
+        self.steps, self.returns = [
+            [lambda i, order=order, k=k: i ^ order[(i & 1) ^ odd(i)][k] ^ 1 for k in steps]
+            for order in (orders, return_orders(axis_width))
         ]
-        self.last = lambda i: i ^ orders[(i & 1) ^ odd(i)][-1] ^ odd(i)
         self.groups = [lambda i, k=k: i ^ 1 << k for k in range(1, bits_of(groups))]
 
 
@@ -235,10 +239,24 @@
     )(*given)
 
 
-def feed_kernel(cut, tile, pairs, first, *refs):
+def arranged(halves, columns, axis_width):
+    rows = jnp.concatenate([half[:, columns] for half in halves], axis=0)
+    groups = axis_width // ATT_TP
+    block = rows.shape[0] // (groups // 2 * ATT_TP)
+    results = []
+    for order, other in zip(slice_orders(axis_width), return_orders(axis_width)):
+        masks = relative_masks(order)
+        places = [masks.index(mask) for mask in relative_masks(other)]
+        starts = [(k * ATT_TP + place) * block for k in range(groups // 2) for place in places]
+        results.append(jnp.concatenate([rows[x : x + block] for x in starts], axis=0))
+    role = (lax.axis_index("wide") & 1) ^ on_odd_chip().astype(jnp.int32)
+    return jnp.where(role == 0, results[0], results[1])
+
+
+def feed_kernel(axis_width, cut, tile, pairs, first, *refs):
     hidden, weights, refs = refs[:2], refs[2 : 2 + pairs], refs[2 + pairs :]
     before, after = (None, refs) if first else (refs[:pairs], refs[pairs:])
-    rows = jnp.concatenate([half[:, : cut[1] - cut[0]] for half in hidden], axis=0)
+    rows = arranged(hidden, slice(0, cut[1] - cut[0]), axis_width)
     for m in range(pairs):
         for n in range(weights[m].shape[2] // tile):
             columns = slice(n * tile, (n + 1) * tile)
@@ -257,8 +275,8 @@
     f32, bf16 = jnp.float32, jnp.bfloat16
     width = cut[1] - cut[0]
     device = lax.axis_index("wide")
-    rows = jnp.concatenate([half[:, :width] for half in hidden], axis=0)
-    parts = jnp.concatenate([half[:, -spare:] for half in carrier], axis=0)
+    rows = arranged(hidden, slice(0, width), axis_width)
+    parts = arranged(carrier, slice(-spare, None), axis_width)
     lane = lax.broadcasted_iota(jnp.int32, parts.shape, 1)
     piece = slice(*cut)
     for m, owner in enumerate(owners):
@@ -321,7 +339,7 @@
     wide = pltpu.VMEM((rows, hidden_width), jnp.float32)
     sums = []
     for c in range(CHUNKS - 1):
-        kernel = functools.partial(feed_kernel, cuts[c], tile, 2 * count, c == 0)
+        kernel = functools.partial(feed_kernel, axis_width, cuts[c], tile, 2 * count, c == 0)
         sums = local_call(kernel, "feed", [wide] * (2 * count), [*hidden[c], *feeds, *sums])
     kept, sent, *rest = local_call(
         functools.partial(finish_kernel, axis_width, spare, cuts[-1], cuts[0], tile, owners),
@@ -405,7 +423,7 @@
     downs = [w_down, others[2]]
     hidden = reduce_and_gather(halves, extra, routes)
     parts = [list(pair) for pair in experts(hidden, owners, feeds, downs)]
-    for route in routes.groups[::-1] + routes.steps[:-1]:
+    for route in routes.groups[::-1] + routes.returns[:-1]:
         earlier = None
         for part in parts:
             kept, sent = part
@@ -414,7 +432,7 @@
             earlier = part[1]
     results, earlier = [], None
     for kept, sent in parts:
-        other = ordered_after(exchange(sent, routes.steps[-1]), earlier).astype(jnp.float32)
+        other = ordered_after(exchange(sent, routes.returns[-1]), earlier).astype(jnp.float32)
         results.append((kept + other).astype(jnp.bfloat16))
         earlier = results[-1]
     result = jnp.concatenate(results, axis=1)

time: 51 us -> 50.5 us (level)
  starting transfers between devices: 28 us -> 26.8 us
  waiting for transfers between devices: 15.4 us -> 16 us
    ppermute x21, starting transfers between devices: 28 us -> 26.8 us  [exchange(): return lax.ppermute(block, 'wide', [(i, route(i)) for i in range(count)])]
    ppermute x21, waiting for transfers between devices: 15.4 us -> 16 us  [exchange(): return lax.ppermute(block, 'wide', [(i, route(i)) for i in range(count)])]
  transfers between devices with their start and end apart: 21 -> 21, of which waited for: 14 -> 15; matrix products, arithmetic and copies ran while one was open for 1% -> 1% of each run, Pallas kernels for 4% -> 4%
where the time goes in v6:
time: 50.5 us; the launch traced here: 50.3 us
  starting transfers between devices  26.8 us (53%)
  waiting for transfers between devices  16 us (32%)
  Pallas kernels  6.2 us (12%)
  other arithmetic  0.94 us (2%)
    ppermute x21, starting transfers between devices, exchange(): return lax.ppermute(block, 'wide', [(i, route(i)) for i in range(count)])  26.8 us
    ppermute x21, waiting for transfers between devices, exchange(): return lax.ppermute(block, 'wide', [(i, route(i)) for i in range(count)])  16 us
    pallas_call x5, Pallas kernels, local_call(): pl.pallas_call(kernel, out_shape=out_shape, in_specs=[pl.BlockSpec(memory...  3.81 us
    pallas_call x1, Pallas kernels, attend(): pl.pallas_call(functools.partial(attend_kernel, axis_width), out_shape=[p...  2.39 us
  transfers between devices with their start and end apart: 21, of which 15 were waited for; matrix products, arithmetic and copies ran while one was open for 1% of the time, Pallas kernels for 4%

profile of v6, /device:TPU:0, one launch (start us, length us, event | category | flops | bytes accessed | tf_op | source)
XLA Modules:
  0.0 50.3 jit_solution(2934194558276761537)
XLA Ops:
  0.0 2.4 %attend.1 = (bf16[128,640]{1,0:T(8,128)(2,1)S(1)}, bf16[512,2048]{1,0:T(8,128)(2,1)S(1)}) custom-call(s32[4,32]{1,0:T(4,128)} %refs_0_.1, s32[4,4]{1,0:T(4,128)} %refs_1_.1, s32[1,4]{1,0:T(1,128)} %refs_2_.2, s32[8,16]{1,0:T(8,128)} %bitcast.2, f32[8,16]{1,0:T(8,128)} %bitcast.3, bf16[128,512]{1,0:T(8,128)(2,1)} %refs_5_.2, bf16[2,128,128]{2,1,0:T(8,128)(2,1)} %refs_6_.1, ...), custom_call_target="tpu_custom_call" | custom-call | tf_op jit(solution)/shard_map/attend/pallas_call | solution.py:227
  4.3 2.7 %collective-permute-start.2 = (bf16[64,1024]{1,0:T(8,128)(2,1)S(1)}, bf16[64,1024]{1,0:T(8,128)(2,1)S(1)}, u32[]{:S(2)}, u32[]{:S(2)}) collective-permute-start(bf16[64,1024]{1,0:T(8,128)(2,1)S(1)} %get-tuple-element.36), channel_id=1, source_target_pairs={{0,5},{1,2},{2,1},{3,6},{4,7},{5,0},{6,3},{7,4},{8,11},{9,12},{10,... | collective-permute-start | bytes 393224 | tf_op jit(solution)/shard_map/ppermute | solution.py:44
  7.4 2.2 %collective-permute-done.2 = bf16[64,1024]{1,0:T(8,128)(2,1)S(1)} collective-permute-done((bf16[64,1024]{1,0:T(8,128)(2,1)S(1)}, bf16[64,1024]{1,0:T(8,128)(2,1)S(1)}, u32[]{:S(2)}, u32[]{:S(2)}) %collective-permute-start.2) | collective-permute-done | bytes 131104 | tf_op jit(solution)/shard_map/ppermute | solution.py:44
  9.7 3.1 %collective-permute-start.4 = (bf16[32,1024]{1,0:T(8,128)(2,1)S(1)}, bf16[32,1024]{1,0:T(8,128)(2,1)S(1)}, u32[]{:S(2)}, u32[]{:S(2)}) collective-permute-start(bf16[32,1024]{1,0:T(8,128)(2,1)S(1)} %slice.109), channel_id=1, source_target_pairs={{0,9},{1,4},{2,7},{3,10},{4,1},{5,12},{6,15},{7,2},{8,13},{9,0},{1... | collective-permute-start | bytes 196616 | tf_op jit(solution)/shard_map/ppermute | solution.py:44
  12.9 1.6 %collective-permute-start.3 = (bf16[32,1024]{1,0:T(8,128)(2,1)S(1)}, bf16[32,1024]{1,0:T(8,128)(2,1)S(1)}, u32[]{:S(2)}, u32[]{:S(2)}) collective-permute-start(bf16[32,1024]{1,0:T(8,128)(2,1)S(1)} %slice.108), channel_id=1, source_target_pairs={{0,9},{1,4},{2,7},{3,10},{4,1},{5,12},{6,15},{7,2},{8,13},{9,0},{1... | collective-permute-start | bytes 196616 | tf_op jit(solution)/shard_map/ppermute | solution.py:44
  15.3 1.8 %collective-permute-start.6 = (bf16[32,1152]{1,0:T(8,128)(2,1)S(1)}, bf16[32,1152]{1,0:T(8,128)(2,1)S(1)}, u32[]{:S(2)}, u32[]{:S(2)}) collective-permute-start(bf16[32,1152]{1,0:T(8,128)(2,1)S(1)} %fusion.2), channel_id=1, source_target_pairs={{0,3},{1,8},{2,11},{3,0},{4,13},{5,6},{6,5},{7,14},{8,1},{9,10},{1... | collective-permute-start | bytes 221192 | tf_op jit(solution)/shard_map/ppermute | solution.py:44
  17.6 1.3 %collective-permute-start.5 = (bf16[32,1024]{1,0:T(8,128)(2,1)S(1)}, bf16[32,1024]{1,0:T(8,128)(2,1)S(1)}, u32[]{:S(2)}, u32[]{:S(2)}) collective-permute-start(bf16[32,1024]{1,0:T(8,128)(2,1)S(1)} %fusion.3), channel_id=1, source_target_pairs={{0,3},{1,8},{2,11},{3,0},{4,13},{5,6},{6,5},{7,14},{8,1},{9,10},{1... | collective-permute-start | bytes 196616 | tf_op jit(solution)/shard_map/ppermute | solution.py:44
  19.2 3.2 %collective-permute-start.8 = (bf16[32,1152]{1,0:T(8,128)(2,1)S(1)}, bf16[32,1152]{1,0:T(8,128)(2,1)S(1)}, u32[]{:S(2)}, u32[]{:S(2)}) collective-permute-start(bf16[32,1152]{1,0:T(8,128)(2,1)S(1)} %fusion), channel_id=1, source_target_pairs={{0,9},{1,4},{2,7},{3,10},{4,1},{5,12},{6,15},{7,2},{8,13},{9,0},{1... | collective-permute-start | bytes 221192 | tf_op jit(solution)/shard_map/ppermute | solution.py:44
  23.3 1.2 %collective-permute-done.8 = bf16[32,1152]{1,0:T(8,128)(2,1)S(1)} collective-permute-done((bf16[32,1152]{1,0:T(8,128)(2,1)S(1)}, bf16[32,1152]{1,0:T(8,128)(2,1)S(1)}, u32[]{:S(2)}, u32[]{:S(2)}) %collective-permute-start.8) | collective-permute-done | bytes 73760 | tf_op jit(solution)/shard_map/ppermute | solution.py:44
  24.5 1.6 %collective-permute-start.10 = (bf16[64,1152]{1,0:T(8,128)(2,1)S(1)}, bf16[64,1152]{1,0:T(8,128)(2,1)S(1)}, u32[]{:S(2)}, u32[]{:S(2)}) collective-permute-start(bf16[64,1152]{1,0:T(8,128)(2,1)S(1)} %pad_maximum_fusion.1.refs_0_.refs_2_), channel_id=1, source_target_pairs={{0,5},{1,2},{2,1},{3,6},{4,7},{5,0},{6,3},{7,4},{8,11},{9,12},{10,... | collective-permute-start | bytes 442376 | tf_op jit(solution)/shard_map/ppermute | solution.py:44
  26.1 1.2 %collective-permute-done.7 = bf16[32,1024]{1,0:T(8,128)(2,1)S(1)} collective-permute-done((bf16[32,1024]{1,0:T(8,128)(2,1)S(1)}, bf16[32,1024]{1,0:T(8,128)(2,1)S(1)}, u32[]{:S(2)}, u32[]{:S(2)}) %collective-permute-start.7) | collective-permute-done | bytes 65568 | tf_op jit(solution)/shard_map/ppermute | solution.py:44
  29.2 1.0 %feed.1 = (f32[128,768]{1,0:T(8,128)S(1)}, f32[128,768]{1,0:T(8,128)S(1)}, f32[128,768]{1,0:T(8,128)S(1)}, f32[128,768]{1,0:T(8,128)S(1)}) custom-call(bf16[64,1152]{1,0:T(8,128)(2,1)S(1)} %pad_maximum_fusion.1.refs_0_.refs_2_, bf16[64,1152]{1,0:T(8,128)(2,1)S(1)} %collective-permute-done.10.refs_1_.refs_3_, bf16[1,2048,768]{2,1,0:T(8,128)(2,1)S(1)} %copy-done, ...), custom_call_target="tpu_custom_call" | custom-call | tf_op jit(solution)/shard_map/feed/pallas_call | solution.py:320
  30.2 1.6 %collective-permute-done.9.refs_1_ = bf16[64,1024]{1,0:T(8,128)(2,1)S(1)} collective-permute-done((bf16[64,1024]{1,0:T(8,128)(2,1)S(1)}, bf16[64,1024]{1,0:T(8,128)(2,1)S(1)}, u32[]{:S(2)}, u32[]{:S(2)}) %collective-permute-start.9) | collective-permute-done | bytes 131104 | tf_op jit(solution)/shard_map/ppermute | solution.py:44
  31.8 1.6 %finish.1 = (f32[64,1024]{1,0:T(8,128)S(1)}, bf16[64,1024]{1,0:T(8,128)(2,1)S(1)}, bf16[128,768]{1,0:T(8,128)(2,1)S(1)}, bf16[128,768]{1,0:T(8,128)(2,1)S(1)}, f...) custom-call(bf16[64,1024]{1,0:T(8,128)(2,1)S(1)} %pad_maximum_fusion.2.refs_0_, ...), custom_call_target="tpu_custom_call" | custom-call | tf_op jit(solution)/shard_map/finish/pallas_call | solution.py:320
  33.4 0.9 %collective-permute-start.14 = (bf16[64,1024]{1,0:T(8,128)(2,1)S(1)}, bf16[64,1024]{1,0:T(8,128)(2,1)S(1)}, u32[]{:S(2)}, u32[]{:S(2)}) collective-permute-start(bf16[64,1024]{1,0:T(8,128)(2,1)S(1)} %get-tuple-element.47), channel_id=1, source_target_pairs={{0,5},{1,2},{2,1},{3,6},{4,7},{5,0},{6,3},{7,4},{8,11},{9,12},{10,... | collective-permute-start | bytes 393224 | tf_op jit(solution)/shard_map/ppermute | solution.py:44
  34.9 1.0 %collective-permute-start.17 = (bf16[64,1024]{1,0:T(8,128)(2,1)S(1)}, bf16[64,1024]{1,0:T(8,128)(2,1)S(1)}, u32[]{:S(2)}, u32[]{:S(2)}) collective-permute-start(bf16[64,1024]{1,0:T(8,128)(2,1)S(1)} %get-tuple-element.53), channel_id=1, source_target_pairs={{0,5},{1,2},{2,1},{3,6},{4,7},{5,0},{6,3},{7,4},{8,11},{9,12},{10,... | collective-permute-start | bytes 393224 | tf_op jit(solution)/shard_map/ppermute | solution.py:44
  35.9 2.0 %collective-permute-done.14 = bf16[64,1024]{1,0:T(8,128)(2,1)S(1)} collective-permute-done((bf16[64,1024]{1,0:T(8,128)(2,1)S(1)}, bf16[64,1024]{1,0:T(8,128)(2,1)S(1)}, u32[]{:S(2)}, u32[]{:S(2)}) %collective-permute-start.14) | collective-permute-done | bytes 131104 | tf_op jit(solution)/shard_map/ppermute | solution.py:44
  37.9 1.2 %collective-permute-start.15 = (bf16[32,1024]{1,0:T(8,128)(2,1)S(1)}, bf16[32,1024]{1,0:T(8,128)(2,1)S(1)}, u32[]{:S(2)}, u32[]{:S(2)}) collective-permute-start(bf16[32,1024]{1,0:T(8,128)(2,1)S(1)} %slice.107), channel_id=1, source_target_pairs={{0,3},{1,4},{2,7},{3,0},{4,1},{5,6},{6,5},{7,2},{8,13},{9,10},{10,... | collective-permute-start | bytes 196616 | tf_op jit(solution)/shard_map/ppermute | solution.py:44
  39.4 2.3 %collective-permute-start.18 = (bf16[32,1024]{1,0:T(8,128)(2,1)S(1)}, bf16[32,1024]{1,0:T(8,128)(2,1)S(1)}, u32[]{:S(2)}, u32[]{:S(2)}) collective-permute-start(bf16[32,1024]{1,0:T(8,128)(2,1)S(1)} %slice.106), channel_id=1, source_target_pairs={{0,3},{1,4},{2,7},{3,0},{4,1},{5,6},{6,5},{7,2},{8,13},{9,10},{10,... | collective-permute-start | bytes 196616 | tf_op jit(solution)/shard_map/ppermute | solution.py:44
  41.8 1.5 %collective-permute-start.16 = (bf16[16,1024]{1,0:T(8,128)(2,1)S(1)}, bf16[16,1024]{1,0:T(8,128)(2,1)S(1)}, u32[]{:S(2)}, u32[]{:S(2)}) collective-permute-start(bf16[16,1024]{1,0:T(8,128)(2,1)S(1)} %slice.111), channel_id=1, source_target_pairs={{0,9},{1,8},{2,11},{3,10},{4,13},{5,12},{6,15},{7,14},{8,1},{9,0},... | collective-permute-start | bytes 98312 | tf_op jit(solution)/shard_map/ppermute | solution.py:44
  43.7 1.5 %collective-permute-start.19 = (bf16[16,1024]{1,0:T(8,128)(2,1)S(1)}, bf16[16,1024]{1,0:T(8,128)(2,1)S(1)}, u32[]{:S(2)}, u32[]{:S(2)}) collective-permute-start(bf16[16,1024]{1,0:T(8,128)(2,1)S(1)} %slice.110), channel_id=1, source_target_pairs={{0,9},{1,8},{2,11},{3,10},{4,13},{5,12},{6,15},{7,14},{8,1},{9,0},... | collective-permute-start | bytes 98312 | tf_op jit(solution)/shard_map/ppermute | solution.py:44
  45.3 1.4 %collective-permute-done.16 = bf16[16,1024]{1,0:T(8,128)(2,1)S(1)} collective-permute-done((bf16[16,1024]{1,0:T(8,128)(2,1)S(1)}, bf16[16,1024]{1,0:T(8,128)(2,1)S(1)}, u32[]{:S(2)}, u32[]{:S(2)}) %collective-permute-start.16) | collective-permute-done | bytes 32800 | tf_op jit(solution)/shard_map/ppermute | solution.py:44
  46.7 1.6 %collective-permute-done.19 = bf16[16,1024]{1,0:T(8,128)(2,1)S(1)} collective-permute-done((bf16[16,1024]{1,0:T(8,128)(2,1)S(1)}, bf16[16,1024]{1,0:T(8,128)(2,1)S(1)}, u32[]{:S(2)}, u32[]{:S(2)}) %collective-permute-start.19) | collective-permute-done | bytes 32800 | tf_op jit(solution)/shard_map/ppermute | solution.py:44
  48.4 1.2 %collective-permute-done.20 = bf16[16,2048]{1,0:T(8,128)(2,1)S(1)} collective-permute-done((bf16[16,2048]{1,0:T(8,128)(2,1)S(1)}, bf16[16,2048]{1,0:T(8,128)(2,1)S(1)}, u32[]{:S(2)}, u32[]{:S(2)}) %collective-permute-start.20) | collective-permute-done | bytes 65568 | tf_op jit(solution)/shard_map/ppermute | solution.py:44
  (56 shorter events, 8.8 us)
Async XLA Ops:
  2.4 1.5 %collective-permute-start = (bf16[128,640]{1,0:T(8,128)(2,1)S(1)}, bf16[128,640]{1,0:T(8,128)(2,1)S(1)}, u32[]{:S(2)}, u32[]{:S(2)}) collective-permute-start(bf16[128,640]{1,0:T(8,128)(2,1)S(1)} %get-tuple-element.31.own), channel_id=1, source_target_pairs={{0,1},{1,0},{2,3},{3,2},{4,5},{5,4},{6,7},{7,6},{8,9},{9,8},{10,11... | collective-permute-start | bytes 491528 | tf_op jit(solution)/shard_map/ppermute | solution.py:44
  2.9 26.2 %collective-permute-start.11 = (bf16[1,2048,768]{2,1,0:T(8,128)(2,1)}, bf16[1,2048,768]{2,1,0:T(8,128)(2,1)S(1)}, u32[]{:S(2)}, u32[]{:S(2)}) collective-permute-start(bf16[1,2048,768]{2,1,0:T(8,128)(2,1)} %refs_4_.2), channel_id=1, source_target_pairs={{0,1},{1,0},{2,3},{3,2},{4,5},{5,4},{6,7},{7,6},{8,9},{9,8},{10,11... | collective-permute-start | bytes 9437192 | tf_op jit(solution)/shard_map/ppermute | solution.py:44
  3.0 26.2 %collective-permute-start.12 = (bf16[1,2048,768]{2,1,0:T(8,128)(2,1)}, bf16[1,2048,768]{2,1,0:T(8,128)(2,1)S(1)}, u32[]{:S(2)}, u32[]{:S(2)}) collective-permute-start(bf16[1,2048,768]{2,1,0:T(8,128)(2,1)} %refs_5_.3), channel_id=1, source_target_pairs={{0,1},{1,0},{2,3},{3,2},{4,5},{5,4},{6,7},{7,6},{8,9},{9,8},{10,11... | collective-permute-start | bytes 9437192 | tf_op jit(solution)/shard_map/ppermute | solution.py:44
  3.4 28.4 %collective-permute-start.13 = (bf16[1,768,2048]{2,1,0:T(8,128)(2,1)}, bf16[1,768,2048]{2,1,0:T(8,128)(2,1)S(1)}, u32[]{:S(2)}, u32[]{:S(2)}) collective-permute-start(bf16[1,768,2048]{2,1,0:T(8,128)(2,1)} %refs_4_.3), channel_id=1, source_target_pairs={{0,1},{1,0},{2,3},{3,2},{4,5},{5,4},{6,7},{7,6},{8,9},{9,8},{10,11... | collective-permute-start | bytes 9437192 | tf_op jit(solution)/shard_map/ppermute | solution.py:44
  4.3 5.4 %collective-permute-start.2 = (bf16[64,1024]{1,0:T(8,128)(2,1)S(1)}, bf16[64,1024]{1,0:T(8,128)(2,1)S(1)}, u32[]{:S(2)}, u32[]{:S(2)}) collective-permute-start(bf16[64,1024]{1,0:T(8,128)(2,1)S(1)} %get-tuple-element.36), channel_id=1, source_target_pairs={{0,5},{1,2},{2,1},{3,6},{4,7},{5,0},{6,3},{7,4},{8,11},{9,12},{10,... | collective-permute-start | bytes 393224 | tf_op jit(solution)/shard_map/ppermute | solution.py:44
  7.0 22.2 %copy-start.1 = (bf16[1,2048,768]{2,1,0:T(8,128)(2,1)S(1)}, bf16[1,2048,768]{2,1,0:T(8,128)(2,1)}, u32[]{:S(2)}) copy-start(bf16[1,2048,768]{2,1,0:T(8,128)(2,1)} %refs_5_.3) | copy-start | bytes 9437188
  7.3 21.8 %copy-start = (bf16[1,2048,768]{2,1,0:T(8,128)(2,1)S(1)}, bf16[1,2048,768]{2,1,0:T(8,128)(2,1)}, u32[]{:S(2)}) copy-start(bf16[1,2048,768]{2,1,0:T(8,128)(2,1)} %refs_4_.2) | copy-start | bytes 9437188
  7.3 5.5 %collective-permute-start.1 = (bf16[64,1024]{1,0:T(8,128)(2,1)S(1)}, bf16[64,1024]{1,0:T(8,128)(2,1)S(1)}, u32[]{:S(2)}, u32[]{:S(2)}) collective-permute-start(bf16[64,1024]{1,0:T(8,128)(2,1)S(1)} %get-tuple-element.34), channel_id=1, source_target_pairs={{0,5},{1,2},{2,1},{3,6},{4,7},{5,0},{6,3},{7,4},{8,11},{9,12},{10,... | collective-permute-start | bytes 393224 | tf_op jit(solution)/shard_map/ppermute | solution.py:44
  9.7 5.6 %collective-permute-start.4 = (bf16[32,1024]{1,0:T(8,128)(2,1)S(1)}, bf16[32,1024]{1,0:T(8,128)(2,1)S(1)}, u32[]{:S(2)}, u32[]{:S(2)}) collective-permute-start(bf16[32,1024]{1,0:T(8,128)(2,1)S(1)} %slice.109), channel_id=1, source_target_pairs={{0,9},{1,4},{2,7},{3,10},{4,1},{5,12},{6,15},{7,2},{8,13},{9,0},{1... | collective-permute-start | bytes 196616 | tf_op jit(solution)/shard_map/ppermute | solution.py:44
  12.9 4.7 %collective-permute-start.3 = (bf16[32,1024]{1,0:T(8,128)(2,1)S(1)}, bf16[32,1024]{1,0:T(8,128)(2,1)S(1)}, u32[]{:S(2)}, u32[]{:S(2)}) collective-permute-start(bf16[32,1024]{1,0:T(8,128)(2,1)S(1)} %slice.108), channel_id=1, source_target_pairs={{0,9},{1,4},{2,7},{3,10},{4,1},{5,12},{6,15},{7,2},{8,13},{9,0},{1... | collective-permute-start | bytes 196616 | tf_op jit(solution)/shard_map/ppermute | solution.py:44
  15.3 3.8 %collective-permute-start.6 = (bf16[32,1152]{1,0:T(8,128)(2,1)S(1)}, bf16[32,1152]{1,0:T(8,128)(2,1)S(1)}, u32[]{:S(2)}, u32[]{:S(2)}) collective-permute-start(bf16[32,1152]{1,0:T(8,128)(2,1)S(1)} %fusion.2), channel_id=1, source_target_pairs={{0,3},{1,8},{2,11},{3,0},{4,13},{5,6},{6,5},{7,14},{8,1},{9,10},{1... | collective-permute-start | bytes 221192 | tf_op jit(solution)/shard_map/ppermute | solution.py:44
  17.6 4.8 %collective-permute-start.5 = (bf16[32,1024]{1,0:T(8,128)(2,1)S(1)}, bf16[32,1024]{1,0:T(8,128)(2,1)S(1)}, u32[]{:S(2)}, u32[]{:S(2)}) collective-permute-start(bf16[32,1024]{1,0:T(8,128)(2,1)S(1)} %fusion.3), channel_id=1, source_target_pairs={{0,3},{1,8},{2,11},{3,0},{4,13},{5,6},{6,5},{7,14},{8,1},{9,10},{1... | collective-permute-start | bytes 196616 | tf_op jit(solution)/shard_map/ppermute | solution.py:44
  19.2 5.3 %collective-permute-start.8 = (bf16[32,1152]{1,0:T(8,128)(2,1)S(1)}, bf16[32,1152]{1,0:T(8,128)(2,1)S(1)}, u32[]{:S(2)}, u32[]{:S(2)}) collective-permute-start(bf16[32,1152]{1,0:T(8,128)(2,1)S(1)} %fusion), channel_id=1, source_target_pairs={{0,9},{1,4},{2,7},{3,10},{4,1},{5,12},{6,15},{7,2},{8,13},{9,0},{1... | collective-permute-start | bytes 221192 | tf_op jit(solution)/shard_map/ppermute | solution.py:44
  22.4 4.9 %collective-permute-start.7 = (bf16[32,1024]{1,0:T(8,128)(2,1)S(1)}, bf16[32,1024]{1,0:T(8,128)(2,1)S(1)}, u32[]{:S(2)}, u32[]{:S(2)}) collective-permute-start(bf16[32,1024]{1,0:T(8,128)(2,1)S(1)} %fusion.1), channel_id=1, source_target_pairs={{0,9},{1,4},{2,7},{3,10},{4,1},{5,12},{6,15},{7,2},{8,13},{9,0},{1... | collective-permute-start | bytes 196616 | tf_op jit(solution)/shard_map/ppermute | solution.py:44
  24.5 4.6 %collective-permute-start.10 = (bf16[64,1152]{1,0:T(8,128)(2,1)S(1)}, bf16[64,1152]{1,0:T(8,128)(2,1)S(1)}, u32[]{:S(2)}, u32[]{:S(2)}) collective-permute-start(bf16[64,1152]{1,0:T(8,128)(2,1)S(1)} %pad_maximum_fusion.1.refs_0_.refs_2_), channel_id=1, source_target_pairs={{0,5},{1,2},{2,1},{3,6},{4,7},{5,0},{6,3},{7,4},{8,11},{9,12},{10,... | collective-permute-start | bytes 442376 | tf_op jit(solution)/shard_map/ppermute | solution.py:44
  27.4 4.5 %copy-start.2 = (bf16[1,768,2048]{2,1,0:T(8,128)(2,1)S(1)}, bf16[1,768,2048]{2,1,0:T(8,128)(2,1)}, u32[]{:S(2)}) copy-start(bf16[1,768,2048]{2,1,0:T(8,128)(2,1)} %refs_4_.3) | copy-start | bytes 9437188
  27.4 4.5 %collective-permute-start.9 = (bf16[64,1024]{1,0:T(8,128)(2,1)S(1)}, bf16[64,1024]{1,0:T(8,128)(2,1)S(1)}, u32[]{:S(2)}, u32[]{:S(2)}) collective-permute-start(bf16[64,1024]{1,0:T(8,128)(2,1)S(1)} %pad_maximum_fusion.2.refs_0_), channel_id=1, source_target_pairs={{0,5},{1,2},{2,1},{3,6},{4,7},{5,0},{6,3},{7,4},{8,11},{9,12},{10,... | collective-permute-start | bytes 393224 | tf_op jit(solution)/shard_map/ppermute | solution.py:44
  33.4 4.5 %collective-permute-start.14 = (bf16[64,1024]{1,0:T(8,128)(2,1)S(1)}, bf16[64,1024]{1,0:T(8,128)(2,1)S(1)}, u32[]{:S(2)}, u32[]{:S(2)}) collective-permute-start(bf16[64,1024]{1,0:T(8,128)(2,1)S(1)} %get-tuple-element.47), channel_id=1, source_target_pairs={{0,5},{1,2},{2,1},{3,6},{4,7},{5,0},{6,3},{7,4},{8,11},{9,12},{10,... | collective-permute-start | bytes 393224 | tf_op jit(solution)/shard_map/ppermute | solution.py:44
  34.9 4.5 %collective-permute-start.17 = (bf16[64,1024]{1,0:T(8,128)(2,1)S(1)}, bf16[64,1024]{1,0:T(8,128)(2,1)S(1)}, u32[]{:S(2)}, u32[]{:S(2)}) collective-permute-start(bf16[64,1024]{1,0:T(8,128)(2,1)S(1)} %get-tuple-element.53), channel_id=1, source_target_pairs={{0,5},{1,2},{2,1},{3,6},{4,7},{5,0},{6,3},{7,4},{8,11},{9,12},{10,... | collective-permute-start | bytes 393224 | tf_op jit(solution)/shard_map/ppermute | solution.py:44
  37.9 3.9 %collective-permute-start.15 = (bf16[32,1024]{1,0:T(8,128)(2,1)S(1)}, bf16[32,1024]{1,0:T(8,128)(2,1)S(1)}, u32[]{:S(2)}, u32[]{:S(2)}) collective-permute-start(bf16[32,1024]{1,0:T(8,128)(2,1)S(1)} %slice.107), channel_id=1, source_target_pairs={{0,3},{1,4},{2,7},{3,0},{4,1},{5,6},{6,5},{7,2},{8,13},{9,10},{10,... | collective-permute-start | bytes 196616 | tf_op jit(solution)/shard_map/ppermute | solution.py:44
  39.4 4.3 %collective-permute-start.18 = (bf16[32,1024]{1,0:T(8,128)(2,1)S(1)}, bf16[32,1024]{1,0:T(8,128)(2,1)S(1)}, u32[]{:S(2)}, u32[]{:S(2)}) collective-permute-start(bf16[32,1024]{1,0:T(8,128)(2,1)S(1)} %slice.106), channel_id=1, source_target_pairs={{0,3},{1,4},{2,7},{3,0},{4,1},{5,6},{6,5},{7,2},{8,13},{9,10},{10,... | collective-permute-start | bytes 196616 | tf_op jit(solution)/shard_map/ppermute | solution.py:44
  41.8 4.9 %collective-permute-start.16 = (bf16[16,1024]{1,0:T(8,128)(2,1)S(1)}, bf16[16,1024]{1,0:T(8,128)(2,1)S(1)}, u32[]{:S(2)}, u32[]{:S(2)}) collective-permute-start(bf16[16,1024]{1,0:T(8,128)(2,1)S(1)} %slice.111), channel_id=1, source_target_pairs={{0,9},{1,8},{2,11},{3,10},{4,13},{5,12},{6,15},{7,14},{8,1},{9,0},... | collective-permute-start | bytes 98312 | tf_op jit(solution)/shard_map/ppermute | solution.py:44
  43.7 4.6 %collective-permute-start.19 = (bf16[16,1024]{1,0:T(8,128)(2,1)S(1)}, bf16[16,1024]{1,0:T(8,128)(2,1)S(1)}, u32[]{:S(2)}, u32[]{:S(2)}) collective-permute-start(bf16[16,1024]{1,0:T(8,128)(2,1)S(1)} %slice.110), channel_id=1, source_target_pairs={{0,9},{1,8},{2,11},{3,10},{4,13},{5,12},{6,15},{7,14},{8,1},{9,0},... | collective-permute-start | bytes 98312 | tf_op jit(solution)/shard_map/ppermute | solution.py:44
  48.3 1.3 %collective-permute-start.20 = (bf16[16,2048]{1,0:T(8,128)(2,1)S(1)}, bf16[16,2048]{1,0:T(8,128)(2,1)S(1)}, u32[]{:S(2)}, u32[]{:S(2)}) collective-permute-start(bf16[16,2048]{1,0:T(8,128)(2,1)S(1)} %pad_maximum_fusion.3), channel_id=1, source_target_pairs={{0,1},{1,0},{2,3},{3,2},{4,5},{5,4},{6,7},{7,6},{8,9},{9,8},{10,11... | collective-permute-start | bytes 196616 | tf_op jit(solution)/shard_map/ppermute | solution.py:44

commit v7 on v6

--- a/solution.py
+++ b/solution.py
@@ -29,14 +29,13 @@
 
 
 def slice_orders(axis_width):
-    groups = axis_width // ATT_TP
-    first = [groups << step for step in range(bits_of(ATT_TP))]
-    return [*first[1:], first[0]], first
+    low, *rest, high = [axis_width // ATT_TP << step for step in range(bits_of(ATT_TP))]
+    return [*rest, high, low], [low, *rest, high]
 
 
 def return_orders(axis_width):
-    second, first = slice_orders(axis_width)
-    return [second[0], second[-1], *second[1:-1]], first
+    low, *rest, high = [axis_width // ATT_TP << step for step in range(bits_of(ATT_TP))]
+    return [*rest, low, high], [low, high, *rest]
 
 
 def exchange(block, route):

time: 50.5 us -> 50 us (0.990)
  waiting for transfers between devices: 16 us -> 15.2 us
    ppermute x21, waiting for transfers between devices: 16 us -> 15.2 us  [exchange(): return lax.ppermute(block, 'wide', [(i, route(i)) for i in range(count)])]
  transfers between devices with their start and end apart: 21 -> 21, of which waited for: 15 -> 15; matrix products, arithmetic and copies ran while one was open for 1% -> 1% of each run, Pallas kernels for 4% -> 5%
where the time goes in v7:
time: 50 us; the launch traced here: 49.8 us
  starting transfers between devices  27.1 us (54%)
  waiting for transfers between devices  15.2 us (30%)
  Pallas kernels  6.22 us (12%)
  other arithmetic  0.94 us (2%)
    ppermute x21, starting transfers between devices, exchange(): return lax.ppermute(block, 'wide', [(i, route(i)) for i in range(count)])  27.1 us
    ppermute x21, waiting for transfers between devices, exchange(): return lax.ppermute(block, 'wide', [(i, route(i)) for i in range(count)])  15.2 us
    pallas_call x5, Pallas kernels, local_call(): pl.pallas_call(kernel, out_shape=out_shape, in_specs=[pl.BlockSpec(memory...  3.83 us
    pallas_call x1, Pallas kernels, attend(): pl.pallas_call(functools.partial(attend_kernel, axis_width), out_shape=[p...  2.39 us
  transfers between devices with their start and end apart: 21, of which 15 were waited for; matrix products, arithmetic and copies ran while one was open for 1% of the time, Pallas kernels for 5%

profile of v7, /device:TPU:0, one launch (start us, length us, event | category | flops | bytes accessed | tf_op | source)
XLA Modules:
  0.0 49.8 jit_solution(11833684723809824623)
XLA Ops:
  0.0 2.4 %attend.1 = (bf16[128,640]{1,0:T(8,128)(2,1)S(1)}, bf16[512,2048]{1,0:T(8,128)(2,1)S(1)}) custom-call(s32[4,32]{1,0:T(4,128)} %refs_0_.1, s32[4,4]{1,0:T(4,128)} %refs_1_.1, s32[1,4]{1,0:T(1,128)} %refs_2_.2, s32[8,16]{1,0:T(8,128)} %bitcast.2, f32[8,16]{1,0:T(8,128)} %bitcast.3, bf16[128,512]{1,0:T(8,128)(2,1)} %refs_5_.2, bf16[2,128,128]{2,1,0:T(8,128)(2,1)} %refs_6_.1, ...), custom_call_target="tpu_custom_call" | custom-call | tf_op jit(solution)/shard_map/attend/pallas_call | solution.py:226
  4.3 2.8 %collective-permute-start.2 = (bf16[64,1024]{1,0:T(8,128)(2,1)S(1)}, bf16[64,1024]{1,0:T(8,128)(2,1)S(1)}, u32[]{:S(2)}, u32[]{:S(2)}) collective-permute-start(bf16[64,1024]{1,0:T(8,128)(2,1)S(1)} %get-tuple-element.36), channel_id=1, source_target_pairs={{0,5},{1,2},{2,1},{3,6},{4,7},{5,0},{6,3},{7,4},{8,11},{9,12},{10,... | collective-permute-start | bytes 393224 | tf_op jit(solution)/shard_map/ppermute | solution.py:43
  7.4 2.2 %collective-permute-done.2 = bf16[64,1024]{1,0:T(8,128)(2,1)S(1)} collective-permute-done((bf16[64,1024]{1,0:T(8,128)(2,1)S(1)}, bf16[64,1024]{1,0:T(8,128)(2,1)S(1)}, u32[]{:S(2)}, u32[]{:S(2)}) %collective-permute-start.2) | collective-permute-done | bytes 131104 | tf_op jit(solution)/shard_map/ppermute | solution.py:43
  9.7 3.1 %collective-permute-start.4 = (bf16[32,1024]{1,0:T(8,128)(2,1)S(1)}, bf16[32,1024]{1,0:T(8,128)(2,1)S(1)}, u32[]{:S(2)}, u32[]{:S(2)}) collective-permute-start(bf16[32,1024]{1,0:T(8,128)(2,1)S(1)} %slice.109), channel_id=1, source_target_pairs={{0,9},{1,4},{2,7},{3,10},{4,1},{5,12},{6,15},{7,2},{8,13},{9,0},{1... | collective-permute-start | bytes 196616 | tf_op jit(solution)/shard_map/ppermute | solution.py:43
  12.9 1.6 %collective-permute-start.3 = (bf16[32,1024]{1,0:T(8,128)(2,1)S(1)}, bf16[32,1024]{1,0:T(8,128)(2,1)S(1)}, u32[]{:S(2)}, u32[]{:S(2)}) collective-permute-start(bf16[32,1024]{1,0:T(8,128)(2,1)S(1)} %slice.108), channel_id=1, source_target_pairs={{0,9},{1,4},{2,7},{3,10},{4,1},{5,12},{6,15},{7,2},{8,13},{9,0},{1... | collective-permute-start | bytes 196616 | tf_op jit(solution)/shard_map/ppermute | solution.py:43
  15.3 1.8 %collective-permute-start.6 = (bf16[32,1152]{1,0:T(8,128)(2,1)S(1)}, bf16[32,1152]{1,0:T(8,128)(2,1)S(1)}, u32[]{:S(2)}, u32[]{:S(2)}) collective-permute-start(bf16[32,1152]{1,0:T(8,128)(2,1)S(1)} %fusion.2), channel_id=1, source_target_pairs={{0,3},{1,8},{2,11},{3,0},{4,13},{5,6},{6,5},{7,14},{8,1},{9,10},{1... | collective-permute-start | bytes 221192 | tf_op jit(solution)/shard_map/ppermute | solution.py:43
  17.6 1.3 %collective-permute-start.5 = (bf16[32,1024]{1,0:T(8,128)(2,1)S(1)}, bf16[32,1024]{1,0:T(8,128)(2,1)S(1)}, u32[]{:S(2)}, u32[]{:S(2)}) collective-permute-start(bf16[32,1024]{1,0:T(8,128)(2,1)S(1)} %fusion.3), channel_id=1, source_target_pairs={{0,3},{1,8},{2,11},{3,0},{4,13},{5,6},{6,5},{7,14},{8,1},{9,10},{1... | collective-permute-start | bytes 196616 | tf_op jit(solution)/shard_map/ppermute | solution.py:43
  19.2 3.2 %collective-permute-start.8 = (bf16[32,1152]{1,0:T(8,128)(2,1)S(1)}, bf16[32,1152]{1,0:T(8,128)(2,1)S(1)}, u32[]{:S(2)}, u32[]{:S(2)}) collective-permute-start(bf16[32,1152]{1,0:T(8,128)(2,1)S(1)} %fusion), channel_id=1, source_target_pairs={{0,9},{1,4},{2,7},{3,10},{4,1},{5,12},{6,15},{7,2},{8,13},{9,0},{1... | collective-permute-start | bytes 221192 | tf_op jit(solution)/shard_map/ppermute | solution.py:43
  23.3 1.2 %collective-permute-done.8 = bf16[32,1152]{1,0:T(8,128)(2,1)S(1)} collective-permute-done((bf16[32,1152]{1,0:T(8,128)(2,1)S(1)}, bf16[32,1152]{1,0:T(8,128)(2,1)S(1)}, u32[]{:S(2)}, u32[]{:S(2)}) %collective-permute-start.8) | collective-permute-done | bytes 73760 | tf_op jit(solution)/shard_map/ppermute | solution.py:43
  24.5 1.6 %collective-permute-start.10 = (bf16[64,1152]{1,0:T(8,128)(2,1)S(1)}, bf16[64,1152]{1,0:T(8,128)(2,1)S(1)}, u32[]{:S(2)}, u32[]{:S(2)}) collective-permute-start(bf16[64,1152]{1,0:T(8,128)(2,1)S(1)} %pad_maximum_fusion.1.refs_0_.refs_2_), channel_id=1, source_target_pairs={{0,5},{1,2},{2,1},{3,6},{4,7},{5,0},{6,3},{7,4},{8,11},{9,12},{10,... | collective-permute-start | bytes 442376 | tf_op jit(solution)/shard_map/ppermute | solution.py:43
  26.1 1.2 %collective-permute-done.7 = bf16[32,1024]{1,0:T(8,128)(2,1)S(1)} collective-permute-done((bf16[32,1024]{1,0:T(8,128)(2,1)S(1)}, bf16[32,1024]{1,0:T(8,128)(2,1)S(1)}, u32[]{:S(2)}, u32[]{:S(2)}) %collective-permute-start.7) | collective-permute-done | bytes 65568 | tf_op jit(solution)/shard_map/ppermute | solution.py:43
  27.4 0.9 %collective-permute-start.9 = (bf16[64,1024]{1,0:T(8,128)(2,1)S(1)}, bf16[64,1024]{1,0:T(8,128)(2,1)S(1)}, u32[]{:S(2)}, u32[]{:S(2)}) collective-permute-start(bf16[64,1024]{1,0:T(8,128)(2,1)S(1)} %pad_maximum_fusion.2.refs_0_), channel_id=1, source_target_pairs={{0,5},{1,2},{2,1},{3,6},{4,7},{5,0},{6,3},{7,4},{8,11},{9,12},{10,... | collective-permute-start | bytes 393224 | tf_op jit(solution)/shard_map/ppermute | solution.py:43
  29.2 1.0 %feed.1 = (f32[128,768]{1,0:T(8,128)S(1)}, f32[128,768]{1,0:T(8,128)S(1)}, f32[128,768]{1,0:T(8,128)S(1)}, f32[128,768]{1,0:T(8,128)S(1)}) custom-call(bf16[64,1152]{1,0:T(8,128)(2,1)S(1)} %pad_maximum_fusion.1.refs_0_.refs_2_, bf16[64,1152]{1,0:T(8,128)(2,1)S(1)} %collective-permute-done.10.refs_1_.refs_3_, bf16[1,2048,768]{2,1,0:T(8,128)(2,1)S(1)} %copy-done, ...), custom_call_target="tpu_custom_call" | custom-call | tf_op jit(solution)/shard_map/feed/pallas_call | solution.py:319
  30.2 1.6 %collective-permute-done.9.refs_1_ = bf16[64,1024]{1,0:T(8,128)(2,1)S(1)} collective-permute-done((bf16[64,1024]{1,0:T(8,128)(2,1)S(1)}, bf16[64,1024]{1,0:T(8,128)(2,1)S(1)}, u32[]{:S(2)}, u32[]{:S(2)}) %collective-permute-start.9) | collective-permute-done | bytes 131104 | tf_op jit(solution)/shard_map/ppermute | solution.py:43
  31.8 1.6 %finish.1 = (f32[64,1024]{1,0:T(8,128)S(1)}, bf16[64,1024]{1,0:T(8,128)(2,1)S(1)}, bf16[128,768]{1,0:T(8,128)(2,1)S(1)}, bf16[128,768]{1,0:T(8,128)(2,1)S(1)}, f...) custom-call(bf16[64,1024]{1,0:T(8,128)(2,1)S(1)} %pad_maximum_fusion.2.refs_0_, ...), custom_call_target="tpu_custom_call" | custom-call | tf_op jit(solution)/shard_map/finish/pallas_call | solution.py:319
  33.4 0.9 %collective-permute-start.14 = (bf16[64,1024]{1,0:T(8,128)(2,1)S(1)}, bf16[64,1024]{1,0:T(8,128)(2,1)S(1)}, u32[]{:S(2)}, u32[]{:S(2)}) collective-permute-start(bf16[64,1024]{1,0:T(8,128)(2,1)S(1)} %get-tuple-element.47), channel_id=1, source_target_pairs={{0,5},{1,2},{2,1},{3,6},{4,7},{5,0},{6,3},{7,4},{8,11},{9,12},{10,... | collective-permute-start | bytes 393224 | tf_op jit(solution)/shard_map/ppermute | solution.py:43
  34.9 1.0 %collective-permute-start.17 = (bf16[64,1024]{1,0:T(8,128)(2,1)S(1)}, bf16[64,1024]{1,0:T(8,128)(2,1)S(1)}, u32[]{:S(2)}, u32[]{:S(2)}) collective-permute-start(bf16[64,1024]{1,0:T(8,128)(2,1)S(1)} %get-tuple-element.53), channel_id=1, source_target_pairs={{0,5},{1,2},{2,1},{3,6},{4,7},{5,0},{6,3},{7,4},{8,11},{9,12},{10,... | collective-permute-start | bytes 393224 | tf_op jit(solution)/shard_map/ppermute | solution.py:43
  35.9 2.0 %collective-permute-done.14 = bf16[64,1024]{1,0:T(8,128)(2,1)S(1)} collective-permute-done((bf16[64,1024]{1,0:T(8,128)(2,1)S(1)}, bf16[64,1024]{1,0:T(8,128)(2,1)S(1)}, u32[]{:S(2)}, u32[]{:S(2)}) %collective-permute-start.14) | collective-permute-done | bytes 131104 | tf_op jit(solution)/shard_map/ppermute | solution.py:43
  37.9 1.2 %collective-permute-start.15 = (bf16[32,1024]{1,0:T(8,128)(2,1)S(1)}, bf16[32,1024]{1,0:T(8,128)(2,1)S(1)}, u32[]{:S(2)}, u32[]{:S(2)}) collective-permute-start(bf16[32,1024]{1,0:T(8,128)(2,1)S(1)} %slice.107), channel_id=1, source_target_pairs={{0,3},{1,8},{2,11},{3,0},{4,13},{5,6},{6,5},{7,14},{8,1},{9,10},{1... | collective-permute-start | bytes 196616 | tf_op jit(solution)/shard_map/ppermute | solution.py:43
  39.5 1.7 %collective-permute-start.18 = (bf16[32,1024]{1,0:T(8,128)(2,1)S(1)}, bf16[32,1024]{1,0:T(8,128)(2,1)S(1)}, u32[]{:S(2)}, u32[]{:S(2)}) collective-permute-start(bf16[32,1024]{1,0:T(8,128)(2,1)S(1)} %slice.106), channel_id=1, source_target_pairs={{0,3},{1,8},{2,11},{3,0},{4,13},{5,6},{6,5},{7,14},{8,1},{9,10},{1... | collective-permute-start | bytes 196616 | tf_op jit(solution)/shard_map/ppermute | solution.py:43
  41.7 1.7 %collective-permute-start.16 = (bf16[16,1024]{1,0:T(8,128)(2,1)S(1)}, bf16[16,1024]{1,0:T(8,128)(2,1)S(1)}, u32[]{:S(2)}, u32[]{:S(2)}) collective-permute-start(bf16[16,1024]{1,0:T(8,128)(2,1)S(1)} %slice.111), channel_id=1, source_target_pairs={{0,9},{1,4},{2,7},{3,10},{4,1},{5,12},{6,15},{7,2},{8,13},{9,0},{1... | collective-permute-start | bytes 98312 | tf_op jit(solution)/shard_map/ppermute | solution.py:43
  43.5 2.1 %collective-permute-start.19 = (bf16[16,1024]{1,0:T(8,128)(2,1)S(1)}, bf16[16,1024]{1,0:T(8,128)(2,1)S(1)}, u32[]{:S(2)}, u32[]{:S(2)}) collective-permute-start(bf16[16,1024]{1,0:T(8,128)(2,1)S(1)} %slice.110), channel_id=1, source_target_pairs={{0,9},{1,4},{2,7},{3,10},{4,1},{5,12},{6,15},{7,2},{8,13},{9,0},{1... | collective-permute-start | bytes 98312 | tf_op jit(solution)/shard_map/ppermute | solution.py:43
  46.1 1.8 %collective-permute-done.19 = bf16[16,1024]{1,0:T(8,128)(2,1)S(1)} collective-permute-done((bf16[16,1024]{1,0:T(8,128)(2,1)S(1)}, bf16[16,1024]{1,0:T(8,128)(2,1)S(1)}, u32[]{:S(2)}, u32[]{:S(2)}) %collective-permute-start.19) | collective-permute-done | bytes 32800 | tf_op jit(solution)/shard_map/ppermute | solution.py:43
  48.1 1.1 %collective-permute-done.20 = bf16[16,2048]{1,0:T(8,128)(2,1)S(1)} collective-permute-done((bf16[16,2048]{1,0:T(8,128)(2,1)S(1)}, bf16[16,2048]{1,0:T(8,128)(2,1)S(1)}, u32[]{:S(2)}, u32[]{:S(2)}) %collective-permute-start.20) | collective-permute-done | bytes 65568 | tf_op jit(solution)/shard_map/ppermute | solution.py:43
  (56 shorter events, 8.6 us)
Async XLA Ops:
  2.4 1.5 %collective-permute-start = (bf16[128,640]{1,0:T(8,128)(2,1)S(1)}, bf16[128,640]{1,0:T(8,128)(2,1)S(1)}, u32[]{:S(2)}, u32[]{:S(2)}) collective-permute-start(bf16[128,640]{1,0:T(8,128)(2,1)S(1)} %get-tuple-element.31.own), channel_id=1, source_target_pairs={{0,1},{1,0},{2,3},{3,2},{4,5},{5,4},{6,7},{7,6},{8,9},{9,8},{10,11... | collective-permute-start | bytes 491528 | tf_op jit(solution)/shard_map/ppermute | solution.py:43
  2.9 26.2 %collective-permute-start.11 = (bf16[1,2048,768]{2,1,0:T(8,128)(2,1)}, bf16[1,2048,768]{2,1,0:T(8,128)(2,1)S(1)}, u32[]{:S(2)}, u32[]{:S(2)}) collective-permute-start(bf16[1,2048,768]{2,1,0:T(8,128)(2,1)} %refs_4_.2), channel_id=1, source_target_pairs={{0,1},{1,0},{2,3},{3,2},{4,5},{5,4},{6,7},{7,6},{8,9},{9,8},{10,11... | collective-permute-start | bytes 9437192 | tf_op jit(solution)/shard_map/ppermute | solution.py:43
  3.0 26.2 %collective-permute-start.12 = (bf16[1,2048,768]{2,1,0:T(8,128)(2,1)}, bf16[1,2048,768]{2,1,0:T(8,128)(2,1)S(1)}, u32[]{:S(2)}, u32[]{:S(2)}) collective-permute-start(bf16[1,2048,768]{2,1,0:T(8,128)(2,1)} %refs_5_.3), channel_id=1, source_target_pairs={{0,1},{1,0},{2,3},{3,2},{4,5},{5,4},{6,7},{7,6},{8,9},{9,8},{10,11... | collective-permute-start | bytes 9437192 | tf_op jit(solution)/shard_map/ppermute | solution.py:43
  3.4 28.4 %collective-permute-start.13 = (bf16[1,768,2048]{2,1,0:T(8,128)(2,1)}, bf16[1,768,2048]{2,1,0:T(8,128)(2,1)S(1)}, u32[]{:S(2)}, u32[]{:S(2)}) collective-permute-start(bf16[1,768,2048]{2,1,0:T(8,128)(2,1)} %refs_4_.3), channel_id=1, source_target_pairs={{0,1},{1,0},{2,3},{3,2},{4,5},{5,4},{6,7},{7,6},{8,9},{9,8},{10,11... | collective-permute-start | bytes 9437192 | tf_op jit(solution)/shard_map/ppermute | solution.py:43
  4.3 5.4 %collective-permute-start.2 = (bf16[64,1024]{1,0:T(8,128)(2,1)S(1)}, bf16[64,1024]{1,0:T(8,128)(2,1)S(1)}, u32[]{:S(2)}, u32[]{:S(2)}) collective-permute-start(bf16[64,1024]{1,0:T(8,128)(2,1)S(1)} %get-tuple-element.36), channel_id=1, source_target_pairs={{0,5},{1,2},{2,1},{3,6},{4,7},{5,0},{6,3},{7,4},{8,11},{9,12},{10,... | collective-permute-start | bytes 393224 | tf_op jit(solution)/shard_map/ppermute | solution.py:43
  7.0 22.2 %copy-start.1 = (bf16[1,2048,768]{2,1,0:T(8,128)(2,1)S(1)}, bf16[1,2048,768]{2,1,0:T(8,128)(2,1)}, u32[]{:S(2)}) copy-start(bf16[1,2048,768]{2,1,0:T(8,128)(2,1)} %refs_5_.3) | copy-start | bytes 9437188
  7.3 21.8 %copy-start = (bf16[1,2048,768]{2,1,0:T(8,128)(2,1)S(1)}, bf16[1,2048,768]{2,1,0:T(8,128)(2,1)}, u32[]{:S(2)}) copy-start(bf16[1,2048,768]{2,1,0:T(8,128)(2,1)} %refs_4_.2) | copy-start | bytes 9437188
  7.3 5.5 %collective-permute-start.1 = (bf16[64,1024]{1,0:T(8,128)(2,1)S(1)}, bf16[64,1024]{1,0:T(8,128)(2,1)S(1)}, u32[]{:S(2)}, u32[]{:S(2)}) collective-permute-start(bf16[64,1024]{1,0:T(8,128)(2,1)S(1)} %get-tuple-element.34), channel_id=1, source_target_pairs={{0,5},{1,2},{2,1},{3,6},{4,7},{5,0},{6,3},{7,4},{8,11},{9,12},{10,... | collective-permute-start | bytes 393224 | tf_op jit(solution)/shard_map/ppermute | solution.py:43
  9.7 5.6 %collective-permute-start.4 = (bf16[32,1024]{1,0:T(8,128)(2,1)S(1)}, bf16[32,1024]{1,0:T(8,128)(2,1)S(1)}, u32[]{:S(2)}, u32[]{:S(2)}) collective-permute-start(bf16[32,1024]{1,0:T(8,128)(2,1)S(1)} %slice.109), channel_id=1, source_target_pairs={{0,9},{1,4},{2,7},{3,10},{4,1},{5,12},{6,15},{7,2},{8,13},{9,0},{1... | collective-permute-start | bytes 196616 | tf_op jit(solution)/shard_map/ppermute | solution.py:43
  12.9 4.7 %collective-permute-start.3 = (bf16[32,1024]{1,0:T(8,128)(2,1)S(1)}, bf16[32,1024]{1,0:T(8,128)(2,1)S(1)}, u32[]{:S(2)}, u32[]{:S(2)}) collective-permute-start(bf16[32,1024]{1,0:T(8,128)(2,1)S(1)} %slice.108), channel_id=1, source_target_pairs={{0,9},{1,4},{2,7},{3,10},{4,1},{5,12},{6,15},{7,2},{8,13},{9,0},{1... | collective-permute-start | bytes 196616 | tf_op jit(solution)/shard_map/ppermute | solution.py:43
  15.3 3.8 %collective-permute-start.6 = (bf16[32,1152]{1,0:T(8,128)(2,1)S(1)}, bf16[32,1152]{1,0:T(8,128)(2,1)S(1)}, u32[]{:S(2)}, u32[]{:S(2)}) collective-permute-start(bf16[32,1152]{1,0:T(8,128)(2,1)S(1)} %fusion.2), channel_id=1, source_target_pairs={{0,3},{1,8},{2,11},{3,0},{4,13},{5,6},{6,5},{7,14},{8,1},{9,10},{1... | collective-permute-start | bytes 221192 | tf_op jit(solution)/shard_map/ppermute | solution.py:43
  17.6 4.8 %collective-permute-start.5 = (bf16[32,1024]{1,0:T(8,128)(2,1)S(1)}, bf16[32,1024]{1,0:T(8,128)(2,1)S(1)}, u32[]{:S(2)}, u32[]{:S(2)}) collective-permute-start(bf16[32,1024]{1,0:T(8,128)(2,1)S(1)} %fusion.3), channel_id=1, source_target_pairs={{0,3},{1,8},{2,11},{3,0},{4,13},{5,6},{6,5},{7,14},{8,1},{9,10},{1... | collective-permute-start | bytes 196616 | tf_op jit(solution)/shard_map/ppermute | solution.py:43
  19.2 5.3 %collective-permute-start.8 = (bf16[32,1152]{1,0:T(8,128)(2,1)S(1)}, bf16[32,1152]{1,0:T(8,128)(2,1)S(1)}, u32[]{:S(2)}, u32[]{:S(2)}) collective-permute-start(bf16[32,1152]{1,0:T(8,128)(2,1)S(1)} %fusion), channel_id=1, source_target_pairs={{0,9},{1,4},{2,7},{3,10},{4,1},{5,12},{6,15},{7,2},{8,13},{9,0},{1... | collective-permute-start | bytes 221192 | tf_op jit(solution)/shard_map/ppermute | solution.py:43
  22.4 4.9 %collective-permute-start.7 = (bf16[32,1024]{1,0:T(8,128)(2,1)S(1)}, bf16[32,1024]{1,0:T(8,128)(2,1)S(1)}, u32[]{:S(2)}, u32[]{:S(2)}) collective-permute-start(bf16[32,1024]{1,0:T(8,128)(2,1)S(1)} %fusion.1), channel_id=1, source_target_pairs={{0,9},{1,4},{2,7},{3,10},{4,1},{5,12},{6,15},{7,2},{8,13},{9,0},{1... | collective-permute-start | bytes 196616 | tf_op jit(solution)/shard_map/ppermute | solution.py:43
  24.5 4.6 %collective-permute-start.10 = (bf16[64,1152]{1,0:T(8,128)(2,1)S(1)}, bf16[64,1152]{1,0:T(8,128)(2,1)S(1)}, u32[]{:S(2)}, u32[]{:S(2)}) collective-permute-start(bf16[64,1152]{1,0:T(8,128)(2,1)S(1)} %pad_maximum_fusion.1.refs_0_.refs_2_), channel_id=1, source_target_pairs={{0,5},{1,2},{2,1},{3,6},{4,7},{5,0},{6,3},{7,4},{8,11},{9,12},{10,... | collective-permute-start | bytes 442376 | tf_op jit(solution)/shard_map/ppermute | solution.py:43
  27.4 4.5 %copy-start.2 = (bf16[1,768,2048]{2,1,0:T(8,128)(2,1)S(1)}, bf16[1,768,2048]{2,1,0:T(8,128)(2,1)}, u32[]{:S(2)}) copy-start(bf16[1,768,2048]{2,1,0:T(8,128)(2,1)} %refs_4_.3) | copy-start | bytes 9437188
  27.4 4.5 %collective-permute-start.9 = (bf16[64,1024]{1,0:T(8,128)(2,1)S(1)}, bf16[64,1024]{1,0:T(8,128)(2,1)S(1)}, u32[]{:S(2)}, u32[]{:S(2)}) collective-permute-start(bf16[64,1024]{1,0:T(8,128)(2,1)S(1)} %pad_maximum_fusion.2.refs_0_), channel_id=1, source_target_pairs={{0,5},{1,2},{2,1},{3,6},{4,7},{5,0},{6,3},{7,4},{8,11},{9,12},{10,... | collective-permute-start | bytes 393224 | tf_op jit(solution)/shard_map/ppermute | solution.py:43
  33.4 4.5 %collective-permute-start.14 = (bf16[64,1024]{1,0:T(8,128)(2,1)S(1)}, bf16[64,1024]{1,0:T(8,128)(2,1)S(1)}, u32[]{:S(2)}, u32[]{:S(2)}) collective-permute-start(bf16[64,1024]{1,0:T(8,128)(2,1)S(1)} %get-tuple-element.47), channel_id=1, source_target_pairs={{0,5},{1,2},{2,1},{3,6},{4,7},{5,0},{6,3},{7,4},{8,11},{9,12},{10,... | collective-permute-start | bytes 393224 | tf_op jit(solution)/shard_map/ppermute | solution.py:43
  34.9 4.5 %collective-permute-start.17 = (bf16[64,1024]{1,0:T(8,128)(2,1)S(1)}, bf16[64,1024]{1,0:T(8,128)(2,1)S(1)}, u32[]{:S(2)}, u32[]{:S(2)}) collective-permute-start(bf16[64,1024]{1,0:T(8,128)(2,1)S(1)} %get-tuple-element.53), channel_id=1, source_target_pairs={{0,5},{1,2},{2,1},{3,6},{4,7},{5,0},{6,3},{7,4},{8,11},{9,12},{10,... | collective-permute-start | bytes 393224 | tf_op jit(solution)/shard_map/ppermute | solution.py:43
  37.9 3.8 %collective-permute-start.15 = (bf16[32,1024]{1,0:T(8,128)(2,1)S(1)}, bf16[32,1024]{1,0:T(8,128)(2,1)S(1)}, u32[]{:S(2)}, u32[]{:S(2)}) collective-permute-start(bf16[32,1024]{1,0:T(8,128)(2,1)S(1)} %slice.107), channel_id=1, source_target_pairs={{0,3},{1,8},{2,11},{3,0},{4,13},{5,6},{6,5},{7,14},{8,1},{9,10},{1... | collective-permute-start | bytes 196616 | tf_op jit(solution)/shard_map/ppermute | solution.py:43
  39.5 4.0 %collective-permute-start.18 = (bf16[32,1024]{1,0:T(8,128)(2,1)S(1)}, bf16[32,1024]{1,0:T(8,128)(2,1)S(1)}, u32[]{:S(2)}, u32[]{:S(2)}) collective-permute-start(bf16[32,1024]{1,0:T(8,128)(2,1)S(1)} %slice.106), channel_id=1, source_target_pairs={{0,3},{1,8},{2,11},{3,0},{4,13},{5,6},{6,5},{7,14},{8,1},{9,10},{1... | collective-permute-start | bytes 196616 | tf_op jit(solution)/shard_map/ppermute | solution.py:43
  41.7 4.3 %collective-permute-start.16 = (bf16[16,1024]{1,0:T(8,128)(2,1)S(1)}, bf16[16,1024]{1,0:T(8,128)(2,1)S(1)}, u32[]{:S(2)}, u32[]{:S(2)}) collective-permute-start(bf16[16,1024]{1,0:T(8,128)(2,1)S(1)} %slice.111), channel_id=1, source_target_pairs={{0,9},{1,4},{2,7},{3,10},{4,1},{5,12},{6,15},{7,2},{8,13},{9,0},{1... | collective-permute-start | bytes 98312 | tf_op jit(solution)/shard_map/ppermute | solution.py:43
  43.5 4.4 %collective-permute-start.19 = (bf16[16,1024]{1,0:T(8,128)(2,1)S(1)}, bf16[16,1024]{1,0:T(8,128)(2,1)S(1)}, u32[]{:S(2)}, u32[]{:S(2)}) collective-permute-start(bf16[16,1024]{1,0:T(8,128)(2,1)S(1)} %slice.110), channel_id=1, source_target_pairs={{0,9},{1,4},{2,7},{3,10},{4,1},{5,12},{6,15},{7,2},{8,13},{9,0},{1... | collective-permute-start | bytes 98312 | tf_op jit(solution)/shard_map/ppermute | solution.py:43
  47.9 1.3 %collective-permute-start.20 = (bf16[16,2048]{1,0:T(8,128)(2,1)S(1)}, bf16[16,2048]{1,0:T(8,128)(2,1)S(1)}, u32[]{:S(2)}, u32[]{:S(2)}) collective-permute-start(bf16[16,2048]{1,0:T(8,128)(2,1)S(1)} %pad_maximum_fusion.3), channel_id=1, source_target_pairs={{0,1},{1,0},{2,3},{3,2},{4,5},{5,4},{6,7},{7,6},{8,9},{9,8},{10,11... | collective-permute-start | bytes 196616 | tf_op jit(solution)/shard_map/ppermute | solution.py:43

commit v8 on v7

--- a/solution.py
+++ b/solution.py
@@ -90,7 +90,10 @@
 def attend_kernel(axis_width, *refs):
     sources, (ordered, w_out), scratch = refs[:9], refs[9:11], refs[11:]
     *inputs, attended, sems = scratch
-    copies = started(sources, [*inputs, w_out], sems)
+    *sources, pools, w_out_source = sources
+    *others, pools_in = inputs
+    sources = [*sources, pools.at[0], pools.at[1], w_out_source]
+    copies = started(sources, [*others, pools_in.at[0], pools_in.at[1], w_out], sems)
     parents, table, lengths, expert_ids, gate_weights, queries, tree_kv, kv_cache = inputs
     seq_count, node_count = parents.shape
     head_dim = tree_kv.shape[-1]
@@ -115,20 +118,19 @@
             above = jnp.take_along_axis(above, above, axis=1)
         words = words | jnp.take_along_axis(words, above, axis=1)
 
-    for copy in copies[1:-1]:
+    for copy in copies[1:-2]:
         copy.wait()
     query_nodes = lax.broadcasted_iota(jnp.int32, (8, query_count), 1) % node_count
     node_rows = lax.broadcasted_iota(jnp.int32, (node_count, query_count), 0)
     positions = lax.broadcasted_iota(jnp.int32, (cached, query_count), 0)
+    weighed = []
     for s in range(seq_count):
         own = slice(s * node_count, (s + 1) * node_count)
         word = jnp.take_along_axis(words, query_nodes + s * node_count, axis=1)
         word = jnp.broadcast_to(word[:1], node_rows.shape)
         tree_open = (lax.shift_right_logical(word, node_rows) & 1) == 1
         keys = [kv_cache[0, table[s, p]] for p in range(pages)]
-        values = [kv_cache[1, table[s, p]] for p in range(pages)]
         key_rows = jnp.concatenate(keys + [tree_kv[0, own]], axis=0)
-        value_rows = jnp.concatenate(values + [tree_kv[1, own]], axis=0)
         query_rows = jnp.concatenate(
             [queries[own, h * head_dim : (h + 1) * head_dim] for h in range(head_count)], axis=0
         )
@@ -141,8 +143,14 @@
         highest = jnp.max(masked, axis=0, keepdims=True)
         probs = jnp.exp(masked - highest)
         total = jnp.broadcast_to(jnp.sum(probs, axis=0, keepdims=True), (head_dim, query_count))
+        weighed.append((probs.astype(bf16), total))
+    copies[-2].wait()
+    for s, (probs, total) in enumerate(weighed):
+        own = slice(s * node_count, (s + 1) * node_count)
+        values = [kv_cache[1, table[s, p]] for p in range(pages)]
+        value_rows = jnp.concatenate(values + [tree_kv[1, own]], axis=0)
         blended = lax.dot_general(
-            probs.astype(bf16), value_rows, (((0,), (0,)), ((), ())), preferred_element_type=f32
+            probs, value_rows, (((0,), (0,)), ((), ())), preferred_element_type=f32
         )
         blended = (blended / total.T).astype(bf16)
         for h in range(head_count):
@@ -232,7 +240,7 @@
         in_specs=[pl.BlockSpec(memory_space=pltpu.HBM)] * len(given),
         out_specs=[pl.BlockSpec(memory_space=pltpu.VMEM)] * 2,
         scratch_shapes=[space(x.shape, x.dtype) for space, x in zip(spaces, given)]
-        + [pltpu.VMEM(queries.shape, jnp.bfloat16), pltpu.SemaphoreType.DMA((len(given),))],
+        + [pltpu.VMEM(queries.shape, jnp.bfloat16), pltpu.SemaphoreType.DMA((len(given) + 1,))],
         compiler_params=pltpu.CompilerParams(vmem_limit_bytes=16 * 1024 * 1024),
         name="attend",
     )(*given)

time: 50 us -> 49.8 us (level)
  no operation moved by 1% of the time
where the time goes in v8:
time: 49.8 us; the launch traced here: 49.6 us
  starting transfers between devices  27.1 us (54%)
  waiting for transfers between devices  15.5 us (31%)
  Pallas kernels  5.8 us (12%)
  other arithmetic  0.94 us (2%)
    ppermute x21, starting transfers between devices, exchange(): return lax.ppermute(block, 'wide', [(i, route(i)) for i in range(count)])  27.1 us
    ppermute x21, waiting for transfers between devices, exchange(): return lax.ppermute(block, 'wide', [(i, route(i)) for i in range(count)])  15.5 us
    pallas_call x5, Pallas kernels, local_call(): pl.pallas_call(kernel, out_shape=out_shape, in_specs=[pl.BlockSpec(memory...  3.83 us
    pallas_call x1, Pallas kernels, attend(): pl.pallas_call(functools.partial(attend_kernel, axis_width), out_shape=[p...  1.97 us
  transfers between devices with their start and end apart: 21, of which 15 were waited for; matrix products, arithmetic and copies ran while one was open for 1% of the time, Pallas kernels for 5%

profile of v8, /device:TPU:0, one launch (start us, length us, event | category | flops | bytes accessed | tf_op | source)
XLA Modules:
  0.0 49.6 jit_solution(16447403640719846333)
XLA Ops:
  0.0 2.0 %attend.1 = (bf16[128,640]{1,0:T(8,128)(2,1)S(1)}, bf16[512,2048]{1,0:T(8,128)(2,1)S(1)}) custom-call(s32[4,32]{1,0:T(4,128)} %refs_0_.1, s32[4,4]{1,0:T(4,128)} %refs_1_.1, s32[1,4]{1,0:T(1,128)} %refs_2_.2, s32[8,16]{1,0:T(8,128)} %bitcast.2, f32[8,16]{1,0:T(8,128)} %bitcast.3, bf16[128,512]{1,0:T(8,128)(2,1)} %refs_5_.2, bf16[2,128,128]{2,1,0:T(8,128)(2,1)} %refs_6_.1, ...), custom_call_target="tpu_custom_call" | custom-call | tf_op jit(solution)/shard_map/attend/pallas_call | solution.py:234
  3.8 2.8 %collective-permute-start.2 = (bf16[64,1024]{1,0:T(8,128)(2,1)S(1)}, bf16[64,1024]{1,0:T(8,128)(2,1)S(1)}, u32[]{:S(2)}, u32[]{:S(2)}) collective-permute-start(bf16[64,1024]{1,0:T(8,128)(2,1)S(1)} %get-tuple-element.36), channel_id=1, source_target_pairs={{0,5},{1,2},{2,1},{3,6},{4,7},{5,0},{6,3},{7,4},{8,11},{9,12},{10,... | collective-permute-start | bytes 393224 | tf_op jit(solution)/shard_map/ppermute | solution.py:43
  7.0 2.2 %collective-permute-done.2 = bf16[64,1024]{1,0:T(8,128)(2,1)S(1)} collective-permute-done((bf16[64,1024]{1,0:T(8,128)(2,1)S(1)}, bf16[64,1024]{1,0:T(8,128)(2,1)S(1)}, u32[]{:S(2)}, u32[]{:S(2)}) %collective-permute-start.2) | collective-permute-done | bytes 131104 | tf_op jit(solution)/shard_map/ppermute | solution.py:43
  9.3 3.1 %collective-permute-start.4 = (bf16[32,1024]{1,0:T(8,128)(2,1)S(1)}, bf16[32,1024]{1,0:T(8,128)(2,1)S(1)}, u32[]{:S(2)}, u32[]{:S(2)}) collective-permute-start(bf16[32,1024]{1,0:T(8,128)(2,1)S(1)} %slice.109), channel_id=1, source_target_pairs={{0,9},{1,4},{2,7},{3,10},{4,1},{5,12},{6,15},{7,2},{8,13},{9,0},{1... | collective-permute-start | bytes 196616 | tf_op jit(solution)/shard_map/ppermute | solution.py:43
  12.5 1.6 %collective-permute-start.3 = (bf16[32,1024]{1,0:T(8,128)(2,1)S(1)}, bf16[32,1024]{1,0:T(8,128)(2,1)S(1)}, u32[]{:S(2)}, u32[]{:S(2)}) collective-permute-start(bf16[32,1024]{1,0:T(8,128)(2,1)S(1)} %slice.108), channel_id=1, source_target_pairs={{0,9},{1,4},{2,7},{3,10},{4,1},{5,12},{6,15},{7,2},{8,13},{9,0},{1... | collective-permute-start | bytes 196616 | tf_op jit(solution)/shard_map/ppermute | solution.py:43
  14.9 1.9 %collective-permute-start.6 = (bf16[32,1152]{1,0:T(8,128)(2,1)S(1)}, bf16[32,1152]{1,0:T(8,128)(2,1)S(1)}, u32[]{:S(2)}, u32[]{:S(2)}) collective-permute-start(bf16[32,1152]{1,0:T(8,128)(2,1)S(1)} %fusion.2), channel_id=1, source_target_pairs={{0,3},{1,8},{2,11},{3,0},{4,13},{5,6},{6,5},{7,14},{8,1},{9,10},{1... | collective-permute-start | bytes 221192 | tf_op jit(solution)/shard_map/ppermute | solution.py:43
  17.1 1.3 %collective-permute-start.5 = (bf16[32,1024]{1,0:T(8,128)(2,1)S(1)}, bf16[32,1024]{1,0:T(8,128)(2,1)S(1)}, u32[]{:S(2)}, u32[]{:S(2)}) collective-permute-start(bf16[32,1024]{1,0:T(8,128)(2,1)S(1)} %fusion.3), channel_id=1, source_target_pairs={{0,3},{1,8},{2,11},{3,0},{4,13},{5,6},{6,5},{7,14},{8,1},{9,10},{1... | collective-permute-start | bytes 196616 | tf_op jit(solution)/shard_map/ppermute | solution.py:43
  18.8 3.1 %collective-permute-start.8 = (bf16[32,1152]{1,0:T(8,128)(2,1)S(1)}, bf16[32,1152]{1,0:T(8,128)(2,1)S(1)}, u32[]{:S(2)}, u32[]{:S(2)}) collective-permute-start(bf16[32,1152]{1,0:T(8,128)(2,1)S(1)} %fusion), channel_id=1, source_target_pairs={{0,9},{1,4},{2,7},{3,10},{4,1},{5,12},{6,15},{7,2},{8,13},{9,0},{1... | collective-permute-start | bytes 221192 | tf_op jit(solution)/shard_map/ppermute | solution.py:43
  22.8 1.2 %collective-permute-done.8 = bf16[32,1152]{1,0:T(8,128)(2,1)S(1)} collective-permute-done((bf16[32,1152]{1,0:T(8,128)(2,1)S(1)}, bf16[32,1152]{1,0:T(8,128)(2,1)S(1)}, u32[]{:S(2)}, u32[]{:S(2)}) %collective-permute-start.8) | collective-permute-done | bytes 73760 | tf_op jit(solution)/shard_map/ppermute | solution.py:43
  24.1 1.6 %collective-permute-start.10 = (bf16[64,1152]{1,0:T(8,128)(2,1)S(1)}, bf16[64,1152]{1,0:T(8,128)(2,1)S(1)}, u32[]{:S(2)}, u32[]{:S(2)}) collective-permute-start(bf16[64,1152]{1,0:T(8,128)(2,1)S(1)} %pad_maximum_fusion.1.refs_0_.refs_2_), channel_id=1, source_target_pairs={{0,5},{1,2},{2,1},{3,6},{4,7},{5,0},{6,3},{7,4},{8,11},{9,12},{10,... | collective-permute-start | bytes 442376 | tf_op jit(solution)/shard_map/ppermute | solution.py:43
  25.7 1.2 %collective-permute-done.7 = bf16[32,1024]{1,0:T(8,128)(2,1)S(1)} collective-permute-done((bf16[32,1024]{1,0:T(8,128)(2,1)S(1)}, bf16[32,1024]{1,0:T(8,128)(2,1)S(1)}, u32[]{:S(2)}, u32[]{:S(2)}) %collective-permute-start.7) | collective-permute-done | bytes 65568 | tf_op jit(solution)/shard_map/ppermute | solution.py:43
  26.9 0.9 %collective-permute-start.9 = (bf16[64,1024]{1,0:T(8,128)(2,1)S(1)}, bf16[64,1024]{1,0:T(8,128)(2,1)S(1)}, u32[]{:S(2)}, u32[]{:S(2)}) collective-permute-start(bf16[64,1024]{1,0:T(8,128)(2,1)S(1)} %pad_maximum_fusion.2.refs_0_), channel_id=1, source_target_pairs={{0,5},{1,2},{2,1},{3,6},{4,7},{5,0},{6,3},{7,4},{8,11},{9,12},{10,... | collective-permute-start | bytes 393224 | tf_op jit(solution)/shard_map/ppermute | solution.py:43
  28.8 1.0 %feed.1 = (f32[128,768]{1,0:T(8,128)S(1)}, f32[128,768]{1,0:T(8,128)S(1)}, f32[128,768]{1,0:T(8,128)S(1)}, f32[128,768]{1,0:T(8,128)S(1)}) custom-call(bf16[64,1152]{1,0:T(8,128)(2,1)S(1)} %pad_maximum_fusion.1.refs_0_.refs_2_, bf16[64,1152]{1,0:T(8,128)(2,1)S(1)} %collective-permute-done.10.refs_1_.refs_3_, bf16[1,2048,768]{2,1,0:T(8,128)(2,1)S(1)} %copy-done, ...), custom_call_target="tpu_custom_call" | custom-call | tf_op jit(solution)/shard_map/feed/pallas_call | solution.py:327
  29.8 1.6 %collective-permute-done.9.refs_1_ = bf16[64,1024]{1,0:T(8,128)(2,1)S(1)} collective-permute-done((bf16[64,1024]{1,0:T(8,128)(2,1)S(1)}, bf16[64,1024]{1,0:T(8,128)(2,1)S(1)}, u32[]{:S(2)}, u32[]{:S(2)}) %collective-permute-start.9) | collective-permute-done | bytes 131104 | tf_op jit(solution)/shard_map/ppermute | solution.py:43
  31.4 1.6 %finish.1 = (f32[64,1024]{1,0:T(8,128)S(1)}, bf16[64,1024]{1,0:T(8,128)(2,1)S(1)}, bf16[128,768]{1,0:T(8,128)(2,1)S(1)}, bf16[128,768]{1,0:T(8,128)(2,1)S(1)}, f...) custom-call(bf16[64,1024]{1,0:T(8,128)(2,1)S(1)} %pad_maximum_fusion.2.refs_0_, ...), custom_call_target="tpu_custom_call" | custom-call | tf_op jit(solution)/shard_map/finish/pallas_call | solution.py:327
  33.0 0.9 %collective-permute-start.14 = (bf16[64,1024]{1,0:T(8,128)(2,1)S(1)}, bf16[64,1024]{1,0:T(8,128)(2,1)S(1)}, u32[]{:S(2)}, u32[]{:S(2)}) collective-permute-start(bf16[64,1024]{1,0:T(8,128)(2,1)S(1)} %get-tuple-element.47), channel_id=1, source_target_pairs={{0,5},{1,2},{2,1},{3,6},{4,7},{5,0},{6,3},{7,4},{8,11},{9,12},{10,... | collective-permute-start | bytes 393224 | tf_op jit(solution)/shard_map/ppermute | solution.py:43
  34.5 1.0 %collective-permute-start.17 = (bf16[64,1024]{1,0:T(8,128)(2,1)S(1)}, bf16[64,1024]{1,0:T(8,128)(2,1)S(1)}, u32[]{:S(2)}, u32[]{:S(2)}) collective-permute-start(bf16[64,1024]{1,0:T(8,128)(2,1)S(1)} %get-tuple-element.53), channel_id=1, source_target_pairs={{0,5},{1,2},{2,1},{3,6},{4,7},{5,0},{6,3},{7,4},{8,11},{9,12},{10,... | collective-permute-start | bytes 393224 | tf_op jit(solution)/shard_map/ppermute | solution.py:43
  35.5 2.0 %collective-permute-done.14 = bf16[64,1024]{1,0:T(8,128)(2,1)S(1)} collective-permute-done((bf16[64,1024]{1,0:T(8,128)(2,1)S(1)}, bf16[64,1024]{1,0:T(8,128)(2,1)S(1)}, u32[]{:S(2)}, u32[]{:S(2)}) %collective-permute-start.14) | collective-permute-done | bytes 131104 | tf_op jit(solution)/shard_map/ppermute | solution.py:43
  37.5 1.2 %collective-permute-start.15 = (bf16[32,1024]{1,0:T(8,128)(2,1)S(1)}, bf16[32,1024]{1,0:T(8,128)(2,1)S(1)}, u32[]{:S(2)}, u32[]{:S(2)}) collective-permute-start(bf16[32,1024]{1,0:T(8,128)(2,1)S(1)} %slice.107), channel_id=1, source_target_pairs={{0,3},{1,8},{2,11},{3,0},{4,13},{5,6},{6,5},{7,14},{8,1},{9,10},{1... | collective-permute-start | bytes 196616 | tf_op jit(solution)/shard_map/ppermute | solution.py:43
  39.0 1.7 %collective-permute-start.18 = (bf16[32,1024]{1,0:T(8,128)(2,1)S(1)}, bf16[32,1024]{1,0:T(8,128)(2,1)S(1)}, u32[]{:S(2)}, u32[]{:S(2)}) collective-permute-start(bf16[32,1024]{1,0:T(8,128)(2,1)S(1)} %slice.106), channel_id=1, source_target_pairs={{0,3},{1,8},{2,11},{3,0},{4,13},{5,6},{6,5},{7,14},{8,1},{9,10},{1... | collective-permute-start | bytes 196616 | tf_op jit(solution)/shard_map/ppermute | solution.py:43
  41.3 1.9 %collective-permute-start.16 = (bf16[16,1024]{1,0:T(8,128)(2,1)S(1)}, bf16[16,1024]{1,0:T(8,128)(2,1)S(1)}, u32[]{:S(2)}, u32[]{:S(2)}) collective-permute-start(bf16[16,1024]{1,0:T(8,128)(2,1)S(1)} %slice.111), channel_id=1, source_target_pairs={{0,9},{1,4},{2,7},{3,10},{4,1},{5,12},{6,15},{7,2},{8,13},{9,0},{1... | collective-permute-start | bytes 98312 | tf_op jit(solution)/shard_map/ppermute | solution.py:43
  43.3 1.9 %collective-permute-start.19 = (bf16[16,1024]{1,0:T(8,128)(2,1)S(1)}, bf16[16,1024]{1,0:T(8,128)(2,1)S(1)}, u32[]{:S(2)}, u32[]{:S(2)}) collective-permute-start(bf16[16,1024]{1,0:T(8,128)(2,1)S(1)} %slice.110), channel_id=1, source_target_pairs={{0,9},{1,4},{2,7},{3,10},{4,1},{5,12},{6,15},{7,2},{8,13},{9,0},{1... | collective-permute-start | bytes 98312 | tf_op jit(solution)/shard_map/ppermute | solution.py:43
  45.6 2.0 %collective-permute-done.19 = bf16[16,1024]{1,0:T(8,128)(2,1)S(1)} collective-permute-done((bf16[16,1024]{1,0:T(8,128)(2,1)S(1)}, bf16[16,1024]{1,0:T(8,128)(2,1)S(1)}, u32[]{:S(2)}, u32[]{:S(2)}) %collective-permute-start.19) | collective-permute-done | bytes 32800 | tf_op jit(solution)/shard_map/ppermute | solution.py:43
  47.8 1.1 %collective-permute-done.20 = bf16[16,2048]{1,0:T(8,128)(2,1)S(1)} collective-permute-done((bf16[16,2048]{1,0:T(8,128)(2,1)S(1)}, bf16[16,2048]{1,0:T(8,128)(2,1)S(1)}, u32[]{:S(2)}, u32[]{:S(2)}) %collective-permute-start.20) | collective-permute-done | bytes 65568 | tf_op jit(solution)/shard_map/ppermute | solution.py:43
  (56 shorter events, 8.6 us)
Async XLA Ops:
  2.0 1.5 %collective-permute-start = (bf16[128,640]{1,0:T(8,128)(2,1)S(1)}, bf16[128,640]{1,0:T(8,128)(2,1)S(1)}, u32[]{:S(2)}, u32[]{:S(2)}) collective-permute-start(bf16[128,640]{1,0:T(8,128)(2,1)S(1)} %get-tuple-element.31.own), channel_id=1, source_target_pairs={{0,1},{1,0},{2,3},{3,2},{4,5},{5,4},{6,7},{7,6},{8,9},{9,8},{10,11... | collective-permute-start | bytes 491528 | tf_op jit(solution)/shard_map/ppermute | solution.py:43
  2.5 26.2 %collective-permute-start.11 = (bf16[1,2048,768]{2,1,0:T(8,128)(2,1)}, bf16[1,2048,768]{2,1,0:T(8,128)(2,1)S(1)}, u32[]{:S(2)}, u32[]{:S(2)}) collective-permute-start(bf16[1,2048,768]{2,1,0:T(8,128)(2,1)} %refs_4_.2), channel_id=1, source_target_pairs={{0,1},{1,0},{2,3},{3,2},{4,5},{5,4},{6,7},{7,6},{8,9},{9,8},{10,11... | collective-permute-start | bytes 9437192 | tf_op jit(solution)/shard_map/ppermute | solution.py:43
  2.6 26.2 %collective-permute-start.12 = (bf16[1,2048,768]{2,1,0:T(8,128)(2,1)}, bf16[1,2048,768]{2,1,0:T(8,128)(2,1)S(1)}, u32[]{:S(2)}, u32[]{:S(2)}) collective-permute-start(bf16[1,2048,768]{2,1,0:T(8,128)(2,1)} %refs_5_.3), channel_id=1, source_target_pairs={{0,1},{1,0},{2,3},{3,2},{4,5},{5,4},{6,7},{7,6},{8,9},{9,8},{10,11... | collective-permute-start | bytes 9437192 | tf_op jit(solution)/shard_map/ppermute | solution.py:43
  3.0 28.4 %collective-permute-start.13 = (bf16[1,768,2048]{2,1,0:T(8,128)(2,1)}, bf16[1,768,2048]{2,1,0:T(8,128)(2,1)S(1)}, u32[]{:S(2)}, u32[]{:S(2)}) collective-permute-start(bf16[1,768,2048]{2,1,0:T(8,128)(2,1)} %refs_4_.3), channel_id=1, source_target_pairs={{0,1},{1,0},{2,3},{3,2},{4,5},{5,4},{6,7},{7,6},{8,9},{9,8},{10,11... | collective-permute-start | bytes 9437192 | tf_op jit(solution)/shard_map/ppermute | solution.py:43
  3.8 5.4 %collective-permute-start.2 = (bf16[64,1024]{1,0:T(8,128)(2,1)S(1)}, bf16[64,1024]{1,0:T(8,128)(2,1)S(1)}, u32[]{:S(2)}, u32[]{:S(2)}) collective-permute-start(bf16[64,1024]{1,0:T(8,128)(2,1)S(1)} %get-tuple-element.36), channel_id=1, source_target_pairs={{0,5},{1,2},{2,1},{3,6},{4,7},{5,0},{6,3},{7,4},{8,11},{9,12},{10,... | collective-permute-start | bytes 393224 | tf_op jit(solution)/shard_map/ppermute | solution.py:43
  6.6 22.2 %copy-start.1 = (bf16[1,2048,768]{2,1,0:T(8,128)(2,1)S(1)}, bf16[1,2048,768]{2,1,0:T(8,128)(2,1)}, u32[]{:S(2)}) copy-start(bf16[1,2048,768]{2,1,0:T(8,128)(2,1)} %refs_5_.3) | copy-start | bytes 9437188
  6.9 21.8 %copy-start = (bf16[1,2048,768]{2,1,0:T(8,128)(2,1)S(1)}, bf16[1,2048,768]{2,1,0:T(8,128)(2,1)}, u32[]{:S(2)}) copy-start(bf16[1,2048,768]{2,1,0:T(8,128)(2,1)} %refs_4_.2) | copy-start | bytes 9437188
  6.9 5.5 %collective-permute-start.1 = (bf16[64,1024]{1,0:T(8,128)(2,1)S(1)}, bf16[64,1024]{1,0:T(8,128)(2,1)S(1)}, u32[]{:S(2)}, u32[]{:S(2)}) collective-permute-start(bf16[64,1024]{1,0:T(8,128)(2,1)S(1)} %get-tuple-element.34), channel_id=1, source_target_pairs={{0,5},{1,2},{2,1},{3,6},{4,7},{5,0},{6,3},{7,4},{8,11},{9,12},{10,... | collective-permute-start | bytes 393224 | tf_op jit(solution)/shard_map/ppermute | solution.py:43
  9.3 5.6 %collective-permute-start.4 = (bf16[32,1024]{1,0:T(8,128)(2,1)S(1)}, bf16[32,1024]{1,0:T(8,128)(2,1)S(1)}, u32[]{:S(2)}, u32[]{:S(2)}) collective-permute-start(bf16[32,1024]{1,0:T(8,128)(2,1)S(1)} %slice.109), channel_id=1, source_target_pairs={{0,9},{1,4},{2,7},{3,10},{4,1},{5,12},{6,15},{7,2},{8,13},{9,0},{1... | collective-permute-start | bytes 196616 | tf_op jit(solution)/shard_map/ppermute | solution.py:43
  12.5 4.7 %collective-permute-start.3 = (bf16[32,1024]{1,0:T(8,128)(2,1)S(1)}, bf16[32,1024]{1,0:T(8,128)(2,1)S(1)}, u32[]{:S(2)}, u32[]{:S(2)}) collective-permute-start(bf16[32,1024]{1,0:T(8,128)(2,1)S(1)} %slice.108), channel_id=1, source_target_pairs={{0,9},{1,4},{2,7},{3,10},{4,1},{5,12},{6,15},{7,2},{8,13},{9,0},{1... | collective-permute-start | bytes 196616 | tf_op jit(solution)/shard_map/ppermute | solution.py:43
  14.9 3.9 %collective-permute-start.6 = (bf16[32,1152]{1,0:T(8,128)(2,1)S(1)}, bf16[32,1152]{1,0:T(8,128)(2,1)S(1)}, u32[]{:S(2)}, u32[]{:S(2)}) collective-permute-start(bf16[32,1152]{1,0:T(8,128)(2,1)S(1)} %fusion.2), channel_id=1, source_target_pairs={{0,3},{1,8},{2,11},{3,0},{4,13},{5,6},{6,5},{7,14},{8,1},{9,10},{1... | collective-permute-start | bytes 221192 | tf_op jit(solution)/shard_map/ppermute | solution.py:43
  17.1 4.8 %collective-permute-start.5 = (bf16[32,1024]{1,0:T(8,128)(2,1)S(1)}, bf16[32,1024]{1,0:T(8,128)(2,1)S(1)}, u32[]{:S(2)}, u32[]{:S(2)}) collective-permute-start(bf16[32,1024]{1,0:T(8,128)(2,1)S(1)} %fusion.3), channel_id=1, source_target_pairs={{0,3},{1,8},{2,11},{3,0},{4,13},{5,6},{6,5},{7,14},{8,1},{9,10},{1... | collective-permute-start | bytes 196616 | tf_op jit(solution)/shard_map/ppermute | solution.py:43
  18.8 5.3 %collective-permute-start.8 = (bf16[32,1152]{1,0:T(8,128)(2,1)S(1)}, bf16[32,1152]{1,0:T(8,128)(2,1)S(1)}, u32[]{:S(2)}, u32[]{:S(2)}) collective-permute-start(bf16[32,1152]{1,0:T(8,128)(2,1)S(1)} %fusion), channel_id=1, source_target_pairs={{0,9},{1,4},{2,7},{3,10},{4,1},{5,12},{6,15},{7,2},{8,13},{9,0},{1... | collective-permute-start | bytes 221192 | tf_op jit(solution)/shard_map/ppermute | solution.py:43
  22.0 4.9 %collective-permute-start.7 = (bf16[32,1024]{1,0:T(8,128)(2,1)S(1)}, bf16[32,1024]{1,0:T(8,128)(2,1)S(1)}, u32[]{:S(2)}, u32[]{:S(2)}) collective-permute-start(bf16[32,1024]{1,0:T(8,128)(2,1)S(1)} %fusion.1), channel_id=1, source_target_pairs={{0,9},{1,4},{2,7},{3,10},{4,1},{5,12},{6,15},{7,2},{8,13},{9,0},{1... | collective-permute-start | bytes 196616 | tf_op jit(solution)/shard_map/ppermute | solution.py:43
  24.1 4.6 %collective-permute-start.10 = (bf16[64,1152]{1,0:T(8,128)(2,1)S(1)}, bf16[64,1152]{1,0:T(8,128)(2,1)S(1)}, u32[]{:S(2)}, u32[]{:S(2)}) collective-permute-start(bf16[64,1152]{1,0:T(8,128)(2,1)S(1)} %pad_maximum_fusion.1.refs_0_.refs_2_), channel_id=1, source_target_pairs={{0,5},{1,2},{2,1},{3,6},{4,7},{5,0},{6,3},{7,4},{8,11},{9,12},{10,... | collective-permute-start | bytes 442376 | tf_op jit(solution)/shard_map/ppermute | solution.py:43
  26.9 4.5 %copy-start.2 = (bf16[1,768,2048]{2,1,0:T(8,128)(2,1)S(1)}, bf16[1,768,2048]{2,1,0:T(8,128)(2,1)}, u32[]{:S(2)}) copy-start(bf16[1,768,2048]{2,1,0:T(8,128)(2,1)} %refs_4_.3) | copy-start | bytes 9437188
  26.9 4.5 %collective-permute-start.9 = (bf16[64,1024]{1,0:T(8,128)(2,1)S(1)}, bf16[64,1024]{1,0:T(8,128)(2,1)S(1)}, u32[]{:S(2)}, u32[]{:S(2)}) collective-permute-start(bf16[64,1024]{1,0:T(8,128)(2,1)S(1)} %pad_maximum_fusion.2.refs_0_), channel_id=1, source_target_pairs={{0,5},{1,2},{2,1},{3,6},{4,7},{5,0},{6,3},{7,4},{8,11},{9,12},{10,... | collective-permute-start | bytes 393224 | tf_op jit(solution)/shard_map/ppermute | solution.py:43
  33.0 4.5 %collective-permute-start.14 = (bf16[64,1024]{1,0:T(8,128)(2,1)S(1)}, bf16[64,1024]{1,0:T(8,128)(2,1)S(1)}, u32[]{:S(2)}, u32[]{:S(2)}) collective-permute-start(bf16[64,1024]{1,0:T(8,128)(2,1)S(1)} %get-tuple-element.47), channel_id=1, source_target_pairs={{0,5},{1,2},{2,1},{3,6},{4,7},{5,0},{6,3},{7,4},{8,11},{9,12},{10,... | collective-permute-start | bytes 393224 | tf_op jit(solution)/shard_map/ppermute | solution.py:43
  34.5 4.5 %collective-permute-start.17 = (bf16[64,1024]{1,0:T(8,128)(2,1)S(1)}, bf16[64,1024]{1,0:T(8,128)(2,1)S(1)}, u32[]{:S(2)}, u32[]{:S(2)}) collective-permute-start(bf16[64,1024]{1,0:T(8,128)(2,1)S(1)} %get-tuple-element.53), channel_id=1, source_target_pairs={{0,5},{1,2},{2,1},{3,6},{4,7},{5,0},{6,3},{7,4},{8,11},{9,12},{10,... | collective-permute-start | bytes 393224 | tf_op jit(solution)/shard_map/ppermute | solution.py:43
  37.5 3.8 %collective-permute-start.15 = (bf16[32,1024]{1,0:T(8,128)(2,1)S(1)}, bf16[32,1024]{1,0:T(8,128)(2,1)S(1)}, u32[]{:S(2)}, u32[]{:S(2)}) collective-permute-start(bf16[32,1024]{1,0:T(8,128)(2,1)S(1)} %slice.107), channel_id=1, source_target_pairs={{0,3},{1,8},{2,11},{3,0},{4,13},{5,6},{6,5},{7,14},{8,1},{9,10},{1... | collective-permute-start | bytes 196616 | tf_op jit(solution)/shard_map/ppermute | solution.py:43
  39.0 4.2 %collective-permute-start.18 = (bf16[32,1024]{1,0:T(8,128)(2,1)S(1)}, bf16[32,1024]{1,0:T(8,128)(2,1)S(1)}, u32[]{:S(2)}, u32[]{:S(2)}) collective-permute-start(bf16[32,1024]{1,0:T(8,128)(2,1)S(1)} %slice.106), channel_id=1, source_target_pairs={{0,3},{1,8},{2,11},{3,0},{4,13},{5,6},{6,5},{7,14},{8,1},{9,10},{1... | collective-permute-start | bytes 196616 | tf_op jit(solution)/shard_map/ppermute | solution.py:43
  41.3 4.3 %collective-permute-start.16 = (bf16[16,1024]{1,0:T(8,128)(2,1)S(1)}, bf16[16,1024]{1,0:T(8,128)(2,1)S(1)}, u32[]{:S(2)}, u32[]{:S(2)}) collective-permute-start(bf16[16,1024]{1,0:T(8,128)(2,1)S(1)} %slice.111), channel_id=1, source_target_pairs={{0,9},{1,4},{2,7},{3,10},{4,1},{5,12},{6,15},{7,2},{8,13},{9,0},{1... | collective-permute-start | bytes 98312 | tf_op jit(solution)/shard_map/ppermute | solution.py:43
  43.3 4.3 %collective-permute-start.19 = (bf16[16,1024]{1,0:T(8,128)(2,1)S(1)}, bf16[16,1024]{1,0:T(8,128)(2,1)S(1)}, u32[]{:S(2)}, u32[]{:S(2)}) collective-permute-start(bf16[16,1024]{1,0:T(8,128)(2,1)S(1)} %slice.110), channel_id=1, source_target_pairs={{0,9},{1,4},{2,7},{3,10},{4,1},{5,12},{6,15},{7,2},{8,13},{9,0},{1... | collective-permute-start | bytes 98312 | tf_op jit(solution)/shard_map/ppermute | solution.py:43
  47.6 1.3 %collective-permute-start.20 = (bf16[16,2048]{1,0:T(8,128)(2,1)S(1)}, bf16[16,2048]{1,0:T(8,128)(2,1)S(1)}, u32[]{:S(2)}, u32[]{:S(2)}) collective-permute-start(bf16[16,2048]{1,0:T(8,128)(2,1)S(1)} %pad_maximum_fusion.3), channel_id=1, source_target_pairs={{0,1},{1,0},{2,3},{3,2},{4,5},{5,4},{6,7},{7,6},{8,9},{9,8},{10,11... | collective-permute-start | bytes 196616 | tf_op jit(solution)/shard_map/ppermute | solution.py:43

commit v9 on v8

--- a/solution.py
+++ b/solution.py
@@ -437,11 +437,10 @@
             other = ordered_after(exchange(sent, route), earlier)
             part[:] = halved(kept + other.astype(jnp.float32))
             earlier = part[1]
-    results, earlier = [], None
+    results = []
     for kept, sent in parts:
-        other = ordered_after(exchange(sent, routes.returns[-1]), earlier).astype(jnp.float32)
+        other = exchange(sent, routes.returns[-1]).astype(jnp.float32)
         results.append((kept + other).astype(jnp.bfloat16))
-        earlier = results[-1]
     result = jnp.concatenate(results, axis=1)
     return jnp.where(on_odd_chip(), exchange(result, routes.pair), result)
 

time: 49.8 us -> 49.8 us (level)
  no operation moved by 1% of the time
where the time goes in v9:
time: 49.8 us; the launch traced here: 49.6 us
  starting transfers between devices  27.1 us (54%)
  waiting for transfers between devices  15.5 us (31%)
  Pallas kernels  5.8 us (12%)
  other arithmetic  0.94 us (2%)
    ppermute x21, starting transfers between devices, exchange(): return lax.ppermute(block, 'wide', [(i, route(i)) for i in range(count)])  27.1 us
    ppermute x21, waiting for transfers between devices, exchange(): return lax.ppermute(block, 'wide', [(i, route(i)) for i in range(count)])  15.5 us
    pallas_call x5, Pallas kernels, local_call(): pl.pallas_call(kernel, out_shape=out_shape, in_specs=[pl.BlockSpec(memory...  3.83 us
    pallas_call x1, Pallas kernels, attend(): pl.pallas_call(functools.partial(attend_kernel, axis_width), out_shape=[p...  1.97 us
  transfers between devices with their start and end apart: 21, of which 15 were waited for; matrix products, arithmetic and copies ran while one was open for 1% of the time, Pallas kernels for 5%

profile of v9, /device:TPU:0, one launch (start us, length us, event | category | flops | bytes accessed | tf_op | source)
XLA Modules:
  0.0 49.6 jit_solution(16447403640719846333)
XLA Ops:
  0.0 2.0 %attend.1 = (bf16[128,640]{1,0:T(8,128)(2,1)S(1)}, bf16[512,2048]{1,0:T(8,128)(2,1)S(1)}) custom-call(s32[4,32]{1,0:T(4,128)} %refs_0_.1, s32[4,4]{1,0:T(4,128)} %refs_1_.1, s32[1,4]{1,0:T(1,128)} %refs_2_.2, s32[8,16]{1,0:T(8,128)} %bitcast.2, f32[8,16]{1,0:T(8,128)} %bitcast.3, bf16[128,512]{1,0:T(8,128)(2,1)} %refs_5_.2, bf16[2,128,128]{2,1,0:T(8,128)(2,1)} %refs_6_.1, ...), custom_call_target="tpu_custom_call" | custom-call | tf_op jit(solution)/shard_map/attend/pallas_call | solution.py:234
  3.8 2.8 %collective-permute-start.2 = (bf16[64,1024]{1,0:T(8,128)(2,1)S(1)}, bf16[64,1024]{1,0:T(8,128)(2,1)S(1)}, u32[]{:S(2)}, u32[]{:S(2)}) collective-permute-start(bf16[64,1024]{1,0:T(8,128)(2,1)S(1)} %get-tuple-element.35), channel_id=1, source_target_pairs={{0,5},{1,2},{2,1},{3,6},{4,7},{5,0},{6,3},{7,4},{8,11},{9,12},{10,... | collective-permute-start | bytes 393224 | tf_op jit(solution)/shard_map/ppermute | solution.py:43
  7.0 2.2 %collective-permute-done.2 = bf16[64,1024]{1,0:T(8,128)(2,1)S(1)} collective-permute-done((bf16[64,1024]{1,0:T(8,128)(2,1)S(1)}, bf16[64,1024]{1,0:T(8,128)(2,1)S(1)}, u32[]{:S(2)}, u32[]{:S(2)}) %collective-permute-start.2) | collective-permute-done | bytes 131104 | tf_op jit(solution)/shard_map/ppermute | solution.py:43
  9.3 3.1 %collective-permute-start.4 = (bf16[32,1024]{1,0:T(8,128)(2,1)S(1)}, bf16[32,1024]{1,0:T(8,128)(2,1)S(1)}, u32[]{:S(2)}, u32[]{:S(2)}) collective-permute-start(bf16[32,1024]{1,0:T(8,128)(2,1)S(1)} %slice.109), channel_id=1, source_target_pairs={{0,9},{1,4},{2,7},{3,10},{4,1},{5,12},{6,15},{7,2},{8,13},{9,0},{1... | collective-permute-start | bytes 196616 | tf_op jit(solution)/shard_map/ppermute | solution.py:43
  12.5 1.6 %collective-permute-start.3 = (bf16[32,1024]{1,0:T(8,128)(2,1)S(1)}, bf16[32,1024]{1,0:T(8,128)(2,1)S(1)}, u32[]{:S(2)}, u32[]{:S(2)}) collective-permute-start(bf16[32,1024]{1,0:T(8,128)(2,1)S(1)} %slice.108), channel_id=1, source_target_pairs={{0,9},{1,4},{2,7},{3,10},{4,1},{5,12},{6,15},{7,2},{8,13},{9,0},{1... | collective-permute-start | bytes 196616 | tf_op jit(solution)/shard_map/ppermute | solution.py:43
  14.9 1.9 %collective-permute-start.6 = (bf16[32,1152]{1,0:T(8,128)(2,1)S(1)}, bf16[32,1152]{1,0:T(8,128)(2,1)S(1)}, u32[]{:S(2)}, u32[]{:S(2)}) collective-permute-start(bf16[32,1152]{1,0:T(8,128)(2,1)S(1)} %fusion.2), channel_id=1, source_target_pairs={{0,3},{1,8},{2,11},{3,0},{4,13},{5,6},{6,5},{7,14},{8,1},{9,10},{1... | collective-permute-start | bytes 221192 | tf_op jit(solution)/shard_map/ppermute | solution.py:43
  17.1 1.3 %collective-permute-start.5 = (bf16[32,1024]{1,0:T(8,128)(2,1)S(1)}, bf16[32,1024]{1,0:T(8,128)(2,1)S(1)}, u32[]{:S(2)}, u32[]{:S(2)}) collective-permute-start(bf16[32,1024]{1,0:T(8,128)(2,1)S(1)} %fusion.3), channel_id=1, source_target_pairs={{0,3},{1,8},{2,11},{3,0},{4,13},{5,6},{6,5},{7,14},{8,1},{9,10},{1... | collective-permute-start | bytes 196616 | tf_op jit(solution)/shard_map/ppermute | solution.py:43
  18.8 3.1 %collective-permute-start.8 = (bf16[32,1152]{1,0:T(8,128)(2,1)S(1)}, bf16[32,1152]{1,0:T(8,128)(2,1)S(1)}, u32[]{:S(2)}, u32[]{:S(2)}) collective-permute-start(bf16[32,1152]{1,0:T(8,128)(2,1)S(1)} %fusion), channel_id=1, source_target_pairs={{0,9},{1,4},{2,7},{3,10},{4,1},{5,12},{6,15},{7,2},{8,13},{9,0},{1... | collective-permute-start | bytes 221192 | tf_op jit(solution)/shard_map/ppermute | solution.py:43
  22.8 1.2 %collective-permute-done.8 = bf16[32,1152]{1,0:T(8,128)(2,1)S(1)} collective-permute-done((bf16[32,1152]{1,0:T(8,128)(2,1)S(1)}, bf16[32,1152]{1,0:T(8,128)(2,1)S(1)}, u32[]{:S(2)}, u32[]{:S(2)}) %collective-permute-start.8) | collective-permute-done | bytes 73760 | tf_op jit(solution)/shard_map/ppermute | solution.py:43
  24.1 1.6 %collective-permute-start.10 = (bf16[64,1152]{1,0:T(8,128)(2,1)S(1)}, bf16[64,1152]{1,0:T(8,128)(2,1)S(1)}, u32[]{:S(2)}, u32[]{:S(2)}) collective-permute-start(bf16[64,1152]{1,0:T(8,128)(2,1)S(1)} %pad_maximum_fusion.1.refs_0_.refs_2_), channel_id=1, source_target_pairs={{0,5},{1,2},{2,1},{3,6},{4,7},{5,0},{6,3},{7,4},{8,11},{9,12},{10,... | collective-permute-start | bytes 442376 | tf_op jit(solution)/shard_map/ppermute | solution.py:43
  25.7 1.2 %collective-permute-done.7 = bf16[32,1024]{1,0:T(8,128)(2,1)S(1)} collective-permute-done((bf16[32,1024]{1,0:T(8,128)(2,1)S(1)}, bf16[32,1024]{1,0:T(8,128)(2,1)S(1)}, u32[]{:S(2)}, u32[]{:S(2)}) %collective-permute-start.7) | collective-permute-done | bytes 65568 | tf_op jit(solution)/shard_map/ppermute | solution.py:43
  26.9 0.9 %collective-permute-start.9 = (bf16[64,1024]{1,0:T(8,128)(2,1)S(1)}, bf16[64,1024]{1,0:T(8,128)(2,1)S(1)}, u32[]{:S(2)}, u32[]{:S(2)}) collective-permute-start(bf16[64,1024]{1,0:T(8,128)(2,1)S(1)} %pad_maximum_fusion.2.refs_0_), channel_id=1, source_target_pairs={{0,5},{1,2},{2,1},{3,6},{4,7},{5,0},{6,3},{7,4},{8,11},{9,12},{10,... | collective-permute-start | bytes 393224 | tf_op jit(solution)/shard_map/ppermute | solution.py:43
  28.8 1.0 %feed.1 = (f32[128,768]{1,0:T(8,128)S(1)}, f32[128,768]{1,0:T(8,128)S(1)}, f32[128,768]{1,0:T(8,128)S(1)}, f32[128,768]{1,0:T(8,128)S(1)}) custom-call(bf16[64,1152]{1,0:T(8,128)(2,1)S(1)} %pad_maximum_fusion.1.refs_0_.refs_2_, bf16[64,1152]{1,0:T(8,128)(2,1)S(1)} %collective-permute-done.10.refs_1_.refs_3_, bf16[1,2048,768]{2,1,0:T(8,128)(2,1)S(1)} %copy-done, ...), custom_call_target="tpu_custom_call" | custom-call | tf_op jit(solution)/shard_map/feed/pallas_call | solution.py:327
  29.8 1.6 %collective-permute-done.9.refs_1_ = bf16[64,1024]{1,0:T(8,128)(2,1)S(1)} collective-permute-done((bf16[64,1024]{1,0:T(8,128)(2,1)S(1)}, bf16[64,1024]{1,0:T(8,128)(2,1)S(1)}, u32[]{:S(2)}, u32[]{:S(2)}) %collective-permute-start.9) | collective-permute-done | bytes 131104 | tf_op jit(solution)/shard_map/ppermute | solution.py:43
  31.4 1.6 %finish.1 = (f32[64,1024]{1,0:T(8,128)S(1)}, bf16[64,1024]{1,0:T(8,128)(2,1)S(1)}, bf16[128,768]{1,0:T(8,128)(2,1)S(1)}, bf16[128,768]{1,0:T(8,128)(2,1)S(1)}, f...) custom-call(bf16[64,1024]{1,0:T(8,128)(2,1)S(1)} %pad_maximum_fusion.2.refs_0_, ...), custom_call_target="tpu_custom_call" | custom-call | tf_op jit(solution)/shard_map/finish/pallas_call | solution.py:327
  33.0 0.9 %collective-permute-start.14 = (bf16[64,1024]{1,0:T(8,128)(2,1)S(1)}, bf16[64,1024]{1,0:T(8,128)(2,1)S(1)}, u32[]{:S(2)}, u32[]{:S(2)}) collective-permute-start(bf16[64,1024]{1,0:T(8,128)(2,1)S(1)} %get-tuple-element.46), channel_id=1, source_target_pairs={{0,5},{1,2},{2,1},{3,6},{4,7},{5,0},{6,3},{7,4},{8,11},{9,12},{10,... | collective-permute-start | bytes 393224 | tf_op jit(solution)/shard_map/ppermute | solution.py:43
  34.5 1.0 %collective-permute-start.17 = (bf16[64,1024]{1,0:T(8,128)(2,1)S(1)}, bf16[64,1024]{1,0:T(8,128)(2,1)S(1)}, u32[]{:S(2)}, u32[]{:S(2)}) collective-permute-start(bf16[64,1024]{1,0:T(8,128)(2,1)S(1)} %get-tuple-element.52), channel_id=1, source_target_pairs={{0,5},{1,2},{2,1},{3,6},{4,7},{5,0},{6,3},{7,4},{8,11},{9,12},{10,... | collective-permute-start | bytes 393224 | tf_op jit(solution)/shard_map/ppermute | solution.py:43
  35.5 2.0 %collective-permute-done.14 = bf16[64,1024]{1,0:T(8,128)(2,1)S(1)} collective-permute-done((bf16[64,1024]{1,0:T(8,128)(2,1)S(1)}, bf16[64,1024]{1,0:T(8,128)(2,1)S(1)}, u32[]{:S(2)}, u32[]{:S(2)}) %collective-permute-start.14) | collective-permute-done | bytes 131104 | tf_op jit(solution)/shard_map/ppermute | solution.py:43
  37.5 1.2 %collective-permute-start.15 = (bf16[32,1024]{1,0:T(8,128)(2,1)S(1)}, bf16[32,1024]{1,0:T(8,128)(2,1)S(1)}, u32[]{:S(2)}, u32[]{:S(2)}) collective-permute-start(bf16[32,1024]{1,0:T(8,128)(2,1)S(1)} %slice.107), channel_id=1, source_target_pairs={{0,3},{1,8},{2,11},{3,0},{4,13},{5,6},{6,5},{7,14},{8,1},{9,10},{1... | collective-permute-start | bytes 196616 | tf_op jit(solution)/shard_map/ppermute | solution.py:43
  39.0 1.7 %collective-permute-start.18 = (bf16[32,1024]{1,0:T(8,128)(2,1)S(1)}, bf16[32,1024]{1,0:T(8,128)(2,1)S(1)}, u32[]{:S(2)}, u32[]{:S(2)}) collective-permute-start(bf16[32,1024]{1,0:T(8,128)(2,1)S(1)} %slice.106), channel_id=1, source_target_pairs={{0,3},{1,8},{2,11},{3,0},{4,13},{5,6},{6,5},{7,14},{8,1},{9,10},{1... | collective-permute-start | bytes 196616 | tf_op jit(solution)/shard_map/ppermute | solution.py:43
  41.3 1.9 %collective-permute-start.16 = (bf16[16,1024]{1,0:T(8,128)(2,1)S(1)}, bf16[16,1024]{1,0:T(8,128)(2,1)S(1)}, u32[]{:S(2)}, u32[]{:S(2)}) collective-permute-start(bf16[16,1024]{1,0:T(8,128)(2,1)S(1)} %slice.111), channel_id=1, source_target_pairs={{0,9},{1,4},{2,7},{3,10},{4,1},{5,12},{6,15},{7,2},{8,13},{9,0},{1... | collective-permute-start | bytes 98312 | tf_op jit(solution)/shard_map/ppermute | solution.py:43
  43.3 1.9 %collective-permute-start.19 = (bf16[16,1024]{1,0:T(8,128)(2,1)S(1)}, bf16[16,1024]{1,0:T(8,128)(2,1)S(1)}, u32[]{:S(2)}, u32[]{:S(2)}) collective-permute-start(bf16[16,1024]{1,0:T(8,128)(2,1)S(1)} %slice.110), channel_id=1, source_target_pairs={{0,9},{1,4},{2,7},{3,10},{4,1},{5,12},{6,15},{7,2},{8,13},{9,0},{1... | collective-permute-start | bytes 98312 | tf_op jit(solution)/shard_map/ppermute | solution.py:43
  45.6 2.0 %collective-permute-done.19 = bf16[16,1024]{1,0:T(8,128)(2,1)S(1)} collective-permute-done((bf16[16,1024]{1,0:T(8,128)(2,1)S(1)}, bf16[16,1024]{1,0:T(8,128)(2,1)S(1)}, u32[]{:S(2)}, u32[]{:S(2)}) %collective-permute-start.19) | collective-permute-done | bytes 32800 | tf_op jit(solution)/shard_map/ppermute | solution.py:43
  47.8 1.1 %collective-permute-done.20 = bf16[16,2048]{1,0:T(8,128)(2,1)S(1)} collective-permute-done((bf16[16,2048]{1,0:T(8,128)(2,1)S(1)}, bf16[16,2048]{1,0:T(8,128)(2,1)S(1)}, u32[]{:S(2)}, u32[]{:S(2)}) %collective-permute-start.20) | collective-permute-done | bytes 65568 | tf_op jit(solution)/shard_map/ppermute | solution.py:43
  (56 shorter events, 8.6 us)
Async XLA Ops:
  2.0 1.5 %collective-permute-start = (bf16[128,640]{1,0:T(8,128)(2,1)S(1)}, bf16[128,640]{1,0:T(8,128)(2,1)S(1)}, u32[]{:S(2)}, u32[]{:S(2)}) collective-permute-start(bf16[128,640]{1,0:T(8,128)(2,1)S(1)} %get-tuple-element.30.own), channel_id=1, source_target_pairs={{0,1},{1,0},{2,3},{3,2},{4,5},{5,4},{6,7},{7,6},{8,9},{9,8},{10,11... | collective-permute-start | bytes 491528 | tf_op jit(solution)/shard_map/ppermute | solution.py:43
  2.5 26.2 %collective-permute-start.11 = (bf16[1,2048,768]{2,1,0:T(8,128)(2,1)}, bf16[1,2048,768]{2,1,0:T(8,128)(2,1)S(1)}, u32[]{:S(2)}, u32[]{:S(2)}) collective-permute-start(bf16[1,2048,768]{2,1,0:T(8,128)(2,1)} %refs_4_.2), channel_id=1, source_target_pairs={{0,1},{1,0},{2,3},{3,2},{4,5},{5,4},{6,7},{7,6},{8,9},{9,8},{10,11... | collective-permute-start | bytes 9437192 | tf_op jit(solution)/shard_map/ppermute | solution.py:43
  2.6 26.2 %collective-permute-start.12 = (bf16[1,2048,768]{2,1,0:T(8,128)(2,1)}, bf16[1,2048,768]{2,1,0:T(8,128)(2,1)S(1)}, u32[]{:S(2)}, u32[]{:S(2)}) collective-permute-start(bf16[1,2048,768]{2,1,0:T(8,128)(2,1)} %refs_5_.3), channel_id=1, source_target_pairs={{0,1},{1,0},{2,3},{3,2},{4,5},{5,4},{6,7},{7,6},{8,9},{9,8},{10,11... | collective-permute-start | bytes 9437192 | tf_op jit(solution)/shard_map/ppermute | solution.py:43
  3.0 28.4 %collective-permute-start.13 = (bf16[1,768,2048]{2,1,0:T(8,128)(2,1)}, bf16[1,768,2048]{2,1,0:T(8,128)(2,1)S(1)}, u32[]{:S(2)}, u32[]{:S(2)}) collective-permute-start(bf16[1,768,2048]{2,1,0:T(8,128)(2,1)} %refs_4_.3), channel_id=1, source_target_pairs={{0,1},{1,0},{2,3},{3,2},{4,5},{5,4},{6,7},{7,6},{8,9},{9,8},{10,11... | collective-permute-start | bytes 9437192 | tf_op jit(solution)/shard_map/ppermute | solution.py:43
  3.8 5.4 %collective-permute-start.2 = (bf16[64,1024]{1,0:T(8,128)(2,1)S(1)}, bf16[64,1024]{1,0:T(8,128)(2,1)S(1)}, u32[]{:S(2)}, u32[]{:S(2)}) collective-permute-start(bf16[64,1024]{1,0:T(8,128)(2,1)S(1)} %get-tuple-element.35), channel_id=1, source_target_pairs={{0,5},{1,2},{2,1},{3,6},{4,7},{5,0},{6,3},{7,4},{8,11},{9,12},{10,... | collective-permute-start | bytes 393224 | tf_op jit(solution)/shard_map/ppermute | solution.py:43
  6.6 22.2 %copy-start.1 = (bf16[1,2048,768]{2,1,0:T(8,128)(2,1)S(1)}, bf16[1,2048,768]{2,1,0:T(8,128)(2,1)}, u32[]{:S(2)}) copy-start(bf16[1,2048,768]{2,1,0:T(8,128)(2,1)} %refs_5_.3) | copy-start | bytes 9437188
  6.9 21.8 %copy-start = (bf16[1,2048,768]{2,1,0:T(8,128)(2,1)S(1)}, bf16[1,2048,768]{2,1,0:T(8,128)(2,1)}, u32[]{:S(2)}) copy-start(bf16[1,2048,768]{2,1,0:T(8,128)(2,1)} %refs_4_.2) | copy-start | bytes 9437188
  6.9 5.5 %collective-permute-start.1 = (bf16[64,1024]{1,0:T(8,128)(2,1)S(1)}, bf16[64,1024]{1,0:T(8,128)(2,1)S(1)}, u32[]{:S(2)}, u32[]{:S(2)}) collective-permute-start(bf16[64,1024]{1,0:T(8,128)(2,1)S(1)} %get-tuple-element.33), channel_id=1, source_target_pairs={{0,5},{1,2},{2,1},{3,6},{4,7},{5,0},{6,3},{7,4},{8,11},{9,12},{10,... | collective-permute-start | bytes 393224 | tf_op jit(solution)/shard_map/ppermute | solution.py:43
  9.3 5.6 %collective-permute-start.4 = (bf16[32,1024]{1,0:T(8,128)(2,1)S(1)}, bf16[32,1024]{1,0:T(8,128)(2,1)S(1)}, u32[]{:S(2)}, u32[]{:S(2)}) collective-permute-start(bf16[32,1024]{1,0:T(8,128)(2,1)S(1)} %slice.109), channel_id=1, source_target_pairs={{0,9},{1,4},{2,7},{3,10},{4,1},{5,12},{6,15},{7,2},{8,13},{9,0},{1... | collective-permute-start | bytes 196616 | tf_op jit(solution)/shard_map/ppermute | solution.py:43
  12.5 4.7 %collective-permute-start.3 = (bf16[32,1024]{1,0:T(8,128)(2,1)S(1)}, bf16[32,1024]{1,0:T(8,128)(2,1)S(1)}, u32[]{:S(2)}, u32[]{:S(2)}) collective-permute-start(bf16[32,1024]{1,0:T(8,128)(2,1)S(1)} %slice.108), channel_id=1, source_target_pairs={{0,9},{1,4},{2,7},{3,10},{4,1},{5,12},{6,15},{7,2},{8,13},{9,0},{1... | collective-permute-start | bytes 196616 | tf_op jit(solution)/shard_map/ppermute | solution.py:43
  14.9 3.9 %collective-permute-start.6 = (bf16[32,1152]{1,0:T(8,128)(2,1)S(1)}, bf16[32,1152]{1,0:T(8,128)(2,1)S(1)}, u32[]{:S(2)}, u32[]{:S(2)}) collective-permute-start(bf16[32,1152]{1,0:T(8,128)(2,1)S(1)} %fusion.2), channel_id=1, source_target_pairs={{0,3},{1,8},{2,11},{3,0},{4,13},{5,6},{6,5},{7,14},{8,1},{9,10},{1... | collective-permute-start | bytes 221192 | tf_op jit(solution)/shard_map/ppermute | solution.py:43
  17.1 4.8 %collective-permute-start.5 = (bf16[32,1024]{1,0:T(8,128)(2,1)S(1)}, bf16[32,1024]{1,0:T(8,128)(2,1)S(1)}, u32[]{:S(2)}, u32[]{:S(2)}) collective-permute-start(bf16[32,1024]{1,0:T(8,128)(2,1)S(1)} %fusion.3), channel_id=1, source_target_pairs={{0,3},{1,8},{2,11},{3,0},{4,13},{5,6},{6,5},{7,14},{8,1},{9,10},{1... | collective-permute-start | bytes 196616 | tf_op jit(solution)/shard_map/ppermute | solution.py:43
  18.8 5.3 %collective-permute-start.8 = (bf16[32,1152]{1,0:T(8,128)(2,1)S(1)}, bf16[32,1152]{1,0:T(8,128)(2,1)S(1)}, u32[]{:S(2)}, u32[]{:S(2)}) collective-permute-start(bf16[32,1152]{1,0:T(8,128)(2,1)S(1)} %fusion), channel_id=1, source_target_pairs={{0,9},{1,4},{2,7},{3,10},{4,1},{5,12},{6,15},{7,2},{8,13},{9,0},{1... | collective-permute-start | bytes 221192 | tf_op jit(solution)/shard_map/ppermute | solution.py:43
  22.0 4.9 %collective-permute-start.7 = (bf16[32,1024]{1,0:T(8,128)(2,1)S(1)}, bf16[32,1024]{1,0:T(8,128)(2,1)S(1)}, u32[]{:S(2)}, u32[]{:S(2)}) collective-permute-start(bf16[32,1024]{1,0:T(8,128)(2,1)S(1)} %fusion.1), channel_id=1, source_target_pairs={{0,9},{1,4},{2,7},{3,10},{4,1},{5,12},{6,15},{7,2},{8,13},{9,0},{1... | collective-permute-start | bytes 196616 | tf_op jit(solution)/shard_map/ppermute | solution.py:43
  24.1 4.6 %collective-permute-start.10 = (bf16[64,1152]{1,0:T(8,128)(2,1)S(1)}, bf16[64,1152]{1,0:T(8,128)(2,1)S(1)}, u32[]{:S(2)}, u32[]{:S(2)}) collective-permute-start(bf16[64,1152]{1,0:T(8,128)(2,1)S(1)} %pad_maximum_fusion.1.refs_0_.refs_2_), channel_id=1, source_target_pairs={{0,5},{1,2},{2,1},{3,6},{4,7},{5,0},{6,3},{7,4},{8,11},{9,12},{10,... | collective-permute-start | bytes 442376 | tf_op jit(solution)/shard_map/ppermute | solution.py:43
  26.9 4.5 %copy-start.2 = (bf16[1,768,2048]{2,1,0:T(8,128)(2,1)S(1)}, bf16[1,768,2048]{2,1,0:T(8,128)(2,1)}, u32[]{:S(2)}) copy-start(bf16[1,768,2048]{2,1,0:T(8,128)(2,1)} %refs_4_.3) | copy-start | bytes 9437188
  26.9 4.5 %collective-permute-start.9 = (bf16[64,1024]{1,0:T(8,128)(2,1)S(1)}, bf16[64,1024]{1,0:T(8,128)(2,1)S(1)}, u32[]{:S(2)}, u32[]{:S(2)}) collective-permute-start(bf16[64,1024]{1,0:T(8,128)(2,1)S(1)} %pad_maximum_fusion.2.refs_0_), channel_id=1, source_target_pairs={{0,5},{1,2},{2,1},{3,6},{4,7},{5,0},{6,3},{7,4},{8,11},{9,12},{10,... | collective-permute-start | bytes 393224 | tf_op jit(solution)/shard_map/ppermute | solution.py:43
  33.0 4.5 %collective-permute-start.14 = (bf16[64,1024]{1,0:T(8,128)(2,1)S(1)}, bf16[64,1024]{1,0:T(8,128)(2,1)S(1)}, u32[]{:S(2)}, u32[]{:S(2)}) collective-permute-start(bf16[64,1024]{1,0:T(8,128)(2,1)S(1)} %get-tuple-element.46), channel_id=1, source_target_pairs={{0,5},{1,2},{2,1},{3,6},{4,7},{5,0},{6,3},{7,4},{8,11},{9,12},{10,... | collective-permute-start | bytes 393224 | tf_op jit(solution)/shard_map/ppermute | solution.py:43
  34.5 4.5 %collective-permute-start.17 = (bf16[64,1024]{1,0:T(8,128)(2,1)S(1)}, bf16[64,1024]{1,0:T(8,128)(2,1)S(1)}, u32[]{:S(2)}, u32[]{:S(2)}) collective-permute-start(bf16[64,1024]{1,0:T(8,128)(2,1)S(1)} %get-tuple-element.52), channel_id=1, source_target_pairs={{0,5},{1,2},{2,1},{3,6},{4,7},{5,0},{6,3},{7,4},{8,11},{9,12},{10,... | collective-permute-start | bytes 393224 | tf_op jit(solution)/shard_map/ppermute | solution.py:43
  37.5 3.8 %collective-permute-start.15 = (bf16[32,1024]{1,0:T(8,128)(2,1)S(1)}, bf16[32,1024]{1,0:T(8,128)(2,1)S(1)}, u32[]{:S(2)}, u32[]{:S(2)}) collective-permute-start(bf16[32,1024]{1,0:T(8,128)(2,1)S(1)} %slice.107), channel_id=1, source_target_pairs={{0,3},{1,8},{2,11},{3,0},{4,13},{5,6},{6,5},{7,14},{8,1},{9,10},{1... | collective-permute-start | bytes 196616 | tf_op jit(solution)/shard_map/ppermute | solution.py:43
  39.0 4.2 %collective-permute-start.18 = (bf16[32,1024]{1,0:T(8,128)(2,1)S(1)}, bf16[32,1024]{1,0:T(8,128)(2,1)S(1)}, u32[]{:S(2)}, u32[]{:S(2)}) collective-permute-start(bf16[32,1024]{1,0:T(8,128)(2,1)S(1)} %slice.106), channel_id=1, source_target_pairs={{0,3},{1,8},{2,11},{3,0},{4,13},{5,6},{6,5},{7,14},{8,1},{9,10},{1... | collective-permute-start | bytes 196616 | tf_op jit(solution)/shard_map/ppermute | solution.py:43
  41.3 4.3 %collective-permute-start.16 = (bf16[16,1024]{1,0:T(8,128)(2,1)S(1)}, bf16[16,1024]{1,0:T(8,128)(2,1)S(1)}, u32[]{:S(2)}, u32[]{:S(2)}) collective-permute-start(bf16[16,1024]{1,0:T(8,128)(2,1)S(1)} %slice.111), channel_id=1, source_target_pairs={{0,9},{1,4},{2,7},{3,10},{4,1},{5,12},{6,15},{7,2},{8,13},{9,0},{1... | collective-permute-start | bytes 98312 | tf_op jit(solution)/shard_map/ppermute | solution.py:43
  43.3 4.3 %collective-permute-start.19 = (bf16[16,1024]{1,0:T(8,128)(2,1)S(1)}, bf16[16,1024]{1,0:T(8,128)(2,1)S(1)}, u32[]{:S(2)}, u32[]{:S(2)}) collective-permute-start(bf16[16,1024]{1,0:T(8,128)(2,1)S(1)} %slice.110), channel_id=1, source_target_pairs={{0,9},{1,4},{2,7},{3,10},{4,1},{5,12},{6,15},{7,2},{8,13},{9,0},{1... | collective-permute-start | bytes 98312 | tf_op jit(solution)/shard_map/ppermute | solution.py:43
  47.6 1.3 %collective-permute-start.20 = (bf16[16,2048]{1,0:T(8,128)(2,1)S(1)}, bf16[16,2048]{1,0:T(8,128)(2,1)S(1)}, u32[]{:S(2)}, u32[]{:S(2)}) collective-permute-start(bf16[16,2048]{1,0:T(8,128)(2,1)S(1)} %pad_maximum_fusion.3), channel_id=1, source_target_pairs={{0,1},{1,0},{2,3},{3,2},{4,5},{5,4},{6,7},{7,6},{8,9},{9,8},{10,11... | collective-permute-start | bytes 196616 | tf_op jit(solution)/shard_map/ppermute | solution.py:43
